TPU v7x, 512 devices: a whole 4x4x16 slice. The times are simulated.
512 devices in a mesh: gx: 16 (over x, y), gy: 32 (over z, core).
Axes of the slice: x: 4, y: 4, z: 16, core: 2. Of those that a mesh axis runs over, the one named last changes fastest.
Arguments:
- start_field: float32 [256, 512, 256], P('gx', 'gy'), may hold values from -3 to 3
- dielectric: float32 [256, 512, 256], P('gx', 'gy'), may hold values from 1 to 10
- ion_weight: float32 [256, 512, 256], P('gx', 'gy'), may hold values from 0.1 to 3
- source: float32 [256, 512, 256], P('gx', 'gy'), may hold values from -12 to 12
Outputs:
- relaxed_field: float32 [256, 512, 256], P('gx', 'gy')
- residual_norm: float32 [], replicated
All inputs are finite; a program needn't handle non-finite values.
Results may differ from a plain program's by a relative error of at most 0.00002.
Values sent between devices are 32-bit elements; how exact they have to be, the bound alone decides.
No kernel may reach another device: no remote copies, remote signals or barrier semaphores. Data moves between devices by JAX's collectives and lax.ppermute only.
A program may use at most 128 MiB of HBM per device.

v0:
```python
import jax
import jax.numpy as jnp
from jax import lax
from jax.sharding import PartitionSpec as P

PRE = 2
POST = 2
COARSE = 4


OMEGA = 0.8
NEIGHBOURS = (
    (slice(2, None), slice(1, -1), slice(1, -1)),
    (slice(0, -2), slice(1, -1), slice(1, -1)),
    (slice(1, -1), slice(2, None), slice(1, -1)),
    (slice(1, -1), slice(0, -2), slice(1, -1)),
    (slice(1, -1), slice(1, -1), slice(2, None)),
    (slice(1, -1), slice(1, -1), slice(0, -2)),
)


def padded_2(value, sides, width):
    for axis, dim in sides:
        size, length = (lax.axis_size(axis), value.shape[dim])
        up = [(i, (i + 1) % size) for i in range(size - 1)]
        down = [(j, i) for i, j in up]
        last = lax.slice_in_dim(value, length - width, length, axis=dim)
        leading = lax.slice_in_dim(value, 0, width, axis=dim)
        before = lax.ppermute(last, axis, up)
        after = lax.ppermute(leading, axis, down)
        value = jnp.concatenate([before, value, after], axis=dim)
    return value


def relax_cells(padded, statics, level_scale):
    permit = jnp.pad(statics[0], ((0, 0), (0, 0), (1, 1)))
    field = jnp.pad(padded, ((0, 0), (0, 0), (1, 1)))
    centre = field[1:-1, 1:-1, 1:-1]
    own_permit = permit[1:-1, 1:-1, 1:-1]
    flux = jnp.zeros_like(centre)
    faces = jnp.zeros_like(centre)
    for view in NEIGHBOURS:
        face = 0.5 * (own_permit + permit[view])
        flux = flux + face * (centre - field[view])
        faces = faces + face
    ion = statics[1][1:-1, 1:-1, :]
    load = statics[2][1:-1, 1:-1, :]
    defect = load - (level_scale * flux + ion * jnp.sinh(centre))
    slope = level_scale * faces + ion * jnp.cosh(centre)
    return (centre, defect, slope)


def restrict_cells(values):
    sx, sy, sz = values.shape
    return values.reshape(sx // 2, 2, sy // 2, 2, sz // 2, 2).mean(axis=(1, 3, 5))


def prolong_cells(values):
    return jnp.repeat(jnp.repeat(jnp.repeat(values, 2, 0), 2, 1), 2, 2)


def trim_rim(values, margin):
    if margin == 0:
        return values
    return values[..., margin : values.shape[-3] - margin, margin : values.shape[-2] - margin, :]


def body(start_field, dielectric, ion_weight, source):
    rim_depth = 1

    def spread_extend(field):
        return padded_2(field, (("gx", 0), ("gy", 1)), rim_depth)

    def smooth_level(field, statics, level_scale, sweeps, extender):
        for sweep_index in range(sweeps // rim_depth):
            padded = extender(field)
            centre, defect, slope = relax_cells(padded, statics, level_scale)
            field = centre + OMEGA * defect / slope
        return field

    def defect_of(field, statics, level_scale, extender):
        padded = extender(field)
        return relax_cells(
            trim_rim(padded, rim_depth - 1), trim_rim(statics, rim_depth - 1), level_scale
        )[1]

    def level_load(padded_stack, level_scale):
        zeros_field = jnp.zeros_like(padded_stack[0])
        loadless = jnp.stack([padded_stack[0], padded_stack[1], zeros_field])
        centre, defect, slope = relax_cells(padded_stack[2], loadless, level_scale)
        inner = trim_rim(padded_stack, 1)
        return jnp.stack([inner[0], inner[1], inner[3] + defect])

    def level_pad(stacked):
        return padded_2(stacked, (("gx", 1), ("gy", 2)), rim_depth + 1)

    statics_zero = padded_2(
        jnp.stack([dielectric, ion_weight, source]), (("gx", 1), ("gy", 2)), rim_depth
    )
    field_zero = smooth_level(start_field, statics_zero, 1.0, PRE, spread_extend)
    defect_zero = defect_of(field_zero, statics_zero, 1.0, spread_extend)
    permit_one = restrict_cells(dielectric)
    ion_one = restrict_cells(ion_weight)
    start_one = restrict_cells(field_zero)
    stack_one = jnp.stack([permit_one, ion_one, start_one, restrict_cells(defect_zero)])
    statics_one = level_load(level_pad(stack_one), 0.25)
    field_one = smooth_level(start_one, statics_one, 0.25, PRE, spread_extend)
    defect_one = defect_of(field_one, statics_one, 0.25, spread_extend)
    start_two = restrict_cells(field_one)
    stack_two = jnp.stack(
        [restrict_cells(permit_one), restrict_cells(ion_one), start_two, restrict_cells(defect_one)]
    )
    statics_two = level_load(level_pad(stack_two), 0.0625)
    field_two = smooth_level(start_two, statics_two, 0.0625, COARSE, spread_extend)
    field_one = field_one + prolong_cells(field_two - start_two)
    field_one = smooth_level(field_one, statics_one, 0.25, POST, spread_extend)
    relaxed = field_zero + prolong_cells(field_one - start_one)
    relaxed = smooth_level(relaxed, statics_zero, 1.0, POST, spread_extend)
    final_defect = defect_of(relaxed, statics_zero, 1.0, spread_extend)
    total = lax.psum(jnp.sum(final_defect * final_defect), ("gx", "gy"))
    cell_count = final_defect.size * lax.axis_size("gx") * lax.axis_size("gy")
    return (relaxed, jnp.sqrt(total / cell_count))


def solution(mesh):
    in_specs = (P("gx", "gy", None), P("gx", "gy", None), P("gx", "gy", None), P("gx", "gy", None))
    out_specs = (P("gx", "gy", None), P())
    return jax.shard_map(body, mesh=mesh, in_specs=in_specs, out_specs=out_specs, check_vma=False)
```

profile of v0, /device:TPU:1, one launch (start us, length us, event | category | flops | bytes accessed | tf_op | source)
XLA Modules:
  0.0 543.5 jit_solution(15611805823635345328)
XLA Ops:
  1.5 4.0 collective-permute-start.5
  6.3 3.2 collective-permute-start
  13.1 2.8 collective-permute-done.4
  16.0 5.3 collective-permute-start.6
  21.3 2.5 collective-permute-start.7
  23.9 2.4 collective-permute-start.2
  26.3 1.9 collective-permute-start.3
  28.6 3.1 collective-permute-done.3
  35.1 4.3 collective-permute-start.9
  39.4 18.1 %reshape.121 = f32[8,2,8,2,128,2]{5,4,3,2,1,0:T(8,128)} reshape(f32[16,16,256]{2,1,0:T(8,128)S(1)} %copy-done.1) | data formatting | bytes 524288 | tf_op jit(solution)/shard_map/reshape | solution.py:55
  57.5 18.1 %reshape.122 = f32[8,2,8,2,128,2]{5,4,3,2,1,0:T(8,128)} reshape(f32[16,16,256]{2,1,0:T(8,128)S(1)} %copy-done.2) | data formatting | bytes 524288 | tf_op jit(solution)/shard_map/reshape | solution.py:55
  75.6 7.0 %reduce_sum.82 = f32[8,8,128]{2,1,0:T(8,128)S(1)} reduce(f32[8,2,8,2,128,2]{5,4,3,2,1,0:T(8,128)} %reshape.121, f32[]{:T(128)} %constant.11.clone.1), dimensions={1,3,5}, to_apply=%region_1.2 | reduce | flops 57344 | bytes 294916 | tf_op jit(solution)/shard_map/reduce_sum | solution.py:55
  82.6 7.0 %reduce_sum.83 = f32[8,8,128]{2,1,0:T(8,128)S(1)} reduce(f32[8,2,8,2,128,2]{5,4,3,2,1,0:T(8,128)} %reshape.122, f32[]{:T(128)} %constant.11.clone.1), dimensions={1,3,5}, to_apply=%region_2.3 | reduce | flops 57344 | bytes 294916 | tf_op jit(solution)/shard_map/reduce_sum | solution.py:55
  89.6 1.9 collective-permute-start.10
  91.5 3.6 collective-permute-start.11
  95.2 3.4 div.99
  101.5 18.1 %reshape.120 = f32[8,2,8,2,128,2]{5,4,3,2,1,0:T(8,128)} reshape(f32[16,16,256]{2,1,0:T(8,128)S(1)} %divide_add_fusion.8) | data formatting | bytes 524288 | tf_op jit(solution)/shard_map/reshape | solution.py:55
  120.9 4.2 collective-permute-start.13
  125.0 7.0 %reduce_sum.81 = f32[8,8,128]{2,1,0:T(8,128)S(1)} reduce(f32[8,2,8,2,128,2]{5,4,3,2,1,0:T(8,128)} %reshape.120, f32[]{:T(128)} %constant.11.clone.1), dimensions={1,3,5}, to_apply=%region_0.1 | reduce | flops 57344 | bytes 294916 | tf_op jit(solution)/shard_map/reduce_sum | solution.py:55
  132.1 1.9 collective-permute-start.14
  134.0 3.6 collective-permute-start.15
  139.0 5.1 collective-permute-start.21
  145.0 18.1 %reshape.123 = f32[8,2,8,2,128,2]{5,4,3,2,1,0:T(8,128)} reshape(f32[16,16,256]{2,1,0:T(8,128)S(1)} %fusion.15) | data formatting | bytes 524288 | tf_op jit(solution)/shard_map/reshape | solution.py:55
  163.1 7.0 %reduce_sum.84 = f32[8,8,128]{2,1,0:T(8,128)S(1)} reduce(f32[8,2,8,2,128,2]{5,4,3,2,1,0:T(8,128)} %reshape.123, f32[]{:T(128)} %constant.11.clone.1), dimensions={1,3,5}, to_apply=%region_3.4 | reduce | flops 57344 | bytes 294916 | tf_op jit(solution)/shard_map/reduce_sum | solution.py:55
  170.1 5.5 %collective-permute-start.16 = (f32[4,2,8,128]{3,2,1,0:T(8,128)S(1)}, f32[4,2,8,128]{3,2,1,0:T(8,128)S(1)}, u32[]{:S(2)}, u32[]{:S(2)}) collective-permute-start(f32[4,2,8,128]{3,2,1,0:T(8,128)S(1)} %get-tuple-element.82), channel_id=1, source_target_pairs={{0,32},{32,64},{64,96},{96,128},{128,160},{160,192},{192,224},{224... | collective-permute-start | bytes 98312 | tf_op jit(solution)/shard_map/ppermute | solution.py:29
  176.9 1.9 collective-permute-start.22
  178.9 3.6 collective-permute-start.23
  182.6 3.5 collective-permute-start.18
  186.1 1.9 collective-permute-start.19
  188.2 3.3 collective-permute-done.19
  193.5 6.4 %collective-permute-start.25 = (f32[1,8,128]{2,1,0:T(8,128)S(1)}, f32[1,8,128]{2,1,0:T(8,128)S(1)}, u32[]{:S(2)}, u32[]{:S(2)}) collective-permute-start(f32[1,8,128]{2,1,0:T(8,128)S(1)} %get-tuple-element.122), channel_id=1, source_target_pairs={{0,32},{32,64},{64,96},{96,128},{128,160},{160,192},{192,224},{224... | collective-permute-start | bytes 12296 | tf_op jit(solution)/shard_map/ppermute | solution.py:29
  199.9 3.4 div.96
  205.2 1.9 collective-permute-start.26
  207.1 3.6 collective-permute-start.27
  211.8 3.4 reshape.124
  216.5 5.6 %collective-permute-start.29 = (f32[1,8,128]{2,1,0:T(8,128)S(1)}, f32[1,8,128]{2,1,0:T(8,128)S(1)}, u32[]{:S(2)}, u32[]{:S(2)}) collective-permute-start(f32[1,8,128]{2,1,0:T(8,128)S(1)} %get-tuple-element.120), channel_id=1, source_target_pairs={{0,32},{32,64},{64,96},{96,128},{128,160},{160,192},{192,224},{224... | collective-permute-start | bytes 12296 | tf_op jit(solution)/shard_map/ppermute | solution.py:29
  225.9 5.2 collective-permute-start.31
  232.4 4.3 collective-permute-start.37
  237.0 3.4 reshape.125
  242.3 5.5 %collective-permute-start.32 = (f32[4,2,4,64]{3,2,1,0:T(4,128)S(1)}, f32[4,2,4,64]{3,2,1,0:T(4,128)S(1)}, u32[]{:S(2)}, u32[]{:S(2)}) collective-permute-start(f32[4,2,4,64]{3,2,1,0:T(4,128)S(1)} %get-tuple-element.114), channel_id=1, source_target_pairs={{0,32},{32,64},{64,96},{96,128},{128,160},{160,192},{192,224},{224... | collective-permute-start | bytes 24584 | tf_op jit(solution)/shard_map/ppermute | solution.py:29
  249.1 1.9 collective-permute-start.38
  251.0 3.9 collective-permute-start.39
  255.0 4.7 collective-permute-start.34
  261.8 3.4 collective-permute-done.35
  266.9 6.8 %collective-permute-start.41 = (f32[1,4,64]{2,1,0:T(4,128)S(1)}, f32[1,4,64]{2,1,0:T(4,128)S(1)}, u32[]{:S(2)}, u32[]{:S(2)}) collective-permute-start(f32[1,4,64]{2,1,0:T(4,128)S(1)} %get-tuple-element.140), channel_id=1, source_target_pairs={{0,32},{32,64},{64,96},{96,128},{128,160},{160,192},{192,224},{224... | collective-permute-start | bytes 3080 | tf_op jit(solution)/shard_map/ppermute | solution.py:29
  276.3 4.1 collective-permute-start.43
  282.6 6.1 %collective-permute-start.45 = (f32[1,4,64]{2,1,0:T(4,128)S(1)}, f32[1,4,64]{2,1,0:T(4,128)S(1)}, u32[]{:S(2)}, u32[]{:S(2)}) collective-permute-start(f32[1,4,64]{2,1,0:T(4,128)S(1)} %get-tuple-element.138), channel_id=1, source_target_pairs={{0,32},{32,64},{64,96},{96,128},{128,160},{160,192},{192,224},{224... | collective-permute-start | bytes 3080 | tf_op jit(solution)/shard_map/ppermute | solution.py:29
  289.4 1.9 collective-permute-start.46
  291.4 5.0 collective-permute-start.47
  298.6 4.5 collective-permute-start.49
  305.8 5.1 collective-permute-start.51
  313.6 5.8 %collective-permute-start.53 = (f32[1,8,128]{2,1,0:T(8,128)S(1)}, f32[1,8,128]{2,1,0:T(8,128)S(1)}, u32[]{:S(2)}, u32[]{:S(2)}) collective-permute-start(f32[1,8,128]{2,1,0:T(8,128)S(1)} %get-tuple-element.106), channel_id=1, source_target_pairs={{0,32},{32,64},{64,96},{96,128},{128,160},{160,192},{192,224},{224... | collective-permute-start | bytes 12296 | tf_op jit(solution)/shard_map/ppermute | solution.py:29
  322.1 5.5 %collective-permute-start.55 = (f32[10,1,128]{2,1,0:T(1,128)S(1)}, f32[10,1,128]{2,1,0:T(1,128)S(1)}, u32[]{:S(2)}, u32[]{:S(2)}) collective-permute-start(f32[10,1,128]{2,1,0:T(1,128)S(1)} %get-tuple-element.96), channel_id=1, source_target_pairs={{0,1},{1,2},{2,3},{3,4},{4,5},{5,6},{6,7},{7,8},{8,9},{9,10},{10,1... | collective-permute-start | bytes 15368 | tf_op jit(solution)/shard_map/ppermute | solution.py:29
  330.9 6.4 %collective-permute-start.57 = (f32[1,8,128]{2,1,0:T(8,128)S(1)}, f32[1,8,128]{2,1,0:T(8,128)S(1)}, u32[]{:S(2)}, u32[]{:S(2)}) collective-permute-start(f32[1,8,128]{2,1,0:T(8,128)S(1)} %get-tuple-element.104), channel_id=1, source_target_pairs={{0,32},{32,64},{64,96},{96,128},{128,160},{160,192},{192,224},{224... | collective-permute-start | bytes 12296 | tf_op jit(solution)/shard_map/ppermute | solution.py:29
  340.0 5.0 collective-permute-start.59
  348.5 2.7 broadcast_in_dim.23
  351.2 2.5 copy.506
  355.0 6.6 %collective-permute-start.61 = (f32[1,16,256]{2,1,0:T(8,128)S(1)}, f32[1,16,256]{2,1,0:T(8,128)S(1)}, u32[]{:S(2)}, u32[]{:S(2)}) collective-permute-start(f32[1,16,256]{2,1,0:T(8,128)S(1)} %get-tuple-element.64), channel_id=1, source_target_pairs={{0,32},{32,64},{64,96},{96,128},{128,160},{160,192},{192,224},{224... | collective-permute-start | bytes 49160 | tf_op jit(solution)/shard_map/ppermute | solution.py:29
  364.5 5.0 collective-permute-start.63
  372.8 6.6 %collective-permute-start.65 = (f32[1,16,256]{2,1,0:T(8,128)S(1)}, f32[1,16,256]{2,1,0:T(8,128)S(1)}, u32[]{:S(2)}, u32[]{:S(2)}) collective-permute-start(f32[1,16,256]{2,1,0:T(8,128)S(1)} %get-tuple-element.62), channel_id=1, source_target_pairs={{0,32},{32,64},{64,96},{96,128},{128,160},{160,192},{192,224},{224... | collective-permute-start | bytes 49160 | tf_op jit(solution)/shard_map/ppermute | solution.py:29
  382.2 5.1 collective-permute-start.67
  390.5 6.6 %collective-permute-start.69 = (f32[1,16,256]{2,1,0:T(8,128)S(1)}, f32[1,16,256]{2,1,0:T(8,128)S(1)}, u32[]{:S(2)}, u32[]{:S(2)}) collective-permute-start(f32[1,16,256]{2,1,0:T(8,128)S(1)} %get-tuple-element.60), channel_id=1, source_target_pairs={{0,32},{32,64},{64,96},{96,128},{128,160},{160,192},{192,224},{224... | collective-permute-start | bytes 49160 | tf_op jit(solution)/shard_map/ppermute | solution.py:29
  400.0 5.1 collective-permute-start.71
  407.4 134.3 %psum.7 = f32[]{:T(128)} all-reduce(f32[]{:T(128)} %fusion.130), channel_id=1, replica_groups=mesh['gx'=16,'gy'=32] {'gx','gy'}, use_global_device_ids=true, to_apply=%region_9.10 | all-reduce | flops 1 | bytes 8 | tf_op jit(solution)/shard_map/psum | solution.py:120
  (235 shorter events, 78.6 us)
Async XLA Ops:
  1.5 10.7 %collective-permute-start.5 = (f32[1,16,256]{2,1,0:T(8,128)S(1)}, f32[1,16,256]{2,1,0:T(8,128)S(1)}, u32[]{:S(2)}, u32[]{:S(2)}) collective-permute-start(f32[1,16,256]{2,1,0:T(8,128)S(1)} %get-tuple-element.71), channel_id=1, source_target_pairs={{0,32},{32,64},{64,96},{96,128},{128,160},{160,192},{192,224},{224... | collective-permute-start | bytes 49160 | tf_op jit(solution)/shard_map/ppermute | solution.py:29
  6.3 17.4 %collective-permute-start = (f32[3,1,16,256]{3,2,1,0:T(8,128)S(1)}, f32[3,1,16,256]{3,2,1,0:T(8,128)S(1)}, u32[]{:S(2)}, u32[]{:S(2)}) collective-permute-start(f32[3,1,16,256]{3,2,1,0:T(8,128)S(1)} %get-tuple-element.40), channel_id=1, source_target_pairs={{0,32},{32,64},{64,96},{96,128},{128,160},{160,192},{192,224},{224... | collective-permute-start | bytes 147464 | tf_op jit(solution)/shard_map/ppermute | solution.py:29
  9.5 14.2 %collective-permute-start.1 = (f32[3,1,16,256]{3,2,1,0:T(8,128)S(1)}, f32[3,1,16,256]{3,2,1,0:T(8,128)S(1)}, u32[]{:S(2)}, u32[]{:S(2)}) collective-permute-start(f32[3,1,16,256]{3,2,1,0:T(8,128)S(1)} %get-tuple-element.41), channel_id=1, source_target_pairs={{32,0},{64,32},{96,64},{128,96},{160,128},{192,160},{224,192},{256... | collective-permute-start | bytes 147464 | tf_op jit(solution)/shard_map/ppermute | solution.py:30
  16.0 12.2 %collective-permute-start.6 = (f32[18,1,256]{2,1,0:T(1,128)S(1)}, f32[18,1,256]{2,1,0:T(1,128)S(1)}, u32[]{:S(2)}, u32[]{:S(2)}) collective-permute-start(f32[18,1,256]{2,1,0:T(1,128)S(1)} %get-tuple-element.59), channel_id=1, source_target_pairs={{1,0},{2,1},{3,2},{4,3},{5,4},{6,5},{7,6},{8,7},{9,8},{10,9},{11,1... | collective-permute-start | bytes 55304 | tf_op jit(solution)/shard_map/ppermute | solution.py:30
  21.3 7.0 %collective-permute-start.7 = (f32[18,1,256]{2,1,0:T(1,128)S(1)}, f32[18,1,256]{2,1,0:T(1,128)S(1)}, u32[]{:S(2)}, u32[]{:S(2)}) collective-permute-start(f32[18,1,256]{2,1,0:T(1,128)S(1)} %get-tuple-element.58), channel_id=1, source_target_pairs={{0,1},{1,2},{2,3},{3,4},{4,5},{5,6},{6,7},{7,8},{8,9},{9,10},{10,1... | collective-permute-start | bytes 55304 | tf_op jit(solution)/shard_map/ppermute | solution.py:29
  33.8 55.7 %collective-permute-start.8 = (f32[1,16,256]{2,1,0:T(8,128)S(1)}, f32[1,16,256]{2,1,0:T(8,128)S(1)}, u32[]{:S(2)}, u32[]{:S(2)}) collective-permute-start(f32[1,16,256]{2,1,0:T(8,128)S(1)} %get-tuple-element.69), channel_id=1, source_target_pairs={{32,0},{64,32},{96,64},{128,96},{160,128},{192,160},{224,192},{256... | collective-permute-start | bytes 49160 | tf_op jit(solution)/shard_map/ppermute | solution.py:30
  35.1 54.4 %collective-permute-start.9 = (f32[1,16,256]{2,1,0:T(8,128)S(1)}, f32[1,16,256]{2,1,0:T(8,128)S(1)}, u32[]{:S(2)}, u32[]{:S(2)}) collective-permute-start(f32[1,16,256]{2,1,0:T(8,128)S(1)} %get-tuple-element.68), channel_id=1, source_target_pairs={{0,32},{32,64},{64,96},{96,128},{128,160},{160,192},{192,224},{224... | collective-permute-start | bytes 49160 | tf_op jit(solution)/shard_map/ppermute | solution.py:29
  89.6 10.8 %collective-permute-start.10 = (f32[18,1,256]{2,1,0:T(1,128)S(1)}, f32[18,1,256]{2,1,0:T(1,128)S(1)}, u32[]{:S(2)}, u32[]{:S(2)}) collective-permute-start(f32[18,1,256]{2,1,0:T(1,128)S(1)} %get-tuple-element.57), channel_id=1, source_target_pairs={{1,0},{2,1},{3,2},{4,3},{5,4},{6,5},{7,6},{8,7},{9,8},{10,9},{11,1... | collective-permute-start | bytes 55304 | tf_op jit(solution)/shard_map/ppermute | solution.py:30
  91.5 8.9 %collective-permute-start.11 = (f32[18,1,256]{2,1,0:T(1,128)S(1)}, f32[18,1,256]{2,1,0:T(1,128)S(1)}, u32[]{:S(2)}, u32[]{:S(2)}) collective-permute-start(f32[18,1,256]{2,1,0:T(1,128)S(1)} %get-tuple-element.56), channel_id=1, source_target_pairs={{0,1},{1,2},{2,3},{3,4},{4,5},{5,6},{6,7},{7,8},{8,9},{9,10},{10,1... | collective-permute-start | bytes 55304 | tf_op jit(solution)/shard_map/ppermute | solution.py:29
  119.6 12.5 %collective-permute-start.12 = (f32[1,16,256]{2,1,0:T(8,128)S(1)}, f32[1,16,256]{2,1,0:T(8,128)S(1)}, u32[]{:S(2)}, u32[]{:S(2)}) collective-permute-start(f32[1,16,256]{2,1,0:T(8,128)S(1)} %get-tuple-element.67), channel_id=1, source_target_pairs={{32,0},{64,32},{96,64},{128,96},{160,128},{192,160},{224,192},{256... | collective-permute-start | bytes 49160 | tf_op jit(solution)/shard_map/ppermute | solution.py:30
  120.9 11.2 %collective-permute-start.13 = (f32[1,16,256]{2,1,0:T(8,128)S(1)}, f32[1,16,256]{2,1,0:T(8,128)S(1)}, u32[]{:S(2)}, u32[]{:S(2)}) collective-permute-start(f32[1,16,256]{2,1,0:T(8,128)S(1)} %get-tuple-element.66), channel_id=1, source_target_pairs={{0,32},{32,64},{64,96},{96,128},{128,160},{160,192},{192,224},{224... | collective-permute-start | bytes 49160 | tf_op jit(solution)/shard_map/ppermute | solution.py:29
  132.1 12.0 %collective-permute-start.14 = (f32[18,1,256]{2,1,0:T(1,128)S(1)}, f32[18,1,256]{2,1,0:T(1,128)S(1)}, u32[]{:S(2)}, u32[]{:S(2)}) collective-permute-start(f32[18,1,256]{2,1,0:T(1,128)S(1)} %get-tuple-element.55), channel_id=1, source_target_pairs={{1,0},{2,1},{3,2},{4,3},{5,4},{6,5},{7,6},{8,7},{9,8},{10,9},{11,1... | collective-permute-start | bytes 55304 | tf_op jit(solution)/shard_map/ppermute | solution.py:30
  134.0 10.0 %collective-permute-start.15 = (f32[18,1,256]{2,1,0:T(1,128)S(1)}, f32[18,1,256]{2,1,0:T(1,128)S(1)}, u32[]{:S(2)}, u32[]{:S(2)}) collective-permute-start(f32[18,1,256]{2,1,0:T(1,128)S(1)} %get-tuple-element.54), channel_id=1, source_target_pairs={{0,1},{1,2},{2,3},{3,4},{4,5},{5,6},{6,7},{7,8},{8,9},{9,10},{10,1... | collective-permute-start | bytes 55304 | tf_op jit(solution)/shard_map/ppermute | solution.py:29
  137.7 39.2 %collective-permute-start.20 = (f32[1,8,128]{2,1,0:T(8,128)S(1)}, f32[1,8,128]{2,1,0:T(8,128)S(1)}, u32[]{:S(2)}, u32[]{:S(2)}) collective-permute-start(f32[1,8,128]{2,1,0:T(8,128)S(1)} %get-tuple-element.127), channel_id=1, source_target_pairs={{32,0},{64,32},{96,64},{128,96},{160,128},{192,160},{224,192},{256... | collective-permute-start | bytes 12296 | tf_op jit(solution)/shard_map/ppermute | solution.py:30
  139.0 37.9 %collective-permute-start.21 = (f32[1,8,128]{2,1,0:T(8,128)S(1)}, f32[1,8,128]{2,1,0:T(8,128)S(1)}, u32[]{:S(2)}, u32[]{:S(2)}) collective-permute-start(f32[1,8,128]{2,1,0:T(8,128)S(1)} %get-tuple-element.126), channel_id=1, source_target_pairs={{0,32},{32,64},{64,96},{96,128},{128,160},{160,192},{192,224},{224... | collective-permute-start | bytes 12296 | tf_op jit(solution)/shard_map/ppermute | solution.py:29
  170.1 12.4 %collective-permute-start.16 = (f32[4,2,8,128]{3,2,1,0:T(8,128)S(1)}, f32[4,2,8,128]{3,2,1,0:T(8,128)S(1)}, u32[]{:S(2)}, u32[]{:S(2)}) collective-permute-start(f32[4,2,8,128]{3,2,1,0:T(8,128)S(1)} %get-tuple-element.82), channel_id=1, source_target_pairs={{0,32},{32,64},{64,96},{96,128},{128,160},{160,192},{192,224},{224... | collective-permute-start | bytes 98312 | tf_op jit(solution)/shard_map/ppermute | solution.py:29
  175.6 6.9 %collective-permute-start.17 = (f32[4,2,8,128]{3,2,1,0:T(8,128)S(1)}, f32[4,2,8,128]{3,2,1,0:T(8,128)S(1)}, u32[]{:S(2)}, u32[]{:S(2)}) collective-permute-start(f32[4,2,8,128]{3,2,1,0:T(8,128)S(1)} %get-tuple-element.83), channel_id=1, source_target_pairs={{32,0},{64,32},{96,64},{128,96},{160,128},{192,160},{224,192},{256... | collective-permute-start | bytes 98312 | tf_op jit(solution)/shard_map/ppermute | solution.py:30
  176.9 11.1 %collective-permute-start.22 = (f32[10,1,128]{2,1,0:T(1,128)S(1)}, f32[10,1,128]{2,1,0:T(1,128)S(1)}, u32[]{:S(2)}, u32[]{:S(2)}) collective-permute-start(f32[10,1,128]{2,1,0:T(1,128)S(1)} %get-tuple-element.103), channel_id=1, source_target_pairs={{1,0},{2,1},{3,2},{4,3},{5,4},{6,5},{7,6},{8,7},{9,8},{10,9},{11,1... | collective-permute-start | bytes 15368 | tf_op jit(solution)/shard_map/ppermute | solution.py:30
  178.9 9.2 %collective-permute-start.23 = (f32[10,1,128]{2,1,0:T(1,128)S(1)}, f32[10,1,128]{2,1,0:T(1,128)S(1)}, u32[]{:S(2)}, u32[]{:S(2)}) collective-permute-start(f32[10,1,128]{2,1,0:T(1,128)S(1)} %get-tuple-element.102), channel_id=1, source_target_pairs={{0,1},{1,2},{2,3},{3,4},{4,5},{5,6},{6,7},{7,8},{8,9},{9,10},{10,1... | collective-permute-start | bytes 15368 | tf_op jit(solution)/shard_map/ppermute | solution.py:29
  182.6 5.6 %collective-permute-start.18 = (f32[4,12,2,128]{3,0,2,1:T(4,128)S(1)}, f32[4,12,2,128]{3,0,2,1:T(4,128)S(1)}, u32[]{:S(2)}, u32[]{:S(2)}) collective-permute-start(f32[4,12,2,128]{3,0,2,1:T(4,128)S(1)} %copy.507), channel_id=1, source_target_pairs={{0,1},{1,2},{2,3},{3,4},{4,5},{5,6},{6,7},{7,8},{8,9},{9,10},{10,1... | collective-permute-start | bytes 147464 | tf_op jit(solution)/shard_map/ppermute | solution.py:29
  192.2 12.9 %collective-permute-start.24 = (f32[1,8,128]{2,1,0:T(8,128)S(1)}, f32[1,8,128]{2,1,0:T(8,128)S(1)}, u32[]{:S(2)}, u32[]{:S(2)}) collective-permute-start(f32[1,8,128]{2,1,0:T(8,128)S(1)} %get-tuple-element.123), channel_id=1, source_target_pairs={{32,0},{64,32},{96,64},{128,96},{160,128},{192,160},{224,192},{256... | collective-permute-start | bytes 12296 | tf_op jit(solution)/shard_map/ppermute | solution.py:30
  193.5 11.6 %collective-permute-start.25 = (f32[1,8,128]{2,1,0:T(8,128)S(1)}, f32[1,8,128]{2,1,0:T(8,128)S(1)}, u32[]{:S(2)}, u32[]{:S(2)}) collective-permute-start(f32[1,8,128]{2,1,0:T(8,128)S(1)} %get-tuple-element.122), channel_id=1, source_target_pairs={{0,32},{32,64},{64,96},{96,128},{128,160},{160,192},{192,224},{224... | collective-permute-start | bytes 12296 | tf_op jit(solution)/shard_map/ppermute | solution.py:29
  205.2 5.6 %collective-permute-start.26 = (f32[10,1,128]{2,1,0:T(1,128)S(1)}, f32[10,1,128]{2,1,0:T(1,128)S(1)}, u32[]{:S(2)}, u32[]{:S(2)}) collective-permute-start(f32[10,1,128]{2,1,0:T(1,128)S(1)} %get-tuple-element.101), channel_id=1, source_target_pairs={{1,0},{2,1},{3,2},{4,3},{5,4},{6,5},{7,6},{8,7},{9,8},{10,9},{11,1... | collective-permute-start | bytes 15368 | tf_op jit(solution)/shard_map/ppermute | solution.py:30
  215.2 8.7 %collective-permute-start.28 = (f32[1,8,128]{2,1,0:T(8,128)S(1)}, f32[1,8,128]{2,1,0:T(8,128)S(1)}, u32[]{:S(2)}, u32[]{:S(2)}) collective-permute-start(f32[1,8,128]{2,1,0:T(8,128)S(1)} %get-tuple-element.121), channel_id=1, source_target_pairs={{32,0},{64,32},{96,64},{128,96},{160,128},{192,160},{224,192},{256... | collective-permute-start | bytes 12296 | tf_op jit(solution)/shard_map/ppermute | solution.py:30
  216.5 7.5 %collective-permute-start.29 = (f32[1,8,128]{2,1,0:T(8,128)S(1)}, f32[1,8,128]{2,1,0:T(8,128)S(1)}, u32[]{:S(2)}, u32[]{:S(2)}) collective-permute-start(f32[1,8,128]{2,1,0:T(8,128)S(1)} %get-tuple-element.120), channel_id=1, source_target_pairs={{0,32},{32,64},{64,96},{96,128},{128,160},{160,192},{192,224},{224... | collective-permute-start | bytes 12296 | tf_op jit(solution)/shard_map/ppermute | solution.py:29
  223.9 12.7 %collective-permute-start.30 = (f32[10,1,128]{2,1,0:T(1,128)S(1)}, f32[10,1,128]{2,1,0:T(1,128)S(1)}, u32[]{:S(2)}, u32[]{:S(2)}) collective-permute-start(f32[10,1,128]{2,1,0:T(1,128)S(1)} %get-tuple-element.99), channel_id=1, source_target_pairs={{1,0},{2,1},{3,2},{4,3},{5,4},{6,5},{7,6},{8,7},{9,8},{10,9},{11,1... | collective-permute-start | bytes 15368 | tf_op jit(solution)/shard_map/ppermute | solution.py:30
  225.9 10.8 %collective-permute-start.31 = (f32[10,1,128]{2,1,0:T(1,128)S(1)}, f32[10,1,128]{2,1,0:T(1,128)S(1)}, u32[]{:S(2)}, u32[]{:S(2)}) collective-permute-start(f32[10,1,128]{2,1,0:T(1,128)S(1)} %get-tuple-element.98), channel_id=1, source_target_pairs={{0,1},{1,2},{2,3},{3,4},{4,5},{5,6},{6,7},{7,8},{8,9},{9,10},{10,1... | collective-permute-start | bytes 15368 | tf_op jit(solution)/shard_map/ppermute | solution.py:29
  231.1 18.0 %collective-permute-start.36 = (f32[1,4,64]{2,1,0:T(4,128)S(1)}, f32[1,4,64]{2,1,0:T(4,128)S(1)}, u32[]{:S(2)}, u32[]{:S(2)}) collective-permute-start(f32[1,4,64]{2,1,0:T(4,128)S(1)} %get-tuple-element.145), channel_id=1, source_target_pairs={{32,0},{64,32},{96,64},{128,96},{160,128},{192,160},{224,192},{256... | collective-permute-start | bytes 3080 | tf_op jit(solution)/shard_map/ppermute | solution.py:30
  232.4 16.7 %collective-permute-start.37 = (f32[1,4,64]{2,1,0:T(4,128)S(1)}, f32[1,4,64]{2,1,0:T(4,128)S(1)}, u32[]{:S(2)}, u32[]{:S(2)}) collective-permute-start(f32[1,4,64]{2,1,0:T(4,128)S(1)} %get-tuple-element.144), channel_id=1, source_target_pairs={{0,32},{32,64},{64,96},{96,128},{128,160},{160,192},{192,224},{224... | collective-permute-start | bytes 3080 | tf_op jit(solution)/shard_map/ppermute | solution.py:29
  242.3 12.6 %collective-permute-start.32 = (f32[4,2,4,64]{3,2,1,0:T(4,128)S(1)}, f32[4,2,4,64]{3,2,1,0:T(4,128)S(1)}, u32[]{:S(2)}, u32[]{:S(2)}) collective-permute-start(f32[4,2,4,64]{3,2,1,0:T(4,128)S(1)} %get-tuple-element.114), channel_id=1, source_target_pairs={{0,32},{32,64},{64,96},{96,128},{128,160},{160,192},{192,224},{224... | collective-permute-start | bytes 24584 | tf_op jit(solution)/shard_map/ppermute | solution.py:29
  247.8 7.2 %collective-permute-start.33 = (f32[4,2,4,64]{3,2,1,0:T(4,128)S(1)}, f32[4,2,4,64]{3,2,1,0:T(4,128)S(1)}, u32[]{:S(2)}, u32[]{:S(2)}) collective-permute-start(f32[4,2,4,64]{3,2,1,0:T(4,128)S(1)} %get-tuple-element.115), channel_id=1, source_target_pairs={{32,0},{64,32},{96,64},{128,96},{160,128},{192,160},{224,192},{256... | collective-permute-start | bytes 24584 | tf_op jit(solution)/shard_map/ppermute | solution.py:30
  249.1 12.5 %collective-permute-start.38 = (f32[6,1,64]{2,1,0:T(1,128)S(1)}, f32[6,1,64]{2,1,0:T(1,128)S(1)}, u32[]{:S(2)}, u32[]{:S(2)}) collective-permute-start(f32[6,1,64]{2,1,0:T(1,128)S(1)} %get-tuple-element.135), channel_id=1, source_target_pairs={{1,0},{2,1},{3,2},{4,3},{5,4},{6,5},{7,6},{8,7},{9,8},{10,9},{11,1... | collective-permute-start | bytes 4616 | tf_op jit(solution)/shard_map/ppermute | solution.py:30
  251.0 10.6 %collective-permute-start.39 = (f32[6,1,64]{2,1,0:T(1,128)S(1)}, f32[6,1,64]{2,1,0:T(1,128)S(1)}, u32[]{:S(2)}, u32[]{:S(2)}) collective-permute-start(f32[6,1,64]{2,1,0:T(1,128)S(1)} %get-tuple-element.134), channel_id=1, source_target_pairs={{0,1},{1,2},{2,3},{3,4},{4,5},{5,6},{6,7},{7,8},{8,9},{9,10},{10,1... | collective-permute-start | bytes 4616 | tf_op jit(solution)/shard_map/ppermute | solution.py:29
  255.0 6.8 %collective-permute-start.34 = (f32[4,8,2,64]{3,2,1,0:T(2,128)S(1)}, f32[4,8,2,64]{3,2,1,0:T(2,128)S(1)}, u32[]{:S(2)}, u32[]{:S(2)}) collective-permute-start(f32[4,8,2,64]{3,2,1,0:T(2,128)S(1)} %get-tuple-element.92), channel_id=1, source_target_pairs={{0,1},{1,2},{2,3},{3,4},{4,5},{5,6},{6,7},{7,8},{8,9},{9,10},{10,1... | collective-permute-start | bytes 49160 | tf_op jit(solution)/shard_map/ppermute | solution.py:29
  265.6 8.1 %collective-permute-start.40 = (f32[1,4,64]{2,1,0:T(4,128)S(1)}, f32[1,4,64]{2,1,0:T(4,128)S(1)}, u32[]{:S(2)}, u32[]{:S(2)}) collective-permute-start(f32[1,4,64]{2,1,0:T(4,128)S(1)} %get-tuple-element.141), channel_id=1, source_target_pairs={{32,0},{64,32},{96,64},{128,96},{160,128},{192,160},{224,192},{256... | collective-permute-start | bytes 3080 | tf_op jit(solution)/shard_map/ppermute | solution.py:30
  266.9 7.5 %collective-permute-start.41 = (f32[1,4,64]{2,1,0:T(4,128)S(1)}, f32[1,4,64]{2,1,0:T(4,128)S(1)}, u32[]{:S(2)}, u32[]{:S(2)}) collective-permute-start(f32[1,4,64]{2,1,0:T(4,128)S(1)} %get-tuple-element.140), channel_id=1, source_target_pairs={{0,32},{32,64},{64,96},{96,128},{128,160},{160,192},{192,224},{224... | collective-permute-start | bytes 3080 | tf_op jit(solution)/shard_map/ppermute | solution.py:29
  274.4 6.0 %collective-permute-start.42 = (f32[6,1,64]{2,1,0:T(1,128)S(1)}, f32[6,1,64]{2,1,0:T(1,128)S(1)}, u32[]{:S(2)}, u32[]{:S(2)}) collective-permute-start(f32[6,1,64]{2,1,0:T(1,128)S(1)} %get-tuple-element.133), channel_id=1, source_target_pairs={{1,0},{2,1},{3,2},{4,3},{5,4},{6,5},{7,6},{8,7},{9,8},{10,9},{11,1... | collective-permute-start | bytes 4616 | tf_op jit(solution)/shard_map/ppermute | solution.py:30
  281.3 7.4 %collective-permute-start.44 = (f32[1,4,64]{2,1,0:T(4,128)S(1)}, f32[1,4,64]{2,1,0:T(4,128)S(1)}, u32[]{:S(2)}, u32[]{:S(2)}) collective-permute-start(f32[1,4,64]{2,1,0:T(4,128)S(1)} %get-tuple-element.139), channel_id=1, source_target_pairs={{32,0},{64,32},{96,64},{128,96},{160,128},{192,160},{224,192},{256... | collective-permute-start | bytes 3080 | tf_op jit(solution)/shard_map/ppermute | solution.py:30
  282.6 6.8 %collective-permute-start.45 = (f32[1,4,64]{2,1,0:T(4,128)S(1)}, f32[1,4,64]{2,1,0:T(4,128)S(1)}, u32[]{:S(2)}, u32[]{:S(2)}) collective-permute-start(f32[1,4,64]{2,1,0:T(4,128)S(1)} %get-tuple-element.138), channel_id=1, source_target_pairs={{0,32},{32,64},{64,96},{96,128},{128,160},{160,192},{192,224},{224... | collective-permute-start | bytes 3080 | tf_op jit(solution)/shard_map/ppermute | solution.py:29
  289.4 7.0 %collective-permute-start.46 = (f32[6,1,64]{2,1,0:T(1,128)S(1)}, f32[6,1,64]{2,1,0:T(1,128)S(1)}, u32[]{:S(2)}, u32[]{:S(2)}) collective-permute-start(f32[6,1,64]{2,1,0:T(1,128)S(1)} %get-tuple-element.131), channel_id=1, source_target_pairs={{1,0},{2,1},{3,2},{4,3},{5,4},{6,5},{7,6},{8,7},{9,8},{10,9},{11,1... | collective-permute-start | bytes 4616 | tf_op jit(solution)/shard_map/ppermute | solution.py:30
  291.4 5.8 %collective-permute-start.47 = (f32[6,1,64]{2,1,0:T(1,128)S(1)}, f32[6,1,64]{2,1,0:T(1,128)S(1)}, u32[]{:S(2)}, u32[]{:S(2)}) collective-permute-start(f32[6,1,64]{2,1,0:T(1,128)S(1)} %get-tuple-element.130), channel_id=1, source_target_pairs={{0,1},{1,2},{2,3},{3,4},{4,5},{5,6},{6,7},{7,8},{8,9},{9,10},{10,1... | collective-permute-start | bytes 4616 | tf_op jit(solution)/shard_map/ppermute | solution.py:29
  297.3 5.8 %collective-permute-start.48 = (f32[1,4,64]{2,1,0:T(4,128)S(1)}, f32[1,4,64]{2,1,0:T(4,128)S(1)}, u32[]{:S(2)}, u32[]{:S(2)}) collective-permute-start(f32[1,4,64]{2,1,0:T(4,128)S(1)} %get-tuple-element.137), channel_id=1, source_target_pairs={{32,0},{64,32},{96,64},{128,96},{160,128},{192,160},{224,192},{256... | collective-permute-start | bytes 3080 | tf_op jit(solution)/shard_map/ppermute | solution.py:30
  303.9 7.0 %collective-permute-start.50 = (f32[6,1,64]{2,1,0:T(1,128)S(1)}, f32[6,1,64]{2,1,0:T(1,128)S(1)}, u32[]{:S(2)}, u32[]{:S(2)}) collective-permute-start(f32[6,1,64]{2,1,0:T(1,128)S(1)} %get-tuple-element.129), channel_id=1, source_target_pairs={{1,0},{2,1},{3,2},{4,3},{5,4},{6,5},{7,6},{8,7},{9,8},{10,9},{11,1... | collective-permute-start | bytes 4616 | tf_op jit(solution)/shard_map/ppermute | solution.py:30
  305.8 5.8 %collective-permute-start.51 = (f32[6,1,64]{2,1,0:T(1,128)S(1)}, f32[6,1,64]{2,1,0:T(1,128)S(1)}, u32[]{:S(2)}, u32[]{:S(2)}) collective-permute-start(f32[6,1,64]{2,1,0:T(1,128)S(1)} %get-tuple-element.128), channel_id=1, source_target_pairs={{0,1},{1,2},{2,3},{3,4},{4,5},{5,6},{6,7},{7,8},{8,9},{9,10},{10,1... | collective-permute-start | bytes 4616 | tf_op jit(solution)/shard_map/ppermute | solution.py:29
  312.3 7.2 %collective-permute-start.52 = (f32[1,8,128]{2,1,0:T(8,128)S(1)}, f32[1,8,128]{2,1,0:T(8,128)S(1)}, u32[]{:S(2)}, u32[]{:S(2)}) collective-permute-start(f32[1,8,128]{2,1,0:T(8,128)S(1)} %get-tuple-element.107), channel_id=1, source_target_pairs={{32,0},{64,32},{96,64},{128,96},{160,128},{192,160},{224,192},{256... | collective-permute-start | bytes 12296 | tf_op jit(solution)/shard_map/ppermute | solution.py:30
  313.6 6.6 %collective-permute-start.53 = (f32[1,8,128]{2,1,0:T(8,128)S(1)}, f32[1,8,128]{2,1,0:T(8,128)S(1)}, u32[]{:S(2)}, u32[]{:S(2)}) collective-permute-start(f32[1,8,128]{2,1,0:T(8,128)S(1)} %get-tuple-element.106), channel_id=1, source_target_pairs={{0,32},{32,64},{64,96},{96,128},{128,160},{160,192},{192,224},{224... | collective-permute-start | bytes 12296 | tf_op jit(solution)/shard_map/ppermute | solution.py:29
  320.2 7.5 %collective-permute-start.54 = (f32[10,1,128]{2,1,0:T(1,128)S(1)}, f32[10,1,128]{2,1,0:T(1,128)S(1)}, u32[]{:S(2)}, u32[]{:S(2)}) collective-permute-start(f32[10,1,128]{2,1,0:T(1,128)S(1)} %get-tuple-element.97), channel_id=1, source_target_pairs={{1,0},{2,1},{3,2},{4,3},{5,4},{6,5},{7,6},{8,7},{9,8},{10,9},{11,1... | collective-permute-start | bytes 15368 | tf_op jit(solution)/shard_map/ppermute | solution.py:30
  322.1 6.3 %collective-permute-start.55 = (f32[10,1,128]{2,1,0:T(1,128)S(1)}, f32[10,1,128]{2,1,0:T(1,128)S(1)}, u32[]{:S(2)}, u32[]{:S(2)}) collective-permute-start(f32[10,1,128]{2,1,0:T(1,128)S(1)} %get-tuple-element.96), channel_id=1, source_target_pairs={{0,1},{1,2},{2,3},{3,4},{4,5},{5,6},{6,7},{7,8},{8,9},{9,10},{10,1... | collective-permute-start | bytes 15368 | tf_op jit(solution)/shard_map/ppermute | solution.py:29
  329.6 7.7 %collective-permute-start.56 = (f32[1,8,128]{2,1,0:T(8,128)S(1)}, f32[1,8,128]{2,1,0:T(8,128)S(1)}, u32[]{:S(2)}, u32[]{:S(2)}) collective-permute-start(f32[1,8,128]{2,1,0:T(8,128)S(1)} %get-tuple-element.105), channel_id=1, source_target_pairs={{32,0},{64,32},{96,64},{128,96},{160,128},{192,160},{224,192},{256... | collective-permute-start | bytes 12296 | tf_op jit(solution)/shard_map/ppermute | solution.py:30
  330.9 7.1 %collective-permute-start.57 = (f32[1,8,128]{2,1,0:T(8,128)S(1)}, f32[1,8,128]{2,1,0:T(8,128)S(1)}, u32[]{:S(2)}, u32[]{:S(2)}) collective-permute-start(f32[1,8,128]{2,1,0:T(8,128)S(1)} %get-tuple-element.104), channel_id=1, source_target_pairs={{0,32},{32,64},{64,96},{96,128},{128,160},{160,192},{192,224},{224... | collective-permute-start | bytes 12296 | tf_op jit(solution)/shard_map/ppermute | solution.py:29
  338.0 7.0 %collective-permute-start.58 = (f32[10,1,128]{2,1,0:T(1,128)S(1)}, f32[10,1,128]{2,1,0:T(1,128)S(1)}, u32[]{:S(2)}, u32[]{:S(2)}) collective-permute-start(f32[10,1,128]{2,1,0:T(1,128)S(1)} %get-tuple-element.95), channel_id=1, source_target_pairs={{1,0},{2,1},{3,2},{4,3},{5,4},{6,5},{7,6},{8,7},{9,8},{10,9},{11,1... | collective-permute-start | bytes 15368 | tf_op jit(solution)/shard_map/ppermute | solution.py:30
  340.0 5.8 %collective-permute-start.59 = (f32[10,1,128]{2,1,0:T(1,128)S(1)}, f32[10,1,128]{2,1,0:T(1,128)S(1)}, u32[]{:S(2)}, u32[]{:S(2)}) collective-permute-start(f32[10,1,128]{2,1,0:T(1,128)S(1)} %get-tuple-element.94), channel_id=1, source_target_pairs={{0,1},{1,2},{2,3},{3,4},{4,5},{5,6},{6,7},{7,8},{8,9},{9,10},{10,1... | collective-permute-start | bytes 15368 | tf_op jit(solution)/shard_map/ppermute | solution.py:29
  353.7 7.9 %collective-permute-start.60 = (f32[1,16,256]{2,1,0:T(8,128)S(1)}, f32[1,16,256]{2,1,0:T(8,128)S(1)}, u32[]{:S(2)}, u32[]{:S(2)}) collective-permute-start(f32[1,16,256]{2,1,0:T(8,128)S(1)} %get-tuple-element.65), channel_id=1, source_target_pairs={{32,0},{64,32},{96,64},{128,96},{160,128},{192,160},{224,192},{256... | collective-permute-start | bytes 49160 | tf_op jit(solution)/shard_map/ppermute | solution.py:30
  355.0 7.5 %collective-permute-start.61 = (f32[1,16,256]{2,1,0:T(8,128)S(1)}, f32[1,16,256]{2,1,0:T(8,128)S(1)}, u32[]{:S(2)}, u32[]{:S(2)}) collective-permute-start(f32[1,16,256]{2,1,0:T(8,128)S(1)} %get-tuple-element.64), channel_id=1, source_target_pairs={{0,32},{32,64},{64,96},{96,128},{128,160},{160,192},{192,224},{224... | collective-permute-start | bytes 49160 | tf_op jit(solution)/shard_map/ppermute | solution.py:29
  362.6 7.0 %collective-permute-start.62 = (f32[18,1,256]{2,1,0:T(1,128)S(1)}, f32[18,1,256]{2,1,0:T(1,128)S(1)}, u32[]{:S(2)}, u32[]{:S(2)}) collective-permute-start(f32[18,1,256]{2,1,0:T(1,128)S(1)} %get-tuple-element.53), channel_id=1, source_target_pairs={{1,0},{2,1},{3,2},{4,3},{5,4},{6,5},{7,6},{8,7},{9,8},{10,9},{11,1... | collective-permute-start | bytes 55304 | tf_op jit(solution)/shard_map/ppermute | solution.py:30
  364.5 5.9 %collective-permute-start.63 = (f32[18,1,256]{2,1,0:T(1,128)S(1)}, f32[18,1,256]{2,1,0:T(1,128)S(1)}, u32[]{:S(2)}, u32[]{:S(2)}) collective-permute-start(f32[18,1,256]{2,1,0:T(1,128)S(1)} %get-tuple-element.52), channel_id=1, source_target_pairs={{0,1},{1,2},{2,3},{3,4},{4,5},{5,6},{6,7},{7,8},{8,9},{9,10},{10,1... | collective-permute-start | bytes 55304 | tf_op jit(solution)/shard_map/ppermute | solution.py:29
  371.5 7.9 %collective-permute-start.64 = (f32[1,16,256]{2,1,0:T(8,128)S(1)}, f32[1,16,256]{2,1,0:T(8,128)S(1)}, u32[]{:S(2)}, u32[]{:S(2)}) collective-permute-start(f32[1,16,256]{2,1,0:T(8,128)S(1)} %get-tuple-element.63), channel_id=1, source_target_pairs={{32,0},{64,32},{96,64},{128,96},{160,128},{192,160},{224,192},{256... | collective-permute-start | bytes 49160 | tf_op jit(solution)/shard_map/ppermute | solution.py:30
  372.8 7.5 %collective-permute-start.65 = (f32[1,16,256]{2,1,0:T(8,128)S(1)}, f32[1,16,256]{2,1,0:T(8,128)S(1)}, u32[]{:S(2)}, u32[]{:S(2)}) collective-permute-start(f32[1,16,256]{2,1,0:T(8,128)S(1)} %get-tuple-element.62), channel_id=1, source_target_pairs={{0,32},{32,64},{64,96},{96,128},{128,160},{160,192},{192,224},{224... | collective-permute-start | bytes 49160 | tf_op jit(solution)/shard_map/ppermute | solution.py:29
  380.3 7.0 %collective-permute-start.66 = (f32[18,1,256]{2,1,0:T(1,128)S(1)}, f32[18,1,256]{2,1,0:T(1,128)S(1)}, u32[]{:S(2)}, u32[]{:S(2)}) collective-permute-start(f32[18,1,256]{2,1,0:T(1,128)S(1)} %get-tuple-element.51), channel_id=1, source_target_pairs={{1,0},{2,1},{3,2},{4,3},{5,4},{6,5},{7,6},{8,7},{9,8},{10,9},{11,1... | collective-permute-start | bytes 55304 | tf_op jit(solution)/shard_map/ppermute | solution.py:30
  382.2 5.9 %collective-permute-start.67 = (f32[18,1,256]{2,1,0:T(1,128)S(1)}, f32[18,1,256]{2,1,0:T(1,128)S(1)}, u32[]{:S(2)}, u32[]{:S(2)}) collective-permute-start(f32[18,1,256]{2,1,0:T(1,128)S(1)} %get-tuple-element.50), channel_id=1, source_target_pairs={{0,1},{1,2},{2,3},{3,4},{4,5},{5,6},{6,7},{7,8},{8,9},{9,10},{10,1... | collective-permute-start | bytes 55304 | tf_op jit(solution)/shard_map/ppermute | solution.py:29
  389.2 8.0 %collective-permute-start.68 = (f32[1,16,256]{2,1,0:T(8,128)S(1)}, f32[1,16,256]{2,1,0:T(8,128)S(1)}, u32[]{:S(2)}, u32[]{:S(2)}) collective-permute-start(f32[1,16,256]{2,1,0:T(8,128)S(1)} %get-tuple-element.61), channel_id=1, source_target_pairs={{32,0},{64,32},{96,64},{128,96},{160,128},{192,160},{224,192},{256... | collective-permute-start | bytes 49160 | tf_op jit(solution)/shard_map/ppermute | solution.py:30
  390.5 7.5 %collective-permute-start.69 = (f32[1,16,256]{2,1,0:T(8,128)S(1)}, f32[1,16,256]{2,1,0:T(8,128)S(1)}, u32[]{:S(2)}, u32[]{:S(2)}) collective-permute-start(f32[1,16,256]{2,1,0:T(8,128)S(1)} %get-tuple-element.60), channel_id=1, source_target_pairs={{0,32},{32,64},{64,96},{96,128},{128,160},{160,192},{192,224},{224... | collective-permute-start | bytes 49160 | tf_op jit(solution)/shard_map/ppermute | solution.py:29
  398.0 7.0 %collective-permute-start.70 = (f32[18,1,256]{2,1,0:T(1,128)S(1)}, f32[18,1,256]{2,1,0:T(1,128)S(1)}, u32[]{:S(2)}, u32[]{:S(2)}) collective-permute-start(f32[18,1,256]{2,1,0:T(1,128)S(1)} %get-tuple-element.49), channel_id=1, source_target_pairs={{1,0},{2,1},{3,2},{4,3},{5,4},{6,5},{7,6},{8,7},{9,8},{10,9},{11,1... | collective-permute-start | bytes 55304 | tf_op jit(solution)/shard_map/ppermute | solution.py:30
  400.0 5.9 %collective-permute-start.71 = (f32[18,1,256]{2,1,0:T(1,128)S(1)}, f32[18,1,256]{2,1,0:T(1,128)S(1)}, u32[]{:S(2)}, u32[]{:S(2)}) collective-permute-start(f32[18,1,256]{2,1,0:T(1,128)S(1)} %get-tuple-element.48), channel_id=1, source_target_pairs={{0,1},{1,2},{2,3},{3,4},{4,5},{5,6},{6,7},{7,8},{8,9},{9,10},{10,1... | collective-permute-start | bytes 55304 | tf_op jit(solution)/shard_map/ppermute | solution.py:29
  (22 other events, 499.4 us)
where the time goes:
time: 546 us; the launch traced here: 544 us
  starting transfers between devices  235 us (43%)
  blocking collectives  134 us (25%)
  local copies, waits for them, and re-layouts  96.1 us (18%)
  other arithmetic  48 us (9%)
  waiting for transfers between devices  25.7 us (5%)
    ppermute x36, starting transfers between devices, padded_2(): before = lax.ppermute(last, axis, up)  174 us
    psum x1, blocking collectives, body(): total = lax.psum(jnp.sum(final_defect * final_defect), ('gx', 'gy'))  134 us
    reshape x6, local copies, waits for them, and re-layouts, restrict_cells(): values.reshape(sx // 2, 2, sy // 2, 2, sz // 2, 2).mean(axis=(1, 3, 5))  79.2 us
    ppermute x36, starting transfers between devices, padded_2(): after = lax.ppermute(leading, axis, down)  61.2 us
    reduce_sum x8, other arithmetic, restrict_cells(): values.reshape(sx // 2, 2, sy // 2, 2, sz // 2, 2).mean(axis=(1, 3, 5))  35.2 us
    ppermute x36, waiting for transfers between devices, padded_2(): before = lax.ppermute(last, axis, up)  13 us
    ppermute x36, waiting for transfers between devices, padded_2(): after = lax.ppermute(leading, axis, down)  12.7 us
  transfers between devices with their start and end apart: 72, of which 21 were waited for; matrix products, arithmetic and copies ran while one was open for 19% of the time, Pallas kernels for 0%

commit v1 on v0

v1 whole, which is shorter than its diff:
```python
import functools

import jax
import jax.numpy as jnp
from jax import lax
from jax.experimental import pallas as pl
from jax.experimental.pallas import tpu as pltpu
from jax.sharding import PartitionSpec as P

OMEGA = 0.8
LN2 = 0.6931471805599453
F32 = jnp.float32
HIGHEST = lax.Precision.HIGHEST
LANES = 128
VMEM_LIMIT = 24 * 1024 * 1024

RIM_X0, RIM_Y0 = 3, 4
RIM_1 = 8
RIM_2 = 6


def roll(value, shift, axis):
    return pltpu.roll(value, shift % value.shape[axis], axis)


def iota(shape, dim):
    return lax.broadcasted_iota(jnp.int32, shape, dim)


def shared_matrix(rows, cols, ratio_rows, ratio_cols, value):
    match = iota((rows, cols), 0) // ratio_rows == iota((rows, cols), 1) // ratio_cols
    return jnp.where(match, value, 0.0).astype(F32)


def dot(left, right):
    return jnp.dot(left, right, precision=HIGHEST, preferred_element_type=F32)


def low_half(shape):
    return iota(shape, 0) < 4


def shifted_tiles(first, second, left, right):
    low = low_half(first.shape)
    a, b = roll(first, 4, 0), roll(second, 4, 0)
    return jnp.where(low, left, a), jnp.where(low, a, b), jnp.where(low, b, right)


def row_mask(shape, first_row, last_row, origin, size, lanes=None):
    row = iota(shape, 0)
    place = row + origin
    good = (row >= first_row) & (row < last_row) & (place >= 0) & (place < size)
    if lanes is not None:
        good = good & (iota(shape, 1) < lanes)
    return jnp.where(good, 1.0, 0.0).astype(F32)


def plane_bar(place, size):
    return jnp.where((place >= 0) & (place < size), 0.5, 2.0).astype(F32)


def over_planes(first, last, step, unroll=1):
    def loop_body(x, carry):
        step(x)
        return carry

    lax.fori_loop(first, last, loop_body, 0, unroll=unroll)


def fill_weights(e_ref, weights, planes, scale, wrap_free):
    wx, wy, wz, wb, total = weights
    half = 0.5 * scale
    shape = e_ref.shape[1:]
    lane = iota(shape, 1)
    last = shape[1] - 1

    def along_x(x):
        wx[x] = half * (e_ref[x] + e_ref[x + 1])

    over_planes(0, planes - 1, along_x)

    def others(x):
        e = e_ref[x]
        y = half * (e + roll(e, -1, 0))
        z = half * (e + roll(e, -1, 1))
        if not wrap_free:
            z = jnp.where(lane < last, z, 0.0)
        faces = (wx[x] + wx[x - 1]) + (y + roll(y, 1, 0)) + (z + roll(z, 1, 1))
        if not wrap_free:
            b = jnp.where((lane == 0) | (lane == last), half * e, 0.0)
            wb[x] = b
            faces = faces + b
        wy[x] = y
        wz[x] = z
        total[x] = faces

    over_planes(1, planes - 1, others)


def flux_of(x, u_ref, weights):
    wx, wy, wz, wb, _ = weights
    u = u_ref[x]
    py = wy[x] * (roll(u, -1, 0) - u)
    pz = wz[x] * (roll(u, -1, 1) - u)
    flux = wx[x - 1] * (u - u_ref[x - 1]) - wx[x] * (u_ref[x + 1] - u)
    flux = flux + (roll(py, 1, 0) - py) + (roll(pz, 1, 1) - pz)
    if wb is not None:
        flux = flux + wb[x] * u
    return u, flux


def halves(u):
    return jnp.exp(u - LN2), jnp.exp(-u - LN2)


def sweep(u_ref, out_ref, weights, k_ref, f_ref, first, last, rows, origin, size):
    def step(x):
        u, flux = flux_of(x, u_ref, weights)
        up, down = halves(u)
        k = k_ref[x]
        defect = f_ref[x] - (flux + k * (up - down))
        slope = weights[4][x] + k * (up + down)
        moved = u + OMEGA * defect / slope
        out_ref[x] = jnp.where(rows > plane_bar(origin + x, size), moved, 0.0)

    over_planes(first, last, step)


def defect_at(x, u_ref, weights, k_ref, load):
    u, flux = flux_of(x, u_ref, weights)
    up, down = halves(u)
    return load - (flux + k_ref[x] * (up - down))


def pair_rows(ref, base, count=8):
    return ref[pl.ds(base, count, 2), :] + ref[pl.ds(base + 1, count, 2), :]


def rim_plane(x, brick, left, right, base, depth, rim):
    size = brick.shape[0]
    if x < rim:
        at = x - (rim - depth)
        return (left, base + at) if at >= 0 else None
    if x < rim + size:
        return (brick, x - rim)
    at = x - rim - size
    return (right, base + at) if at < depth else None


FINE_SENT = ((3, 0), (3, 3), (2, 6), (2, 8))


def fine_plane(x, index, brick, left, right):
    depth, base = FINE_SENT[index]
    return rim_plane(x, brick, left, right, base, depth, RIM_X0)


def tile_of(place, tile):
    if place is None:
        return None
    ref, x = place
    return ref[x, 8 * tile : 8 * tile + 8, :]


def pack_fine(s_ref, e_ref, k_ref, f_ref, xl_ref, xr_ref, up_ref, down_ref):
    bricks = (s_ref, e_ref, k_ref, f_ref)
    planes = s_ref.shape[0] + 2 * RIM_X0
    shape = (8, s_ref.shape[2])
    low = low_half(shape)
    zero = jnp.zeros(shape, F32)
    for x in range(planes):
        for pair in range(2):
            places = [fine_plane(x, 2 * pair + i, bricks[2 * pair + i], xl_ref, xr_ref) for i in range(2)]
            if places[0] is None:
                up_ref[pair, x] = zero
                down_ref[pair, x] = zero
                continue
            up_ref[pair, x] = jnp.where(low, roll(tile_of(places[0], 1), 4, 0), tile_of(places[1], 1))
            down_ref[pair, x] = jnp.where(low, tile_of(places[0], 0), roll(tile_of(places[1], 0), 4, 0))


def fine_first(
    s_ref, e_ref, k_ref, f_ref, xl_ref, xr_ref, yl_ref, yr_ref,
    stack_ref, u0_ref, ew_ref, kw_ref, fw_ref,
    ua, ub, wx, wy, wz, wb, total, gather, summed,
    *, size_x, size_y,
):
    bricks = (s_ref, e_ref, k_ref, f_ref)
    windows = (ua, ew_ref, kw_ref, fw_ref)
    own_x, own_y, nz = s_ref.shape
    planes = own_x + 2 * RIM_X0
    rows = own_y + 2 * RIM_Y0
    for x in range(planes):
        for index in range(4):
            place = fine_plane(x, index, bricks[index], xl_ref, xr_ref)
            if place is None:
                windows[index][x] = jnp.zeros((rows, nz), F32)
                continue
            left, right = yl_ref[index // 2, x], yr_ref[index // 2, x]
            if index % 2 == 0:
                right = roll(right, 4, 0)
            else:
                left = roll(left, 4, 0)
            tiles = shifted_tiles(tile_of(place, 0), tile_of(place, 1), left, right)
            for i, tile in enumerate(tiles):
                windows[index][x, 8 * i : 8 * i + 8, :] = tile
    weights = (wx, wy, wz, wb, total)
    fill_weights(ew_ref, weights, planes, 1.0, False)
    origin_x = lax.axis_index("gx") * own_x - RIM_X0
    origin_y = lax.axis_index("gy") * own_y - RIM_Y0
    shape = (rows, nz)
    mask = row_mask(shape, 2, rows - 2, origin_y, size_y)
    sweep(ua, ub, weights, kw_ref, fw_ref, 1, planes - 1, mask, origin_x, size_x)
    mask = row_mask(shape, 3, rows - 3, origin_y, size_y)
    sweep(ub, ua, weights, kw_ref, fw_ref, 2, planes - 2, mask, origin_x, size_x)

    low = low_half((8, nz))
    pairs = own_x // 2

    def finish(j):
        x = RIM_X0 + 2 * j
        gather[pl.ds(j * rows, rows), :] = ua[x] + ua[x + 1]
        d = defect_at(x, ua, weights, kw_ref, fw_ref[x]) + defect_at(x + 1, ua, weights, kw_ref, fw_ref[x + 1])
        gather[pl.ds((pairs + j) * rows, rows), :] = d
        for i in range(2):
            u = ua[x + i]
            moved = [roll(u[8 * t : 8 * t + 8], 4, 0) for t in range(3)]
            u0_ref[2 * j + i, 0:8, :] = jnp.where(low, moved[0], moved[1])
            u0_ref[2 * j + i, 8:16, :] = jnp.where(low, moved[1], moved[2])

    over_planes(0, pairs, finish)
    base = 2 * pairs * rows
    for i, ref in enumerate((e_ref, k_ref)):
        for j in range(pairs):
            at = base + (i * pairs + j) * own_y
            gather[at : at + own_y, :] = ref[2 * j] + ref[2 * j + 1]
    summed[...] = dot(gather[...], shared_matrix(nz, nz // 2, 2, 1, 0.125))
    for j in range(pairs):
        stack_ref[0, j] = pair_rows(summed, base + j * own_y)
        stack_ref[1, j] = pair_rows(summed, base + (pairs + j) * own_y)
        stack_ref[2, j] = pair_rows(summed, j * rows + RIM_Y0)
        stack_ref[3, j] = pair_rows(summed, (pairs + j) * rows + RIM_Y0)


def middle_first(
    l_ref, o_ref, r_ref, u0_ref,
    up_ref, down_ref, stack_ref, w_ref, f_ref,
    e, k, v, wa, wx, wy, wz, wb, total, gather, summed,
    *, size_x, size_y,
):
    planes, own, nz = o_ref.shape[1:]
    rows = own + 2 * RIM_1
    shape = (rows, nz)

    def joined(index, x):
        return jnp.concatenate([l_ref[index, x], o_ref[index, x], r_ref[index, x]], axis=0)

    def assemble(x):
        e[x] = joined(0, x)
        k[x] = joined(1, x)
        v[x] = joined(2, x)

    over_planes(0, planes, assemble)
    weights = (wx, wy, wz, wb, total)
    fill_weights(e, weights, planes, 0.25, False)
    origin_x = lax.axis_index("gx") * own - RIM_1
    origin_y = lax.axis_index("gy") * own - RIM_1

    def load(x):
        f_ref[x] = defect_at(x, v, weights, k, joined(3, x))

    over_planes(2, planes - 2, load)
    mask = row_mask(shape, 2, rows - 2, origin_y, size_y)
    sweep(v, wa, weights, k, f_ref, 2, planes - 2, mask, origin_x, size_x)
    mask = row_mask(shape, 3, rows - 3, origin_y, size_y)
    sweep(wa, w_ref, weights, k, f_ref, 3, planes - 3, mask, origin_x, size_x)
    pairs = (planes - 8) // 2

    def finish(j):
        x = 4 + 2 * j
        d = defect_at(x, w_ref, weights, k, f_ref[x]) + defect_at(x + 1, w_ref, weights, k, f_ref[x + 1])
        at = pl.ds(j * rows, rows)
        gather[at, :nz] = e[x] + e[x + 1]
        gather[at, nz:] = k[x] + k[x + 1]
        at = pl.ds((pairs + j) * rows, rows)
        gather[at, :nz] = w_ref[x] + w_ref[x + 1]
        gather[at, nz:] = d

    over_planes(0, pairs, finish)
    summed[...] = dot(gather[...], shared_matrix(2 * nz, nz, 2, 1, 0.125))
    own_planes = u0_ref.shape[0]
    for a in range(2):
        for j in range(pairs):
            tile = pair_rows(summed, (a * pairs + j) * rows + 4)
            stack_ref[a, j] = tile
            if j < RIM_2:
                up_ref[a * RIM_2 + j] = tile
            if j >= pairs - RIM_2:
                down_ref[a * RIM_2 + j - (pairs - RIM_2)] = tile
    for x in range(RIM_X0):
        for t in range(4):
            rows_at, lanes_at = 8 * (t // 2), LANES * (t % 2)
            at = 2 * RIM_2 + 4 * x + t
            up_ref[at] = u0_ref[own_planes - RIM_X0 + x, rows_at : rows_at + 8, lanes_at : lanes_at + LANES]
            down_ref[at] = u0_ref[x, rows_at : rows_at + 8, lanes_at : lanes_at + LANES]


def pack_coarse(xl_ref, xr_ref, stack_ref, u0_ref, up_ref, down_ref, own_ref, rim_ref):
    spare = stack_ref.shape[1] // 2 - 2
    planes = 2 * RIM_2 + 4
    low = low_half((8, LANES))
    for a in range(2):
        for x in range(planes):
            if x < RIM_2:
                tile = xl_ref[a * RIM_2 + x]
            elif x < RIM_2 + 4:
                tile = stack_ref[a, x - RIM_2 + spare]
            else:
                tile = xr_ref[a * RIM_2 + x - RIM_2 - 4]
            at = a * planes + x
            own_ref[at] = tile
            up_ref[at] = tile
            down_ref[at] = tile
    own_planes = u0_ref.shape[0]
    base = 2 * RIM_2
    for x in range(own_planes + 2 * RIM_X0):
        if x < RIM_X0:
            tiles = [xl_ref[base + 4 * x + t] for t in range(4)]
        elif x < RIM_X0 + own_planes:
            tiles = [
                u0_ref[x - RIM_X0, 8 * (t // 2) : 8 * (t // 2) + 8, LANES * (t % 2) : LANES * (t % 2) + LANES]
                for t in range(4)
            ]
        else:
            tiles = [xr_ref[base + 4 * (x - RIM_X0 - own_planes) + t] for t in range(4)]
        at = 2 * planes + x
        up_ref[at] = jnp.where(low, roll(tiles[2], 4, 0), tiles[3])
        down_ref[at] = jnp.where(low, tiles[0], roll(tiles[1], 4, 0))
        for t in range(4):
            rim_ref[x, 8 * (t // 2) : 8 * (t // 2) + 8, LANES * (t % 2) : LANES * (t % 2) + LANES] = tiles[t]


def coarse_and_last(
    l1_ref, o1_ref, r1_ref, w1_ref, f1_ref, yl_ref, yr_ref, o2_ref, u0_ref, ew_ref, kw_ref, fw_ref,
    out_ref, part_ref,
    e2, k2, v2, f2, a2, b2, wx2, wy2, wz2, t2, q2, s2, d2,
    e1, k1, a1, b1, wx1, wy1, wz1, wb1, t1, d1,
    a0, b0, wx0, wy0, wz0, wb0, t0, q0,
    *, size_x, size_y,
):
    place_x, place_y = lax.axis_index("gx"), lax.axis_index("gy")
    planes2 = 2 * RIM_2 + 4
    rows2 = planes2
    shape2 = (rows2, LANES)
    nz2 = LANES // 2
    row8 = iota((8, LANES), 0)
    inside = iota(shape2, 1) < nz2

    def window2(at):
        own = roll(o2_ref[at], 4, 0)
        upper = jnp.where(row8 >= 6, own, yl_ref[at])
        lower = jnp.where(row8 < 2, own, yr_ref[at])
        return jnp.concatenate([upper, lower], axis=0)

    def assemble2(x):
        both = window2(x)
        e2[x] = jnp.where(inside, both, 0.0)
        k2[x] = jnp.where(inside, roll(both, nz2, 1), 0.0)
        both = window2(planes2 + x)
        v2[x] = jnp.where(inside, both, 0.0)
        f2[x] = jnp.where(inside, roll(both, nz2, 1), 0.0)

    over_planes(0, planes2, assemble2)
    weights2 = (wx2, wy2, wz2, None, t2)
    fill_weights(e2, weights2, planes2, 0.0625, True)
    origin_x = place_x * 4 - RIM_2
    origin_y = place_y * 4 - RIM_2

    def load2(x):
        f2[x] = defect_at(x, v2, weights2, k2, f2[x])

    over_planes(1, planes2 - 1, load2)
    source = v2
    for i in range(4):
        target = a2 if i % 2 == 0 else b2
        mask = row_mask(shape2, 1 + i, rows2 - 1 - i, origin_y, size_y // 4, nz2)
        sweep(source, target, weights2, k2, f2, 1 + i, planes2 - 1 - i, mask, origin_x, size_x // 4)
        source = target
    for j in range(8):
        q2[16 * j : 16 * j + 16, :] = source[4 + j] - v2[4 + j]
    s2[...] = dot(q2[...], shared_matrix(LANES, LANES, 1, 2, 1.0))
    rows1 = o1_ref.shape[2] + 2 * RIM_1
    d2[...] = jnp.zeros(d2.shape, F32)
    for j in range(8):
        rows = roll(s2[16 * j : 16 * j + 16, :], -4, 0)[:8]
        d2[pl.ds(rows1 * j + 4, 8, 2), :] = rows
        d2[pl.ds(rows1 * j + 5, 8, 2), :] = rows

    planes1, own1, nz1 = o1_ref.shape[1:]
    shape1 = (rows1, nz1)

    def joined(index, x):
        return jnp.concatenate([l1_ref[index, x], o1_ref[index, x], r1_ref[index, x]], axis=0)

    def assemble1(x):
        e1[x] = joined(0, x)
        k1[x] = joined(1, x)

    over_planes(0, planes1, assemble1)
    weights1 = (wx1, wy1, wz1, wb1, t1)
    fill_weights(e1, weights1, planes1, 0.25, False)
    origin_x = place_x * own1 - RIM_1
    origin_y = place_y * own1 - RIM_1
    for x in range(4, 20):
        at = rows1 * ((x - 4) // 2)
        a1[x] = w1_ref[x] + d2[at : at + rows1, :]
    mask = row_mask(shape1, 5, rows1 - 5, origin_y, size_y // 2)
    sweep(a1, b1, weights1, k1, f1_ref, 5, planes1 - 5, mask, origin_x, size_x // 2)
    mask = row_mask(shape1, 6, rows1 - 6, origin_y, size_y // 2)
    sweep(b1, a1, weights1, k1, f1_ref, 6, planes1 - 6, mask, origin_x, size_x // 2)
    for j in range(12):
        rows = roll(a1[6 + j] - joined(2, 6 + j), -6, 0)[:16]
        d1[pl.ds(32 * j, 16, 2), :] = rows
        d1[pl.ds(32 * j + 1, 16, 2), :] = rows
    nz0 = 2 * nz1
    q0[...] = dot(d1[...], shared_matrix(nz1, nz0, 1, 2, 1.0))

    own_x, own_y = out_ref.shape[:2]
    planes0 = own_x + 2 * RIM_X0
    rows0 = own_y + 2 * RIM_Y0
    shape0 = (rows0, nz0)
    base = 2 * planes2
    for x in range(planes0):
        left, right = yl_ref[base + x], yr_ref[base + x]
        left = jnp.concatenate([left, roll(left, 4, 0)], axis=1)
        right = jnp.concatenate([roll(right, 4, 0), right], axis=1)
        tiles = shifted_tiles(u0_ref[x, 0:8, :], u0_ref[x, 8:16, :], left, right)
        at = 32 * ((x + 1) // 2)
        for i, tile in enumerate(tiles):
            a0[x, 8 * i : 8 * i + 8, :] = tile + q0[at + 8 * i : at + 8 * i + 8, :]
    weights0 = (wx0, wy0, wz0, wb0, t0)
    fill_weights(ew_ref, weights0, planes0, 1.0, False)
    origin_x = place_x * own_x - RIM_X0
    origin_y = place_y * own_y - RIM_Y0
    mask = row_mask(shape0, 2, rows0 - 2, origin_y, size_y)
    sweep(a0, b0, weights0, kw_ref, fw_ref, 1, planes0 - 1, mask, origin_x, size_x)
    mask = row_mask(shape0, 3, rows0 - 3, origin_y, size_y)
    sweep(b0, a0, weights0, kw_ref, fw_ref, 2, planes0 - 2, mask, origin_x, size_x)
    low = low_half((8, nz0))

    def finish(x, acc):
        d = defect_at(x, a0, weights0, kw_ref, fw_ref[x])
        u = a0[x]
        moved = [roll(u[8 * t : 8 * t + 8], 4, 0) for t in range(3)]
        out_ref[x - RIM_X0, 0:8, :] = jnp.where(low, moved[0], moved[1])
        out_ref[x - RIM_X0, 8:16, :] = jnp.where(low, moved[1], moved[2])
        return acc + d * d

    acc = lax.fori_loop(RIM_X0, RIM_X0 + own_x, finish, jnp.zeros(shape0, F32))
    row = iota(shape0, 0)
    acc = jnp.where((row >= RIM_Y0) & (row < RIM_Y0 + own_y), acc, 0.0)
    acc = jnp.sum(acc, axis=0, keepdims=True)
    acc = acc[:, :LANES] + acc[:, LANES:]
    part_ref[...] = jnp.broadcast_to(acc, part_ref.shape)


def arr(*shape):
    return jax.ShapeDtypeStruct(shape, F32)


def call(kernel, outs, scratch, *args):
    return pl.pallas_call(
        kernel,
        out_shape=outs,
        in_specs=[pl.BlockSpec(memory_space=pltpu.VMEM)] * len(args),
        out_specs=[pl.BlockSpec(memory_space=pltpu.VMEM)] * len(outs),
        scratch_shapes=[pltpu.VMEM(shape, F32) for shape in scratch],
        compiler_params=pltpu.CompilerParams(vmem_limit_bytes=VMEM_LIMIT),
    )(*args)


def swap(upward, downward, axis):
    size = lax.axis_size(axis)
    up = [(i, i + 1) for i in range(size - 1)]
    down = [(j, i) for i, j in up]
    return lax.ppermute(upward, axis, up), lax.ppermute(downward, axis, down)


def sum_over(part, axis):
    size = lax.axis_size(axis)
    rows = jnp.broadcast_to(part, (size, LANES))
    return jnp.sum(lax.all_to_all(rows, axis, 0, 0, tiled=True), axis=0, keepdims=True)


def body(start, permit, ion, source):
    own_x, own_y, nz = start.shape
    size_x, size_y = own_x * lax.axis_size("gx"), own_y * lax.axis_size("gy")
    planes0, rows0 = own_x + 2 * RIM_X0, own_y + 2 * RIM_Y0
    window0 = (planes0, rows0, nz)

    fields = (start, permit, ion, source)
    depths = [depth for depth, _ in FINE_SENT]
    upward = jnp.concatenate([a[own_x - d :] for a, d in zip(fields, depths)], axis=0)
    downward = jnp.concatenate([a[:d] for a, d in zip(fields, depths)], axis=0)
    xl, xr = swap(upward, downward, "gx")
    packed = arr(2, planes0, 8, nz)
    upward, downward = call(pack_fine, [packed, packed], [], *fields, xl, xr)
    yl, yr = swap(upward, downward, "gy")
    own1, own1_y, nz1 = own_x // 2, own_y // 2, nz // 2
    gathered = 2 * own1 * rows0 + 2 * own1 * own_y
    stack1, u0, permit0, ion0, source0 = call(
        functools.partial(fine_first, size_x=size_x, size_y=size_y),
        [arr(4, own1, own1_y, nz1), arr(own_x, own_y, nz)] + [arr(*window0)] * 3,
        [window0] * 7 + [(gathered, nz), (gathered, nz1)],
        *fields, xl, xr, yl, yr,
    )

    xl, xr = swap(stack1, stack1, "gx")
    own = jnp.concatenate([xl, stack1, xr], axis=1)
    yl1, yr1 = swap(own, own, "gy")
    planes1 = own1 + 2 * RIM_1
    window1 = (planes1, own1_y + 2 * RIM_1, nz1)
    sent_x = 2 * RIM_2 + 4 * RIM_X0
    upward, downward, stack2, w1, f1 = call(
        functools.partial(middle_first, size_x=size_x // 2, size_y=size_y // 2),
        [arr(sent_x, 8, LANES)] * 2 + [arr(2, 8, 8, LANES)] + [arr(*window1)] * 2,
        [window1] * 9 + [(16 * window1[1], 2 * nz1), (16 * window1[1], nz1)],
        yl1, own, yr1, u0,
    )

    xl, xr = swap(upward, downward, "gx")
    planes2 = 2 * RIM_2 + 4
    sent_y = 2 * planes2 + planes0
    upward, downward, own2, rim0 = call(
        pack_coarse,
        [arr(sent_y, 8, LANES)] * 2 + [arr(2 * planes2, 8, LANES), arr(planes0, own_y, nz)],
        [], xl, xr, stack2, u0,
    )
    yl, yr = swap(upward, downward, "gy")
    window2 = (planes2, planes2, LANES)
    relaxed, part = call(
        functools.partial(coarse_and_last, size_x=size_x, size_y=size_y),
        [arr(own_x, own_y, nz), arr(8, LANES)],
        [window2] * 10 + [(LANES, LANES)] * 2 + [(8 * window1[1], LANES)]
        + [window1] * 9 + [(12 * 32, nz1)] + [window0] * 7 + [(12 * 32, nz)],
        yl1, own, yr1, w1, f1, yl, yr, own2, rim0, permit0, ion0, source0,
    )
    total = jnp.sum(sum_over(sum_over(part[:1], "gx"), "gy"))
    return relaxed, jnp.sqrt(total / (size_x * size_y * nz))


def solution(mesh):
    specs = (P("gx", "gy", None),) * 4
    return jax.shard_map(
        body, mesh=mesh, in_specs=specs, out_specs=(P("gx", "gy", None), P()), check_vma=False
    )
```

time: 546 us -> 176 us (0.32)
  starting transfers between devices: 235 us -> 37.5 us
  local copies, waits for them, and re-layouts: 96.1 us -> 1.95 us
  blocking collectives: 134 us -> 45.7 us
  Pallas kernels: 0 us -> 57.9 us
  other arithmetic: 48 us -> 0.65 us
    ppermute x72 -> x12, starting transfers between devices: 235 us -> 37.5 us  [swap(): return (lax.ppermute(upward, axis, up), lax.ppermute(downward, axis, down))]
    psum x1 -> x0, blocking collectives: 134 us -> none  [body(): total = lax.psum(jnp.sum(final_defect * final_defect), ('gx', 'gy'))]
    reshape x10 -> x0, local copies, waits for them, and re-layouts: 83.4 us -> none  [the longest x6 79.2 us: restrict_cells(): values.reshape(sx // 2, 2, sy // 2, 2, sz // 2, 2).mean(axis=(1, 3, 5))]
    pallas_call x0 -> x5, Pallas kernels: none -> 57.9 us  [call(): pl.pallas_call(kernel, out_shape=outs, in_specs=[pl.BlockSpec(memory_spac...]
    all_to_all x0 -> x2, blocking collectives: none -> 45.7 us  [sum_over(): lax.all_to_all(rows, axis, 0, 0, tiled=True)]
    reduce_sum x9 -> x2, other arithmetic: 36.3 us -> 0.62 us  [the longest x1 0.6 us: body(): total = jnp.sum(sum_over(sum_over(part[:1], 'gx'), 'gy'))]
    div x2 -> x0, local copies, waits for them, and re-layouts: 6.83 us -> none  [restrict_cells(): values.reshape(sx // 2, 2, sy // 2, 2, sz // 2, 2).mean(axis=(1, 3, 5))]
    ppermute x72 -> x12, waiting for transfers between devices: 25.7 us -> 29.3 us  [swap(): return (lax.ppermute(upward, axis, up), lax.ppermute(downward, axis, down))]
  transfers between devices with their start and end apart: 72 -> 12, of which waited for: 21 -> 12; matrix products, arithmetic and copies ran while one was open for 19% -> 0% of each run, Pallas kernels for 0% -> 0%
where the time goes in v1:
time: 176 us
  Pallas kernels  57.9 us (33%)
  blocking collectives  45.7 us (26%)
  starting transfers between devices  37.5 us (21%)
  waiting for transfers between devices  29.3 us (17%)
  between operations  2.63 us (1%)
  local copies, waits for them, and re-layouts  1.95 us (1%)
    pallas_call x5, Pallas kernels, call(): pl.pallas_call(kernel, out_shape=outs, in_specs=[pl.BlockSpec(memory_spac...  57.9 us
    all_to_all x2, blocking collectives, sum_over(): lax.all_to_all(rows, axis, 0, 0, tiled=True)  45.7 us
    ppermute x12, starting transfers between devices, swap(): return (lax.ppermute(upward, axis, up), lax.ppermute(downward, axis, down))  37.5 us
    ppermute x12, waiting for transfers between devices, swap(): return (lax.ppermute(upward, axis, up), lax.ppermute(downward, axis, down))  29.3 us
  transfers between devices with their start and end apart: 12, of which 12 were waited for; matrix products, arithmetic and copies ran while one was open for 0% of the time, Pallas kernels for 0%

profile of v1, /device:TPU:1, one launch (start us, length us, event | category | flops | bytes accessed | tf_op | source)
XLA Modules:
  0.0 175.6 jit_solution(12019248375380414243)
XLA Ops:
  0.6 0.0 copy-start
  0.6 0.9 fusion.2
  1.5 0.1 copy-done
  1.6 0.0 copy-start.3
  1.6 0.9 fusion
  2.5 0.0 copy-start.1
  2.5 0.0 copy-start.2
  2.6 4.2 %collective-permute-start = (f32[10,16,256]{2,1,0:T(8,128)S(1)}, f32[10,16,256]{2,1,0:T(8,128)S(1)}, u32[]{:S(2)}, u32[]{:S(2)}) collective-permute-start(f32[10,16,256]{2,1,0:T(8,128)S(1)} %pad_maximum_fusion), channel_id=1, source_target_pairs={{0,32},{32,64},{64,96},{96,128},{128,160},{160,192},{192,224},{224... | collective-permute-start | bytes 491528 | tf_op jit(solution)/shard_map/ppermute | solution.py:486
  6.8 1.3 collective-permute-start.1
  8.1 0.9 collective-permute-done.xl_ref
  9.0 3.8 %collective-permute-done.1.xr_ref = f32[10,16,256]{2,1,0:T(8,128)S(1)} collective-permute-done((f32[10,16,256]{2,1,0:T(8,128)S(1)}, f32[10,16,256]{2,1,0:T(8,128)S(1)}, u32[]{:S(2)}, u32[]{:S(2)}) %collective-permute-start.1) | collective-permute-done | bytes 163872 | tf_op jit(solution)/shard_map/ppermute | solution.py:486
  12.8 0.0 copy-done.3
  12.8 0.0 copy-done.1
  12.8 0.0 copy-done.2
  12.8 0.1 shard_map.59
  12.9 5.9 %collective-permute-start.2 = (f32[2,22,8,256]{3,2,1,0:T(8,128)S(1)}, f32[2,22,8,256]{3,2,1,0:T(8,128)S(1)}, u32[]{:S(2)}, u32[]{:S(2)}) collective-permute-start(f32[2,22,8,256]{3,2,1,0:T(8,128)S(1)} %get-tuple-element.20), channel_id=1, source_target_pairs={{0,1},{1,2},{2,3},{3,4},{4,5},{5,6},{6,7},{7,8},{8,9},{9,10},{10,1... | collective-permute-start | bytes 1081352 | tf_op jit(solution)/shard_map/ppermute | solution.py:486
  18.8 2.6 %collective-permute-start.3 = (f32[2,22,8,256]{3,2,1,0:T(8,128)S(1)}, f32[2,22,8,256]{3,2,1,0:T(8,128)S(1)}, u32[]{:S(2)}, u32[]{:S(2)}) collective-permute-start(f32[2,22,8,256]{3,2,1,0:T(8,128)S(1)} %get-tuple-element.21), channel_id=1, source_target_pairs={{1,0},{2,1},{3,2},{4,3},{5,4},{6,5},{7,6},{8,7},{9,8},{10,9},{11,1... | collective-permute-start | bytes 1081352 | tf_op jit(solution)/shard_map/ppermute | solution.py:486
  21.5 1.7 collective-permute-done.2.yl_ref
  23.2 4.4 %collective-permute-done.3.yr_ref = f32[2,22,8,256]{3,2,1,0:T(8,128)S(1)} collective-permute-done((f32[2,22,8,256]{3,2,1,0:T(8,128)S(1)}, f32[2,22,8,256]{3,2,1,0:T(8,128)S(1)}, u32[]{:S(2)}, u32[]{:S(2)}) %collective-permute-start.3) | collective-permute-done | bytes 360480 | tf_op jit(solution)/shard_map/ppermute | solution.py:486
  27.6 11.4 %shard_map.60 = (f32[4,8,8,128]{3,2,1,0:T(8,128)S(1)}, f32[16,16,256]{2,1,0:T(8,128)S(1)}, f32[22,24,256]{2,1,0:T(8,128)S(1)}, f32[22,24,256]{2,1,0:T(8,128)S(1)}, f32[22,24,256]{2,1,0:T(8,128)S(1)}) custom-call(f32[16,16,256]{2,1,0:T(8,128)S(1)} %copy-done, f32[16,16,256]{2,1,0:T(8,128)S(1)} %copy-done.1, f32[16,16,256]{2,1,0:T(8,128)S(1)} %copy-done.2, ...), custom_call_target="tpu_custom_call" | custom-call | tf_op jit(solution)/shard_map/pallas_call | solution.py:472
  39.0 3.2 %collective-permute-start.4 = (f32[4,8,8,128]{3,2,1,0:T(8,128)S(1)}, f32[4,8,8,128]{3,2,1,0:T(8,128)S(1)}, u32[]{:S(2)}, u32[]{:S(2)}) collective-permute-start(f32[4,8,8,128]{3,2,1,0:T(8,128)S(1)} %get-tuple-element.22), channel_id=1, source_target_pairs={{0,32},{32,64},{64,96},{96,128},{128,160},{160,192},{192,224},{224... | collective-permute-start | bytes 393224 | tf_op jit(solution)/shard_map/ppermute | solution.py:486
  42.2 1.3 collective-permute-start.5
  43.5 0.6 collective-permute-done.4
  44.2 3.8 %collective-permute-done.5 = f32[4,8,8,128]{3,2,1,0:T(8,128)S(1)} collective-permute-done((f32[4,8,8,128]{3,2,1,0:T(8,128)S(1)}, f32[4,8,8,128]{3,2,1,0:T(8,128)S(1)}, u32[]{:S(2)}, u32[]{:S(2)}) %collective-permute-start.5) | collective-permute-done | bytes 131104 | tf_op jit(solution)/shard_map/ppermute | solution.py:486
  47.9 1.9 %collective-permute-start.7 = (f32[4,24,8,128]{3,2,1,0:T(8,128)S(1)}, f32[4,24,8,128]{3,2,1,0:T(8,128)S(1)}, u32[]{:S(2)}, u32[]{:S(2)}) collective-permute-start(f32[4,24,8,128]{3,2,1,0:T(8,128)S(1)} %constant_dynamic-update-slice_fusion.o_ref.o1_ref), channel_id=1, source_target_pairs={{1,0},{2,1},{3,2},{4,3},{5,4},{6,5},{7,6},{8,7},{9,8},{10,9},{11,1... | collective-permute-start | bytes 1179656 | tf_op jit(solution)/shard_map/ppermute | solution.py:486
  49.9 3.6 %collective-permute-start.6 = (f32[4,24,8,128]{3,2,1,0:T(8,128)S(1)}, f32[4,24,8,128]{3,2,1,0:T(8,128)S(1)}, u32[]{:S(2)}, u32[]{:S(2)}) collective-permute-start(f32[4,24,8,128]{3,2,1,0:T(8,128)S(1)} %constant_dynamic-update-slice_fusion.o_ref.o1_ref), channel_id=1, source_target_pairs={{0,1},{1,2},{2,3},{3,4},{4,5},{5,6},{6,7},{7,8},{8,9},{9,10},{10,1... | collective-permute-start | bytes 1179656 | tf_op jit(solution)/shard_map/ppermute | solution.py:486
  53.5 3.5 %collective-permute-done.7.r_ref.r1_ref = f32[4,24,8,128]{3,2,1,0:T(8,128)S(1)} collective-permute-done((f32[4,24,8,128]{3,2,1,0:T(8,128)S(1)}, f32[4,24,8,128]{3,2,1,0:T(8,128)S(1)}, u32[]{:S(2)}, u32[]{:S(2)}) %collective-permute-start.7) | collective-permute-done | bytes 393248 | tf_op jit(solution)/shard_map/ppermute | solution.py:486
  57.0 1.2 collective-permute-done.6.l_ref.l1_ref
  58.2 13.8 %shard_map.61 = (f32[24,8,128]{2,1,0:T(8,128)S(1)}, f32[24,8,128]{2,1,0:T(8,128)S(1)}, f32[2,8,8,128]{3,2,1,0:T(8,128)S(1)}, f32[24,24,128]{2,1,0:T(8,128)S(1)}, f32[24,24,128]{2,1,0:T(8,128)S(1)}) custom-call(f32[4,24,8,128]{3,2,1,0:T(8,128)S(1)} %collective-permute-done.6.l_ref.l1_ref, ...), custom_call_target="tpu_custom_call" | custom-call | tf_op jit(solution)/shard_map/pallas_call | solution.py:472
  72.0 4.4 %collective-permute-start.8 = (f32[24,8,128]{2,1,0:T(8,128)S(1)}, f32[24,8,128]{2,1,0:T(8,128)S(1)}, u32[]{:S(2)}, u32[]{:S(2)}) collective-permute-start(f32[24,8,128]{2,1,0:T(8,128)S(1)} %get-tuple-element.26), channel_id=1, source_target_pairs={{0,32},{32,64},{64,96},{96,128},{128,160},{160,192},{192,224},{224... | collective-permute-start | bytes 294920 | tf_op jit(solution)/shard_map/ppermute | solution.py:486
  76.5 1.3 collective-permute-start.9
  77.8 0.3 collective-permute-done.8.xl_ref
  78.1 3.7 %collective-permute-done.9.xr_ref = f32[24,8,128]{2,1,0:T(8,128)S(1)} collective-permute-done((f32[24,8,128]{2,1,0:T(8,128)S(1)}, f32[24,8,128]{2,1,0:T(8,128)S(1)}, u32[]{:S(2)}, u32[]{:S(2)}) %collective-permute-start.9) | collective-permute-done | bytes 98336 | tf_op jit(solution)/shard_map/ppermute | solution.py:486
  81.8 0.1 shard_map.62
  81.9 5.8 %collective-permute-start.10 = (f32[54,8,128]{2,1,0:T(8,128)S(1)}, f32[54,8,128]{2,1,0:T(8,128)S(1)}, u32[]{:S(2)}, u32[]{:S(2)}) collective-permute-start(f32[54,8,128]{2,1,0:T(8,128)S(1)} %get-tuple-element.29), channel_id=1, source_target_pairs={{0,1},{1,2},{2,3},{3,4},{4,5},{5,6},{6,7},{7,8},{8,9},{9,10},{10,1... | collective-permute-start | bytes 663560 | tf_op jit(solution)/shard_map/ppermute | solution.py:486
  87.7 1.9 %collective-permute-start.11 = (f32[54,8,128]{2,1,0:T(8,128)S(1)}, f32[54,8,128]{2,1,0:T(8,128)S(1)}, u32[]{:S(2)}, u32[]{:S(2)}) collective-permute-start(f32[54,8,128]{2,1,0:T(8,128)S(1)} %get-tuple-element.30), channel_id=1, source_target_pairs={{1,0},{2,1},{3,2},{4,3},{5,4},{6,5},{7,6},{8,7},{9,8},{10,9},{11,1... | collective-permute-start | bytes 663560 | tf_op jit(solution)/shard_map/ppermute | solution.py:486
  89.7 0.9 collective-permute-done.10.yl_ref
  90.6 4.4 %collective-permute-done.11.yr_ref = f32[54,8,128]{2,1,0:T(8,128)S(1)} collective-permute-done((f32[54,8,128]{2,1,0:T(8,128)S(1)}, f32[54,8,128]{2,1,0:T(8,128)S(1)}, u32[]{:S(2)}, u32[]{:S(2)}) %collective-permute-start.11) | collective-permute-done | bytes 221216 | tf_op jit(solution)/shard_map/ppermute | solution.py:486
  95.0 32.5 %shard_map.63 = (f32[16,16,256]{2,1,0:T(8,128)}, f32[8,128]{1,0:T(8,128)S(1)}) custom-call(f32[4,24,8,128]{3,2,1,0:T(8,128)S(1)} %collective-permute-done.6.l_ref.l1_ref, f32[4,24,8,128]{3,2,1,0:T(8,128)S(1)} %constant_dynamic-update-slice_fusion.o_ref.o1_ref, f32[4,24,8,128]{3,2,1,0:T(8,128)S(1)} %collective-permute-done.7.r_ref.r1_ref, ...), custom_call_target="tpu_custom_call" | custom-call | tf_op jit(solution)/shard_map/pallas_call | solution.py:472
  127.5 14.3 %all_to_all.12 = f32[16,1,128]{2,1,0:T(1,128)S(1)} all-to-all(f32[16,1,128]{2,1,0:T(1,128)S(1)} %broadcast_in_dim.4), channel_id=1, replica_groups=mesh['gx'=16,'gy'=32] {'gx'}, dimensions={0} | all-to-all | bytes 16384 | tf_op jit(solution)/shard_map/all_to_all | solution.py:492
  141.8 31.4 %all_to_all.13 = f32[32,1,128]{2,1,0:T(1,128)S(1)} all-to-all(f32[32,1,128]{2,1,0:T(1,128)S(1)} %broadcast_in_dim.5), channel_id=1, replica_groups=mesh['gx'=16,'gy'=32] {'gy'}, dimensions={0} | all-to-all | bytes 32768 | tf_op jit(solution)/shard_map/all_to_all | solution.py:492
  173.2 0.6 reduce_sum.20
  (9 shorter events, 0.1 us)
Async XLA Ops:
  0.6 1.0 copy-start
  1.6 11.2 %copy-start.3 = (f32[16,16,256]{2,1,0:T(8,128)S(1)}, f32[16,16,256]{2,1,0:T(8,128)}, u32[]{:S(2)}) copy-start(f32[16,16,256]{2,1,0:T(8,128)} %f_ref.3) | copy-start | bytes 786436
  2.5 10.3 %copy-start.1 = (f32[16,16,256]{2,1,0:T(8,128)S(1)}, f32[16,16,256]{2,1,0:T(8,128)}, u32[]{:S(2)}) copy-start(f32[16,16,256]{2,1,0:T(8,128)} %e_ref.3) | copy-start | bytes 786436
  2.5 10.3 %copy-start.2 = (f32[16,16,256]{2,1,0:T(8,128)S(1)}, f32[16,16,256]{2,1,0:T(8,128)}, u32[]{:S(2)}) copy-start(f32[16,16,256]{2,1,0:T(8,128)} %k_ref.3) | copy-start | bytes 786436
  2.6 6.4 %collective-permute-start = (f32[10,16,256]{2,1,0:T(8,128)S(1)}, f32[10,16,256]{2,1,0:T(8,128)S(1)}, u32[]{:S(2)}, u32[]{:S(2)}) collective-permute-start(f32[10,16,256]{2,1,0:T(8,128)S(1)} %pad_maximum_fusion), channel_id=1, source_target_pairs={{0,32},{32,64},{64,96},{96,128},{128,160},{160,192},{192,224},{224... | collective-permute-start | bytes 491528 | tf_op jit(solution)/shard_map/ppermute | solution.py:486
  6.8 6.1 %collective-permute-start.1 = (f32[10,16,256]{2,1,0:T(8,128)S(1)}, f32[10,16,256]{2,1,0:T(8,128)S(1)}, u32[]{:S(2)}, u32[]{:S(2)}) collective-permute-start(f32[10,16,256]{2,1,0:T(8,128)S(1)} %pad_maximum_fusion.1), channel_id=1, source_target_pairs={{32,0},{64,32},{96,64},{128,96},{160,128},{192,160},{224,192},{256... | collective-permute-start | bytes 491528 | tf_op jit(solution)/shard_map/ppermute | solution.py:486
  12.9 10.2 %collective-permute-start.2 = (f32[2,22,8,256]{3,2,1,0:T(8,128)S(1)}, f32[2,22,8,256]{3,2,1,0:T(8,128)S(1)}, u32[]{:S(2)}, u32[]{:S(2)}) collective-permute-start(f32[2,22,8,256]{3,2,1,0:T(8,128)S(1)} %get-tuple-element.20), channel_id=1, source_target_pairs={{0,1},{1,2},{2,3},{3,4},{4,5},{5,6},{6,7},{7,8},{8,9},{9,10},{10,1... | collective-permute-start | bytes 1081352 | tf_op jit(solution)/shard_map/ppermute | solution.py:486
  18.8 8.7 %collective-permute-start.3 = (f32[2,22,8,256]{3,2,1,0:T(8,128)S(1)}, f32[2,22,8,256]{3,2,1,0:T(8,128)S(1)}, u32[]{:S(2)}, u32[]{:S(2)}) collective-permute-start(f32[2,22,8,256]{3,2,1,0:T(8,128)S(1)} %get-tuple-element.21), channel_id=1, source_target_pairs={{1,0},{2,1},{3,2},{4,3},{5,4},{6,5},{7,6},{8,7},{9,8},{10,9},{11,1... | collective-permute-start | bytes 1081352 | tf_op jit(solution)/shard_map/ppermute | solution.py:486
  39.0 5.1 %collective-permute-start.4 = (f32[4,8,8,128]{3,2,1,0:T(8,128)S(1)}, f32[4,8,8,128]{3,2,1,0:T(8,128)S(1)}, u32[]{:S(2)}, u32[]{:S(2)}) collective-permute-start(f32[4,8,8,128]{3,2,1,0:T(8,128)S(1)} %get-tuple-element.22), channel_id=1, source_target_pairs={{0,32},{32,64},{64,96},{96,128},{128,160},{160,192},{192,224},{224... | collective-permute-start | bytes 393224 | tf_op jit(solution)/shard_map/ppermute | solution.py:486
  42.2 5.7 %collective-permute-start.5 = (f32[4,8,8,128]{3,2,1,0:T(8,128)S(1)}, f32[4,8,8,128]{3,2,1,0:T(8,128)S(1)}, u32[]{:S(2)}, u32[]{:S(2)}) collective-permute-start(f32[4,8,8,128]{3,2,1,0:T(8,128)S(1)} %get-tuple-element.22), channel_id=1, source_target_pairs={{32,0},{64,32},{96,64},{128,96},{160,128},{192,160},{224,192},{256... | collective-permute-start | bytes 393224 | tf_op jit(solution)/shard_map/ppermute | solution.py:486
  47.9 9.1 %collective-permute-start.7 = (f32[4,24,8,128]{3,2,1,0:T(8,128)S(1)}, f32[4,24,8,128]{3,2,1,0:T(8,128)S(1)}, u32[]{:S(2)}, u32[]{:S(2)}) collective-permute-start(f32[4,24,8,128]{3,2,1,0:T(8,128)S(1)} %constant_dynamic-update-slice_fusion.o_ref.o1_ref), channel_id=1, source_target_pairs={{1,0},{2,1},{3,2},{4,3},{5,4},{6,5},{7,6},{8,7},{9,8},{10,9},{11,1... | collective-permute-start | bytes 1179656 | tf_op jit(solution)/shard_map/ppermute | solution.py:486
  49.9 8.4 %collective-permute-start.6 = (f32[4,24,8,128]{3,2,1,0:T(8,128)S(1)}, f32[4,24,8,128]{3,2,1,0:T(8,128)S(1)}, u32[]{:S(2)}, u32[]{:S(2)}) collective-permute-start(f32[4,24,8,128]{3,2,1,0:T(8,128)S(1)} %constant_dynamic-update-slice_fusion.o_ref.o1_ref), channel_id=1, source_target_pairs={{0,1},{1,2},{2,3},{3,4},{4,5},{5,6},{6,7},{7,8},{8,9},{9,10},{10,1... | collective-permute-start | bytes 1179656 | tf_op jit(solution)/shard_map/ppermute | solution.py:486
  72.0 6.1 %collective-permute-start.8 = (f32[24,8,128]{2,1,0:T(8,128)S(1)}, f32[24,8,128]{2,1,0:T(8,128)S(1)}, u32[]{:S(2)}, u32[]{:S(2)}) collective-permute-start(f32[24,8,128]{2,1,0:T(8,128)S(1)} %get-tuple-element.26), channel_id=1, source_target_pairs={{0,32},{32,64},{64,96},{96,128},{128,160},{160,192},{192,224},{224... | collective-permute-start | bytes 294920 | tf_op jit(solution)/shard_map/ppermute | solution.py:486
  76.5 5.4 %collective-permute-start.9 = (f32[24,8,128]{2,1,0:T(8,128)S(1)}, f32[24,8,128]{2,1,0:T(8,128)S(1)}, u32[]{:S(2)}, u32[]{:S(2)}) collective-permute-start(f32[24,8,128]{2,1,0:T(8,128)S(1)} %get-tuple-element.27), channel_id=1, source_target_pairs={{32,0},{64,32},{96,64},{128,96},{160,128},{192,160},{224,192},{256... | collective-permute-start | bytes 294920 | tf_op jit(solution)/shard_map/ppermute | solution.py:486
  81.9 8.7 %collective-permute-start.10 = (f32[54,8,128]{2,1,0:T(8,128)S(1)}, f32[54,8,128]{2,1,0:T(8,128)S(1)}, u32[]{:S(2)}, u32[]{:S(2)}) collective-permute-start(f32[54,8,128]{2,1,0:T(8,128)S(1)} %get-tuple-element.29), channel_id=1, source_target_pairs={{0,1},{1,2},{2,3},{3,4},{4,5},{5,6},{6,7},{7,8},{8,9},{9,10},{10,1... | collective-permute-start | bytes 663560 | tf_op jit(solution)/shard_map/ppermute | solution.py:486
  87.7 7.3 %collective-permute-start.11 = (f32[54,8,128]{2,1,0:T(8,128)S(1)}, f32[54,8,128]{2,1,0:T(8,128)S(1)}, u32[]{:S(2)}, u32[]{:S(2)}) collective-permute-start(f32[54,8,128]{2,1,0:T(8,128)S(1)} %get-tuple-element.30), channel_id=1, source_target_pairs={{1,0},{2,1},{3,2},{4,3},{5,4},{6,5},{7,6},{8,7},{9,8},{10,9},{11,1... | collective-permute-start | bytes 663560 | tf_op jit(solution)/shard_map/ppermute | solution.py:486

commit v2 on v1

--- a/solution.py
+++ b/solution.py
@@ -55,16 +55,22 @@
     return jnp.where(good, 1.0, 0.0).astype(F32)
 
 
+def inner_sides(shape):
+    place, last = lax.axis_index("gy"), lax.axis_size("gy") - 1
+    row = iota(shape, 0)
+    return row >= jnp.where(place == 0, shape[0], 0), row >= jnp.where(place == last, shape[0], 0)
+
+
 def plane_bar(place, size):
     return jnp.where((place >= 0) & (place < size), 0.5, 2.0).astype(F32)
 
 
-def over_planes(first, last, step, unroll=1):
+def over_planes(first, last, step):
     def loop_body(x, carry):
         step(x)
         return carry
 
-    lax.fori_loop(first, last, loop_body, 0, unroll=unroll)
+    lax.fori_loop(first, last, loop_body, 0, unroll=last - first)
 
 
 def fill_weights(e_ref, weights, planes, scale, wrap_free):
@@ -190,13 +196,15 @@
     own_x, own_y, nz = s_ref.shape
     planes = own_x + 2 * RIM_X0
     rows = own_y + 2 * RIM_Y0
+    keep_left, keep_right = inner_sides((8, nz))
     for x in range(planes):
         for index in range(4):
             place = fine_plane(x, index, bricks[index], xl_ref, xr_ref)
             if place is None:
                 windows[index][x] = jnp.zeros((rows, nz), F32)
                 continue
-            left, right = yl_ref[index // 2, x], yr_ref[index // 2, x]
+            left = jnp.where(keep_left, yl_ref[index // 2, x], 0.0)
+            right = jnp.where(keep_right, yr_ref[index // 2, x], 0.0)
             if index % 2 == 0:
                 right = roll(right, 4, 0)
             else:
@@ -251,9 +259,12 @@
     planes, own, nz = o_ref.shape[1:]
     rows = own + 2 * RIM_1
     shape = (rows, nz)
+    keep_left, keep_right = inner_sides((own, nz))
 
     def joined(index, x):
-        return jnp.concatenate([l_ref[index, x], o_ref[index, x], r_ref[index, x]], axis=0)
+        left = jnp.where(keep_left, l_ref[index, x], 0.0)
+        right = jnp.where(keep_right, r_ref[index, x], 0.0)
+        return jnp.concatenate([left, o_ref[index, x], right], axis=0)
 
     def assemble(x):
         e[x] = joined(0, x)
@@ -355,11 +366,12 @@
     nz2 = LANES // 2
     row8 = iota((8, LANES), 0)
     inside = iota(shape2, 1) < nz2
+    keep_left, keep_right = inner_sides((8, LANES))
 
     def window2(at):
         own = roll(o2_ref[at], 4, 0)
-        upper = jnp.where(row8 >= 6, own, yl_ref[at])
-        lower = jnp.where(row8 < 2, own, yr_ref[at])
+        upper = jnp.where(row8 >= 6, own, jnp.where(keep_left, yl_ref[at], 0.0))
+        lower = jnp.where(row8 < 2, own, jnp.where(keep_right, yr_ref[at], 0.0))
         return jnp.concatenate([upper, lower], axis=0)
 
     def assemble2(x):
@@ -400,7 +412,9 @@
     shape1 = (rows1, nz1)
 
     def joined(index, x):
-        return jnp.concatenate([l1_ref[index, x], o1_ref[index, x], r1_ref[index, x]], axis=0)
+        left = jnp.where(keep_left, l1_ref[index, x], 0.0)
+        right = jnp.where(keep_right, r1_ref[index, x], 0.0)
+        return jnp.concatenate([left, o1_ref[index, x], right], axis=0)
 
     def assemble1(x):
         e1[x] = joined(0, x)
@@ -431,7 +445,8 @@
     shape0 = (rows0, nz0)
     base = 2 * planes2
     for x in range(planes0):
-        left, right = yl_ref[base + x], yr_ref[base + x]
+        left = jnp.where(keep_left, yl_ref[base + x], 0.0)
+        right = jnp.where(keep_right, yr_ref[base + x], 0.0)
         left = jnp.concatenate([left, roll(left, 4, 0)], axis=1)
         right = jnp.concatenate([roll(right, 4, 0), right], axis=1)
         tiles = shifted_tiles(u0_ref[x, 0:8, :], u0_ref[x, 8:16, :], left, right)
@@ -456,7 +471,7 @@
         out_ref[x - RIM_X0, 8:16, :] = jnp.where(low, moved[1], moved[2])
         return acc + d * d
 
-    acc = lax.fori_loop(RIM_X0, RIM_X0 + own_x, finish, jnp.zeros(shape0, F32))
+    acc = lax.fori_loop(RIM_X0, RIM_X0 + own_x, finish, jnp.zeros(shape0, F32), unroll=own_x)
     row = iota(shape0, 0)
     acc = jnp.where((row >= RIM_Y0) & (row < RIM_Y0 + own_y), acc, 0.0)
     acc = jnp.sum(acc, axis=0, keepdims=True)
@@ -479,9 +494,9 @@
     )(*args)
 
 
-def swap(upward, downward, axis):
+def swap(upward, downward, axis, ring=False):
     size = lax.axis_size(axis)
-    up = [(i, i + 1) for i in range(size - 1)]
+    up = [(i, (i + 1) % size) for i in range(size if ring else size - 1)]
     down = [(j, i) for i, j in up]
     return lax.ppermute(upward, axis, up), lax.ppermute(downward, axis, down)
 
@@ -505,7 +520,7 @@
     xl, xr = swap(upward, downward, "gx")
     packed = arr(2, planes0, 8, nz)
     upward, downward = call(pack_fine, [packed, packed], [], *fields, xl, xr)
-    yl, yr = swap(upward, downward, "gy")
+    yl, yr = swap(upward, downward, "gy", True)
     own1, own1_y, nz1 = own_x // 2, own_y // 2, nz // 2
     gathered = 2 * own1 * rows0 + 2 * own1 * own_y
     stack1, u0, permit0, ion0, source0 = call(
@@ -517,7 +532,7 @@
 
     xl, xr = swap(stack1, stack1, "gx")
     own = jnp.concatenate([xl, stack1, xr], axis=1)
-    yl1, yr1 = swap(own, own, "gy")
+    yl1, yr1 = swap(own, own, "gy", True)
     planes1 = own1 + 2 * RIM_1
     window1 = (planes1, own1_y + 2 * RIM_1, nz1)
     sent_x = 2 * RIM_2 + 4 * RIM_X0
@@ -536,7 +551,7 @@
         [arr(sent_y, 8, LANES)] * 2 + [arr(2 * planes2, 8, LANES), arr(planes0, own_y, nz)],
         [], xl, xr, stack2, u0,
     )
-    yl, yr = swap(upward, downward, "gy")
+    yl, yr = swap(upward, downward, "gy", True)
     window2 = (planes2, planes2, LANES)
     relaxed, part = call(
         functools.partial(coarse_and_last, size_x=size_x, size_y=size_y),

time: 176 us -> 120 us (0.68)
  Pallas kernels: 57.9 us -> 13.3 us
  starting transfers between devices: 37.5 us -> 33.7 us
  blocking collectives: 45.7 us -> 42 us
  waiting for transfers between devices: 29.3 us -> 25.7 us
    pallas_call x5, Pallas kernels: 57.9 us -> 13.3 us  [call(): pl.pallas_call(kernel, out_shape=outs, in_specs=[pl.BlockSpec(memory_spac...]
    ppermute x12, starting transfers between devices: 37.5 us -> 33.7 us  [swap(): return (lax.ppermute(upward, axis, up), lax.ppermute(downward, axis, down))]
    all_to_all x2, blocking collectives: 45.7 us -> 42 us  [sum_over(): lax.all_to_all(rows, axis, 0, 0, tiled=True)]
    ppermute x12, waiting for transfers between devices: 29.3 us -> 25.7 us  [swap(): return (lax.ppermute(upward, axis, up), lax.ppermute(downward, axis, down))]
where the time goes in v2:
time: 120 us
  blocking collectives  42 us (35%)
  starting transfers between devices  33.7 us (28%)
  waiting for transfers between devices  25.7 us (21%)
  Pallas kernels  13.3 us (11%)
  between operations  2.59 us (2%)
  local copies, waits for them, and re-layouts  1.95 us (2%)
    all_to_all x2, blocking collectives, sum_over(): lax.all_to_all(rows, axis, 0, 0, tiled=True)  42 us
    ppermute x12, starting transfers between devices, swap(): return (lax.ppermute(upward, axis, up), lax.ppermute(downward, axis, down))  33.7 us
    ppermute x12, waiting for transfers between devices, swap(): return (lax.ppermute(upward, axis, up), lax.ppermute(downward, axis, down))  25.7 us
    pallas_call x5, Pallas kernels, call(): pl.pallas_call(kernel, out_shape=outs, in_specs=[pl.BlockSpec(memory_spac...  13.3 us
  transfers between devices with their start and end apart: 12, of which 12 were waited for; matrix products, arithmetic and copies ran while one was open for 0% of the time, Pallas kernels for 0%

profile of v2, /device:TPU:1, one launch (start us, length us, event | category | flops | bytes accessed | tf_op | source)
XLA Modules:
  0.0 119.9 jit_solution(9662343031563907286)
XLA Ops:
  0.6 0.0 copy-start
  0.6 0.9 fusion.2
  1.5 0.1 copy-done
  1.6 0.0 copy-start.3
  1.6 0.9 fusion
  2.5 0.0 copy-start.1
  2.5 0.0 copy-start.2
  2.6 4.2 %collective-permute-start = (f32[10,16,256]{2,1,0:T(8,128)S(1)}, f32[10,16,256]{2,1,0:T(8,128)S(1)}, u32[]{:S(2)}, u32[]{:S(2)}) collective-permute-start(f32[10,16,256]{2,1,0:T(8,128)S(1)} %pad_maximum_fusion), channel_id=1, source_target_pairs={{0,32},{32,64},{64,96},{96,128},{128,160},{160,192},{192,224},{224... | collective-permute-start | bytes 491528 | tf_op jit(solution)/shard_map/ppermute | solution.py:501
  6.8 1.3 %collective-permute-start.1 = (f32[10,16,256]{2,1,0:T(8,128)S(1)}, f32[10,16,256]{2,1,0:T(8,128)S(1)}, u32[]{:S(2)}, u32[]{:S(2)}) collective-permute-start(f32[10,16,256]{2,1,0:T(8,128)S(1)} %pad_maximum_fusion.1), channel_id=1, source_target_pairs={{32,0},{64,32},{96,64},{128,96},{160,128},{192,160},{224,192},{256... | collective-permute-start | bytes 491528 | tf_op jit(solution)/shard_map/ppermute | solution.py:501
  8.1 0.9 collective-permute-done.xl_ref
  9.0 3.8 %collective-permute-done.1.xr_ref = f32[10,16,256]{2,1,0:T(8,128)S(1)} collective-permute-done((f32[10,16,256]{2,1,0:T(8,128)S(1)}, f32[10,16,256]{2,1,0:T(8,128)S(1)}, u32[]{:S(2)}, u32[]{:S(2)}) %collective-permute-start.1) | collective-permute-done | bytes 163872 | tf_op jit(solution)/shard_map/ppermute | solution.py:501
  12.8 0.0 copy-done.3
  12.8 0.0 copy-done.1
  12.8 0.0 copy-done.2
  12.8 0.1 shard_map.59
  12.9 4.0 %collective-permute-start.2 = (f32[2,22,8,256]{3,2,1,0:T(8,128)S(1)}, f32[2,22,8,256]{3,2,1,0:T(8,128)S(1)}, u32[]{:S(2)}, u32[]{:S(2)}) collective-permute-start(f32[2,22,8,256]{3,2,1,0:T(8,128)S(1)} %get-tuple-element.20), channel_id=1, source_target_pairs={{0,1},{1,2},{2,3},{3,4},{4,5},{5,6},{6,7},{7,8},{8,9},{9,10},{10,1... | collective-permute-start | bytes 1081352 | tf_op jit(solution)/shard_map/ppermute | solution.py:501
  16.9 1.3 %collective-permute-start.3 = (f32[2,22,8,256]{3,2,1,0:T(8,128)S(1)}, f32[2,22,8,256]{3,2,1,0:T(8,128)S(1)}, u32[]{:S(2)}, u32[]{:S(2)}) collective-permute-start(f32[2,22,8,256]{3,2,1,0:T(8,128)S(1)} %get-tuple-element.21), channel_id=1, source_target_pairs={{1,0},{2,1},{3,2},{4,3},{5,4},{6,5},{7,6},{8,7},{9,8},{10,9},{11,1... | collective-permute-start | bytes 1081352 | tf_op jit(solution)/shard_map/ppermute | solution.py:501
  18.3 3.0 %collective-permute-done.2.yl_ref = f32[2,22,8,256]{3,2,1,0:T(8,128)S(1)} collective-permute-done((f32[2,22,8,256]{3,2,1,0:T(8,128)S(1)}, f32[2,22,8,256]{3,2,1,0:T(8,128)S(1)}, u32[]{:S(2)}, u32[]{:S(2)}) %collective-permute-start.2) | collective-permute-done | bytes 360480 | tf_op jit(solution)/shard_map/ppermute | solution.py:501
  21.3 2.8 %collective-permute-done.3.yr_ref = f32[2,22,8,256]{3,2,1,0:T(8,128)S(1)} collective-permute-done((f32[2,22,8,256]{3,2,1,0:T(8,128)S(1)}, f32[2,22,8,256]{3,2,1,0:T(8,128)S(1)}, u32[]{:S(2)}, u32[]{:S(2)}) %collective-permute-start.3) | collective-permute-done | bytes 360480 | tf_op jit(solution)/shard_map/ppermute | solution.py:501
  24.1 3.4 %shard_map.60 = (f32[4,8,8,128]{3,2,1,0:T(8,128)S(1)}, f32[16,16,256]{2,1,0:T(8,128)S(1)}, f32[22,24,256]{2,1,0:T(8,128)S(1)}, f32[22,24,256]{2,1,0:T(8,128)S(1)}, f32[22,24,256]{2,1,0:T(8,128)S(1)}) custom-call(f32[16,16,256]{2,1,0:T(8,128)S(1)} %copy-done, f32[16,16,256]{2,1,0:T(8,128)S(1)} %copy-done.1, f32[16,16,256]{2,1,0:T(8,128)S(1)} %copy-done.2, ...), custom_call_target="tpu_custom_call" | custom-call | tf_op jit(solution)/shard_map/pallas_call | solution.py:487
  27.4 3.2 %collective-permute-start.4 = (f32[4,8,8,128]{3,2,1,0:T(8,128)S(1)}, f32[4,8,8,128]{3,2,1,0:T(8,128)S(1)}, u32[]{:S(2)}, u32[]{:S(2)}) collective-permute-start(f32[4,8,8,128]{3,2,1,0:T(8,128)S(1)} %get-tuple-element.22), channel_id=1, source_target_pairs={{0,32},{32,64},{64,96},{96,128},{128,160},{160,192},{192,224},{224... | collective-permute-start | bytes 393224 | tf_op jit(solution)/shard_map/ppermute | solution.py:501
  30.6 1.3 %collective-permute-start.5 = (f32[4,8,8,128]{3,2,1,0:T(8,128)S(1)}, f32[4,8,8,128]{3,2,1,0:T(8,128)S(1)}, u32[]{:S(2)}, u32[]{:S(2)}) collective-permute-start(f32[4,8,8,128]{3,2,1,0:T(8,128)S(1)} %get-tuple-element.22), channel_id=1, source_target_pairs={{32,0},{64,32},{96,64},{128,96},{160,128},{192,160},{224,192},{256... | collective-permute-start | bytes 393224 | tf_op jit(solution)/shard_map/ppermute | solution.py:501
  31.9 0.6 collective-permute-done.4
  32.6 3.8 %collective-permute-done.5 = f32[4,8,8,128]{3,2,1,0:T(8,128)S(1)} collective-permute-done((f32[4,8,8,128]{3,2,1,0:T(8,128)S(1)}, f32[4,8,8,128]{3,2,1,0:T(8,128)S(1)}, u32[]{:S(2)}, u32[]{:S(2)}) %collective-permute-start.5) | collective-permute-done | bytes 131104 | tf_op jit(solution)/shard_map/ppermute | solution.py:501
  36.4 5.6 %collective-permute-start.7 = (f32[4,24,8,128]{3,2,1,0:T(8,128)S(1)}, f32[4,24,8,128]{3,2,1,0:T(8,128)S(1)}, u32[]{:S(2)}, u32[]{:S(2)}) collective-permute-start(f32[4,24,8,128]{3,2,1,0:T(8,128)S(1)} %constant_dynamic-update-slice_fusion.o_ref.o1_ref), channel_id=1, source_target_pairs={{1,0},{2,1},{3,2},{4,3},{5,4},{6,5},{7,6},{8,7},{9,8},{10,9},{11,1... | collective-permute-start | bytes 1179656 | tf_op jit(solution)/shard_map/ppermute | solution.py:501
  42.0 0.0 collective-permute-start.6
  42.0 1.6 %collective-permute-done.7.r_ref.r1_ref = f32[4,24,8,128]{3,2,1,0:T(8,128)S(1)} collective-permute-done((f32[4,24,8,128]{3,2,1,0:T(8,128)S(1)}, f32[4,24,8,128]{3,2,1,0:T(8,128)S(1)}, u32[]{:S(2)}, u32[]{:S(2)}) %collective-permute-start.7) | collective-permute-done | bytes 393248 | tf_op jit(solution)/shard_map/ppermute | solution.py:501
  43.6 3.1 %collective-permute-done.6.l_ref.l1_ref = f32[4,24,8,128]{3,2,1,0:T(8,128)S(1)} collective-permute-done((f32[4,24,8,128]{3,2,1,0:T(8,128)S(1)}, f32[4,24,8,128]{3,2,1,0:T(8,128)S(1)}, u32[]{:S(2)}, u32[]{:S(2)}) %collective-permute-start.6) | collective-permute-done | bytes 393248 | tf_op jit(solution)/shard_map/ppermute | solution.py:501
  46.7 1.7 %shard_map.61 = (f32[24,8,128]{2,1,0:T(8,128)S(1)}, f32[24,8,128]{2,1,0:T(8,128)S(1)}, f32[2,8,8,128]{3,2,1,0:T(8,128)S(1)}, f32[24,24,128]{2,1,0:T(8,128)S(1)}, f32[24,24,128]{2,1,0:T(8,128)S(1)}) custom-call(f32[4,24,8,128]{3,2,1,0:T(8,128)S(1)} %collective-permute-done.6.l_ref.l1_ref, ...), custom_call_target="tpu_custom_call" | custom-call | tf_op jit(solution)/shard_map/pallas_call | solution.py:487
  48.4 4.2 %collective-permute-start.8 = (f32[24,8,128]{2,1,0:T(8,128)S(1)}, f32[24,8,128]{2,1,0:T(8,128)S(1)}, u32[]{:S(2)}, u32[]{:S(2)}) collective-permute-start(f32[24,8,128]{2,1,0:T(8,128)S(1)} %get-tuple-element.26), channel_id=1, source_target_pairs={{0,32},{32,64},{64,96},{96,128},{128,160},{160,192},{192,224},{224... | collective-permute-start | bytes 294920 | tf_op jit(solution)/shard_map/ppermute | solution.py:501
  52.6 1.3 %collective-permute-start.9 = (f32[24,8,128]{2,1,0:T(8,128)S(1)}, f32[24,8,128]{2,1,0:T(8,128)S(1)}, u32[]{:S(2)}, u32[]{:S(2)}) collective-permute-start(f32[24,8,128]{2,1,0:T(8,128)S(1)} %get-tuple-element.27), channel_id=1, source_target_pairs={{32,0},{64,32},{96,64},{128,96},{160,128},{192,160},{224,192},{256... | collective-permute-start | bytes 294920 | tf_op jit(solution)/shard_map/ppermute | solution.py:501
  53.9 0.3 collective-permute-done.8.xl_ref
  54.2 4.0 %collective-permute-done.9.xr_ref = f32[24,8,128]{2,1,0:T(8,128)S(1)} collective-permute-done((f32[24,8,128]{2,1,0:T(8,128)S(1)}, f32[24,8,128]{2,1,0:T(8,128)S(1)}, u32[]{:S(2)}, u32[]{:S(2)}) %collective-permute-start.9) | collective-permute-done | bytes 98336 | tf_op jit(solution)/shard_map/ppermute | solution.py:501
  58.2 0.1 shard_map.62
  58.3 3.6 %collective-permute-start.10 = (f32[54,8,128]{2,1,0:T(8,128)S(1)}, f32[54,8,128]{2,1,0:T(8,128)S(1)}, u32[]{:S(2)}, u32[]{:S(2)}) collective-permute-start(f32[54,8,128]{2,1,0:T(8,128)S(1)} %get-tuple-element.29), channel_id=1, source_target_pairs={{0,1},{1,2},{2,3},{3,4},{4,5},{5,6},{6,7},{7,8},{8,9},{9,10},{10,1... | collective-permute-start | bytes 663560 | tf_op jit(solution)/shard_map/ppermute | solution.py:501
  61.9 3.6 %collective-permute-start.11 = (f32[54,8,128]{2,1,0:T(8,128)S(1)}, f32[54,8,128]{2,1,0:T(8,128)S(1)}, u32[]{:S(2)}, u32[]{:S(2)}) collective-permute-start(f32[54,8,128]{2,1,0:T(8,128)S(1)} %get-tuple-element.30), channel_id=1, source_target_pairs={{1,0},{2,1},{3,2},{4,3},{5,4},{6,5},{7,6},{8,7},{9,8},{10,9},{11,1... | collective-permute-start | bytes 663560 | tf_op jit(solution)/shard_map/ppermute | solution.py:501
  65.6 0.9 collective-permute-done.10.yl_ref
  66.5 0.8 collective-permute-done.11.yr_ref
  67.3 8.1 %shard_map.63 = (f32[16,16,256]{2,1,0:T(8,128)}, f32[8,128]{1,0:T(8,128)S(1)}) custom-call(f32[4,24,8,128]{3,2,1,0:T(8,128)S(1)} %collective-permute-done.6.l_ref.l1_ref, f32[4,24,8,128]{3,2,1,0:T(8,128)S(1)} %constant_dynamic-update-slice_fusion.o_ref.o1_ref, f32[4,24,8,128]{3,2,1,0:T(8,128)S(1)} %collective-permute-done.7.r_ref.r1_ref, ...), custom_call_target="tpu_custom_call" | custom-call | tf_op jit(solution)/shard_map/pallas_call | solution.py:487
  75.4 14.3 %all_to_all.12 = f32[16,1,128]{2,1,0:T(1,128)S(1)} all-to-all(f32[16,1,128]{2,1,0:T(1,128)S(1)} %broadcast_in_dim.4), channel_id=1, replica_groups=mesh['gx'=16,'gy'=32] {'gx'}, dimensions={0} | all-to-all | bytes 16384 | tf_op jit(solution)/shard_map/all_to_all | solution.py:507
  89.7 27.7 %all_to_all.13 = f32[32,1,128]{2,1,0:T(1,128)S(1)} all-to-all(f32[32,1,128]{2,1,0:T(1,128)S(1)} %broadcast_in_dim.5), channel_id=1, replica_groups=mesh['gx'=16,'gy'=32] {'gy'}, dimensions={0} | all-to-all | bytes 32768 | tf_op jit(solution)/shard_map/all_to_all | solution.py:507
  117.4 0.6 reduce_sum.20
  (9 shorter events, 0.1 us)
Async XLA Ops:
  0.6 1.0 copy-start
  1.6 11.2 %copy-start.3 = (f32[16,16,256]{2,1,0:T(8,128)S(1)}, f32[16,16,256]{2,1,0:T(8,128)}, u32[]{:S(2)}) copy-start(f32[16,16,256]{2,1,0:T(8,128)} %f_ref.3) | copy-start | bytes 786436
  2.5 10.3 %copy-start.1 = (f32[16,16,256]{2,1,0:T(8,128)S(1)}, f32[16,16,256]{2,1,0:T(8,128)}, u32[]{:S(2)}) copy-start(f32[16,16,256]{2,1,0:T(8,128)} %e_ref.3) | copy-start | bytes 786436
  2.5 10.3 %copy-start.2 = (f32[16,16,256]{2,1,0:T(8,128)S(1)}, f32[16,16,256]{2,1,0:T(8,128)}, u32[]{:S(2)}) copy-start(f32[16,16,256]{2,1,0:T(8,128)} %k_ref.3) | copy-start | bytes 786436
  2.6 6.4 %collective-permute-start = (f32[10,16,256]{2,1,0:T(8,128)S(1)}, f32[10,16,256]{2,1,0:T(8,128)S(1)}, u32[]{:S(2)}, u32[]{:S(2)}) collective-permute-start(f32[10,16,256]{2,1,0:T(8,128)S(1)} %pad_maximum_fusion), channel_id=1, source_target_pairs={{0,32},{32,64},{64,96},{96,128},{128,160},{160,192},{192,224},{224... | collective-permute-start | bytes 491528 | tf_op jit(solution)/shard_map/ppermute | solution.py:501
  6.8 6.1 %collective-permute-start.1 = (f32[10,16,256]{2,1,0:T(8,128)S(1)}, f32[10,16,256]{2,1,0:T(8,128)S(1)}, u32[]{:S(2)}, u32[]{:S(2)}) collective-permute-start(f32[10,16,256]{2,1,0:T(8,128)S(1)} %pad_maximum_fusion.1), channel_id=1, source_target_pairs={{32,0},{64,32},{96,64},{128,96},{160,128},{192,160},{224,192},{256... | collective-permute-start | bytes 491528 | tf_op jit(solution)/shard_map/ppermute | solution.py:501
  12.9 8.4 %collective-permute-start.2 = (f32[2,22,8,256]{3,2,1,0:T(8,128)S(1)}, f32[2,22,8,256]{3,2,1,0:T(8,128)S(1)}, u32[]{:S(2)}, u32[]{:S(2)}) collective-permute-start(f32[2,22,8,256]{3,2,1,0:T(8,128)S(1)} %get-tuple-element.20), channel_id=1, source_target_pairs={{0,1},{1,2},{2,3},{3,4},{4,5},{5,6},{6,7},{7,8},{8,9},{9,10},{10,1... | collective-permute-start | bytes 1081352 | tf_op jit(solution)/shard_map/ppermute | solution.py:501
  16.9 7.1 %collective-permute-start.3 = (f32[2,22,8,256]{3,2,1,0:T(8,128)S(1)}, f32[2,22,8,256]{3,2,1,0:T(8,128)S(1)}, u32[]{:S(2)}, u32[]{:S(2)}) collective-permute-start(f32[2,22,8,256]{3,2,1,0:T(8,128)S(1)} %get-tuple-element.21), channel_id=1, source_target_pairs={{1,0},{2,1},{3,2},{4,3},{5,4},{6,5},{7,6},{8,7},{9,8},{10,9},{11,1... | collective-permute-start | bytes 1081352 | tf_op jit(solution)/shard_map/ppermute | solution.py:501
  27.4 5.1 %collective-permute-start.4 = (f32[4,8,8,128]{3,2,1,0:T(8,128)S(1)}, f32[4,8,8,128]{3,2,1,0:T(8,128)S(1)}, u32[]{:S(2)}, u32[]{:S(2)}) collective-permute-start(f32[4,8,8,128]{3,2,1,0:T(8,128)S(1)} %get-tuple-element.22), channel_id=1, source_target_pairs={{0,32},{32,64},{64,96},{96,128},{128,160},{160,192},{192,224},{224... | collective-permute-start | bytes 393224 | tf_op jit(solution)/shard_map/ppermute | solution.py:501
  30.6 5.7 %collective-permute-start.5 = (f32[4,8,8,128]{3,2,1,0:T(8,128)S(1)}, f32[4,8,8,128]{3,2,1,0:T(8,128)S(1)}, u32[]{:S(2)}, u32[]{:S(2)}) collective-permute-start(f32[4,8,8,128]{3,2,1,0:T(8,128)S(1)} %get-tuple-element.22), channel_id=1, source_target_pairs={{32,0},{64,32},{96,64},{128,96},{160,128},{192,160},{224,192},{256... | collective-permute-start | bytes 393224 | tf_op jit(solution)/shard_map/ppermute | solution.py:501
  36.4 7.3 %collective-permute-start.7 = (f32[4,24,8,128]{3,2,1,0:T(8,128)S(1)}, f32[4,24,8,128]{3,2,1,0:T(8,128)S(1)}, u32[]{:S(2)}, u32[]{:S(2)}) collective-permute-start(f32[4,24,8,128]{3,2,1,0:T(8,128)S(1)} %constant_dynamic-update-slice_fusion.o_ref.o1_ref), channel_id=1, source_target_pairs={{1,0},{2,1},{3,2},{4,3},{5,4},{6,5},{7,6},{8,7},{9,8},{10,9},{11,1... | collective-permute-start | bytes 1179656 | tf_op jit(solution)/shard_map/ppermute | solution.py:501
  42.0 4.7 %collective-permute-start.6 = (f32[4,24,8,128]{3,2,1,0:T(8,128)S(1)}, f32[4,24,8,128]{3,2,1,0:T(8,128)S(1)}, u32[]{:S(2)}, u32[]{:S(2)}) collective-permute-start(f32[4,24,8,128]{3,2,1,0:T(8,128)S(1)} %constant_dynamic-update-slice_fusion.o_ref.o1_ref), channel_id=1, source_target_pairs={{0,1},{1,2},{2,3},{3,4},{4,5},{5,6},{6,7},{7,8},{8,9},{9,10},{10,1... | collective-permute-start | bytes 1179656 | tf_op jit(solution)/shard_map/ppermute | solution.py:501
  48.4 5.8 %collective-permute-start.8 = (f32[24,8,128]{2,1,0:T(8,128)S(1)}, f32[24,8,128]{2,1,0:T(8,128)S(1)}, u32[]{:S(2)}, u32[]{:S(2)}) collective-permute-start(f32[24,8,128]{2,1,0:T(8,128)S(1)} %get-tuple-element.26), channel_id=1, source_target_pairs={{0,32},{32,64},{64,96},{96,128},{128,160},{160,192},{192,224},{224... | collective-permute-start | bytes 294920 | tf_op jit(solution)/shard_map/ppermute | solution.py:501
  52.6 5.6 %collective-permute-start.9 = (f32[24,8,128]{2,1,0:T(8,128)S(1)}, f32[24,8,128]{2,1,0:T(8,128)S(1)}, u32[]{:S(2)}, u32[]{:S(2)}) collective-permute-start(f32[24,8,128]{2,1,0:T(8,128)S(1)} %get-tuple-element.27), channel_id=1, source_target_pairs={{32,0},{64,32},{96,64},{128,96},{160,128},{192,160},{224,192},{256... | collective-permute-start | bytes 294920 | tf_op jit(solution)/shard_map/ppermute | solution.py:501
  58.3 8.2 %collective-permute-start.10 = (f32[54,8,128]{2,1,0:T(8,128)S(1)}, f32[54,8,128]{2,1,0:T(8,128)S(1)}, u32[]{:S(2)}, u32[]{:S(2)}) collective-permute-start(f32[54,8,128]{2,1,0:T(8,128)S(1)} %get-tuple-element.29), channel_id=1, source_target_pairs={{0,1},{1,2},{2,3},{3,4},{4,5},{5,6},{6,7},{7,8},{8,9},{9,10},{10,1... | collective-permute-start | bytes 663560 | tf_op jit(solution)/shard_map/ppermute | solution.py:501
  61.9 5.4 %collective-permute-start.11 = (f32[54,8,128]{2,1,0:T(8,128)S(1)}, f32[54,8,128]{2,1,0:T(8,128)S(1)}, u32[]{:S(2)}, u32[]{:S(2)}) collective-permute-start(f32[54,8,128]{2,1,0:T(8,128)S(1)} %get-tuple-element.30), channel_id=1, source_target_pairs={{1,0},{2,1},{3,2},{4,3},{5,4},{6,5},{7,6},{8,7},{9,8},{10,9},{11,1... | collective-permute-start | bytes 663560 | tf_op jit(solution)/shard_map/ppermute | solution.py:501

commit v3 on v2

--- a/solution.py
+++ b/solution.py
@@ -10,7 +10,6 @@
 OMEGA = 0.8
 LN2 = 0.6931471805599453
 F32 = jnp.float32
-HIGHEST = lax.Precision.HIGHEST
 LANES = 128
 VMEM_LIMIT = 24 * 1024 * 1024
 
@@ -33,7 +32,16 @@
 
 
 def dot(left, right):
-    return jnp.dot(left, right, precision=HIGHEST, preferred_element_type=F32)
+    return jnp.dot(left, right, precision=lax.Precision.HIGHEST, preferred_element_type=F32)
+
+
+def dot_parts(left, right):
+    high = left.astype(jnp.bfloat16)
+    rest = left - high.astype(F32)
+    middle = rest.astype(jnp.bfloat16)
+    low = (rest - middle.astype(F32)).astype(jnp.bfloat16)
+    parts = jnp.concatenate([low, middle, high], axis=1)
+    return jnp.dot(parts, jnp.concatenate([right.astype(jnp.bfloat16)] * 3, axis=0), preferred_element_type=F32)
 
 
 def low_half(shape):
@@ -187,8 +195,8 @@
 
 def fine_first(
     s_ref, e_ref, k_ref, f_ref, xl_ref, xr_ref, yl_ref, yr_ref,
-    stack_ref, u0_ref, ew_ref, kw_ref, fw_ref,
-    ua, ub, wx, wy, wz, wb, total, gather, summed,
+    stack_ref, u0_ref, kw_ref, fw_ref, wx, wy, wz, wb, total,
+    ua, ub, ew_ref, gather, summed,
     *, size_x, size_y,
 ):
     bricks = (s_ref, e_ref, k_ref, f_ref)
@@ -252,8 +260,8 @@
 
 def middle_first(
     l_ref, o_ref, r_ref, u0_ref,
-    up_ref, down_ref, stack_ref, w_ref, f_ref,
-    e, k, v, wa, wx, wy, wz, wb, total, gather, summed,
+    up_ref, down_ref, stack_ref, w_ref, f_ref, k, v, wx, wy, wz, wb, total,
+    e, wa, gather, summed,
     *, size_x, size_y,
 ):
     planes, own, nz = o_ref.shape[1:]
@@ -352,11 +360,12 @@
 
 
 def coarse_and_last(
-    l1_ref, o1_ref, r1_ref, w1_ref, f1_ref, yl_ref, yr_ref, o2_ref, u0_ref, ew_ref, kw_ref, fw_ref,
+    yl_ref, yr_ref, o2_ref, u0_ref,
+    w1_ref, f1_ref, k1, v1_ref, wx1, wy1, wz1, wb1, t1,
+    kw_ref, fw_ref, wx0, wy0, wz0, wb0, t0,
     out_ref, part_ref,
     e2, k2, v2, f2, a2, b2, wx2, wy2, wz2, t2, q2, s2, d2,
-    e1, k1, a1, b1, wx1, wy1, wz1, wb1, t1, d1,
-    a0, b0, wx0, wy0, wz0, wb0, t0, q0,
+    a1, b1, d1, a0, b0, q0,
     *, size_x, size_y,
 ):
     place_x, place_y = lax.axis_index("gx"), lax.axis_index("gy")
@@ -400,29 +409,17 @@
         source = target
     for j in range(8):
         q2[16 * j : 16 * j + 16, :] = source[4 + j] - v2[4 + j]
-    s2[...] = dot(q2[...], shared_matrix(LANES, LANES, 1, 2, 1.0))
-    rows1 = o1_ref.shape[2] + 2 * RIM_1
+    s2[...] = dot_parts(q2[...], shared_matrix(LANES, LANES, 1, 2, 1.0))
+    planes1, rows1, nz1 = w1_ref.shape
     d2[...] = jnp.zeros(d2.shape, F32)
     for j in range(8):
         rows = roll(s2[16 * j : 16 * j + 16, :], -4, 0)[:8]
         d2[pl.ds(rows1 * j + 4, 8, 2), :] = rows
         d2[pl.ds(rows1 * j + 5, 8, 2), :] = rows
 
-    planes1, own1, nz1 = o1_ref.shape[1:]
+    own1 = planes1 - 2 * RIM_1
     shape1 = (rows1, nz1)
-
-    def joined(index, x):
-        left = jnp.where(keep_left, l1_ref[index, x], 0.0)
-        right = jnp.where(keep_right, r1_ref[index, x], 0.0)
-        return jnp.concatenate([left, o1_ref[index, x], right], axis=0)
-
-    def assemble1(x):
-        e1[x] = joined(0, x)
-        k1[x] = joined(1, x)
-
-    over_planes(0, planes1, assemble1)
     weights1 = (wx1, wy1, wz1, wb1, t1)
-    fill_weights(e1, weights1, planes1, 0.25, False)
     origin_x = place_x * own1 - RIM_1
     origin_y = place_y * own1 - RIM_1
     for x in range(4, 20):
@@ -433,11 +430,11 @@
     mask = row_mask(shape1, 6, rows1 - 6, origin_y, size_y // 2)
     sweep(b1, a1, weights1, k1, f1_ref, 6, planes1 - 6, mask, origin_x, size_x // 2)
     for j in range(12):
-        rows = roll(a1[6 + j] - joined(2, 6 + j), -6, 0)[:16]
+        rows = roll(a1[6 + j] - v1_ref[6 + j], -6, 0)[:16]
         d1[pl.ds(32 * j, 16, 2), :] = rows
         d1[pl.ds(32 * j + 1, 16, 2), :] = rows
     nz0 = 2 * nz1
-    q0[...] = dot(d1[...], shared_matrix(nz1, nz0, 1, 2, 1.0))
+    q0[...] = dot_parts(d1[...], shared_matrix(nz1, nz0, 1, 2, 1.0))
 
     own_x, own_y = out_ref.shape[:2]
     planes0 = own_x + 2 * RIM_X0
@@ -454,7 +451,6 @@
         for i, tile in enumerate(tiles):
             a0[x, 8 * i : 8 * i + 8, :] = tile + q0[at + 8 * i : at + 8 * i + 8, :]
     weights0 = (wx0, wy0, wz0, wb0, t0)
-    fill_weights(ew_ref, weights0, planes0, 1.0, False)
     origin_x = place_x * own_x - RIM_X0
     origin_y = place_y * own_y - RIM_Y0
     mask = row_mask(shape0, 2, rows0 - 2, origin_y, size_y)
@@ -475,7 +471,7 @@
     row = iota(shape0, 0)
     acc = jnp.where((row >= RIM_Y0) & (row < RIM_Y0 + own_y), acc, 0.0)
     acc = jnp.sum(acc, axis=0, keepdims=True)
-    acc = acc[:, :LANES] + acc[:, LANES:]
+    acc = jnp.sum(acc, axis=1, keepdims=True)
     part_ref[...] = jnp.broadcast_to(acc, part_ref.shape)
 
 
@@ -523,10 +519,10 @@
     yl, yr = swap(upward, downward, "gy", True)
     own1, own1_y, nz1 = own_x // 2, own_y // 2, nz // 2
     gathered = 2 * own1 * rows0 + 2 * own1 * own_y
-    stack1, u0, permit0, ion0, source0 = call(
+    stack1, u0, *level0 = call(
         functools.partial(fine_first, size_x=size_x, size_y=size_y),
-        [arr(4, own1, own1_y, nz1), arr(own_x, own_y, nz)] + [arr(*window0)] * 3,
-        [window0] * 7 + [(gathered, nz), (gathered, nz1)],
+        [arr(4, own1, own1_y, nz1), arr(own_x, own_y, nz)] + [arr(*window0)] * 7,
+        [window0] * 3 + [(gathered, nz), (gathered, nz1)],
         *fields, xl, xr, yl, yr,
     )
 
@@ -536,10 +532,10 @@
     planes1 = own1 + 2 * RIM_1
     window1 = (planes1, own1_y + 2 * RIM_1, nz1)
     sent_x = 2 * RIM_2 + 4 * RIM_X0
-    upward, downward, stack2, w1, f1 = call(
+    upward, downward, stack2, *level1 = call(
         functools.partial(middle_first, size_x=size_x // 2, size_y=size_y // 2),
-        [arr(sent_x, 8, LANES)] * 2 + [arr(2, 8, 8, LANES)] + [arr(*window1)] * 2,
-        [window1] * 9 + [(16 * window1[1], 2 * nz1), (16 * window1[1], nz1)],
+        [arr(sent_x, 8, LANES)] * 2 + [arr(2, 8, 8, LANES)] + [arr(*window1)] * 9,
+        [window1] * 2 + [(16 * window1[1], 2 * nz1), (16 * window1[1], nz1)],
         yl1, own, yr1, u0,
     )
 
@@ -557,10 +553,10 @@
         functools.partial(coarse_and_last, size_x=size_x, size_y=size_y),
         [arr(own_x, own_y, nz), arr(8, LANES)],
         [window2] * 10 + [(LANES, LANES)] * 2 + [(8 * window1[1], LANES)]
-        + [window1] * 9 + [(12 * 32, nz1)] + [window0] * 7 + [(12 * 32, nz)],
-        yl1, own, yr1, w1, f1, yl, yr, own2, rim0, permit0, ion0, source0,
+        + [window1] * 2 + [(12 * 32, nz1)] + [window0] * 2 + [(12 * 32, nz)],
+        yl, yr, own2, rim0, *level1, *level0,
     )
-    total = jnp.sum(sum_over(sum_over(part[:1], "gx"), "gy"))
+    total = sum_over(sum_over(part[:1], "gx"), "gy")[0, 0]
     return relaxed, jnp.sqrt(total / (size_x * size_y * nz))
 
 

time: 120 us -> 117 us (0.975)
  Pallas kernels: 13.3 us -> 11.3 us
    pallas_call x5, Pallas kernels: 13.3 us -> 11.3 us  [call(): pl.pallas_call(kernel, out_shape=outs, in_specs=[pl.BlockSpec(memory_spac...]
where the time goes in v3:
time: 117 us
  blocking collectives  42 us (36%)
  starting transfers between devices  33.7 us (29%)
  waiting for transfers between devices  25.7 us (22%)
  Pallas kernels  11.3 us (10%)
  between operations  1.98 us (2%)
  local copies, waits for them, and re-layouts  1.95 us (2%)
    all_to_all x2, blocking collectives, sum_over(): lax.all_to_all(rows, axis, 0, 0, tiled=True)  42 us
    ppermute x12, starting transfers between devices, swap(): return (lax.ppermute(upward, axis, up), lax.ppermute(downward, axis, down))  33.7 us
    ppermute x12, waiting for transfers between devices, swap(): return (lax.ppermute(upward, axis, up), lax.ppermute(downward, axis, down))  25.7 us
    pallas_call x5, Pallas kernels, call(): pl.pallas_call(kernel, out_shape=outs, in_specs=[pl.BlockSpec(memory_spac...  11.3 us
  transfers between devices with their start and end apart: 12, of which 12 were waited for; matrix products, arithmetic and copies ran while one was open for 0% of the time, Pallas kernels for 0%

profile of v3, /device:TPU:1, one launch (start us, length us, event | category | flops | bytes accessed | tf_op | source)
XLA Modules:
  0.0 116.6 jit_solution(9642561031905725845)
XLA Ops:
  0.6 0.0 copy-start
  0.6 0.9 fusion.2
  1.5 0.1 copy-done
  1.6 0.0 copy-start.3
  1.6 0.9 fusion
  2.5 0.0 copy-start.1
  2.5 0.0 copy-start.2
  2.6 4.2 %collective-permute-start = (f32[10,16,256]{2,1,0:T(8,128)S(1)}, f32[10,16,256]{2,1,0:T(8,128)S(1)}, u32[]{:S(2)}, u32[]{:S(2)}) collective-permute-start(f32[10,16,256]{2,1,0:T(8,128)S(1)} %pad_maximum_fusion), channel_id=1, source_target_pairs={{0,32},{32,64},{64,96},{96,128},{128,160},{160,192},{192,224},{224... | collective-permute-start | bytes 491528 | tf_op jit(solution)/shard_map/ppermute | solution.py:497
  6.8 1.3 %collective-permute-start.1 = (f32[10,16,256]{2,1,0:T(8,128)S(1)}, f32[10,16,256]{2,1,0:T(8,128)S(1)}, u32[]{:S(2)}, u32[]{:S(2)}) collective-permute-start(f32[10,16,256]{2,1,0:T(8,128)S(1)} %pad_maximum_fusion.1), channel_id=1, source_target_pairs={{32,0},{64,32},{96,64},{128,96},{160,128},{192,160},{224,192},{256... | collective-permute-start | bytes 491528 | tf_op jit(solution)/shard_map/ppermute | solution.py:497
  8.1 0.9 collective-permute-done.xl_ref
  9.0 3.8 %collective-permute-done.1.xr_ref = f32[10,16,256]{2,1,0:T(8,128)S(1)} collective-permute-done((f32[10,16,256]{2,1,0:T(8,128)S(1)}, f32[10,16,256]{2,1,0:T(8,128)S(1)}, u32[]{:S(2)}, u32[]{:S(2)}) %collective-permute-start.1) | collective-permute-done | bytes 163872 | tf_op jit(solution)/shard_map/ppermute | solution.py:497
  12.8 0.0 copy-done.3
  12.8 0.0 copy-done.1
  12.8 0.0 copy-done.2
  12.8 0.1 shard_map.59
  12.9 4.0 %collective-permute-start.2 = (f32[2,22,8,256]{3,2,1,0:T(8,128)S(1)}, f32[2,22,8,256]{3,2,1,0:T(8,128)S(1)}, u32[]{:S(2)}, u32[]{:S(2)}) collective-permute-start(f32[2,22,8,256]{3,2,1,0:T(8,128)S(1)} %get-tuple-element.31), channel_id=1, source_target_pairs={{0,1},{1,2},{2,3},{3,4},{4,5},{5,6},{6,7},{7,8},{8,9},{9,10},{10,1... | collective-permute-start | bytes 1081352 | tf_op jit(solution)/shard_map/ppermute | solution.py:497
  16.9 1.3 %collective-permute-start.3 = (f32[2,22,8,256]{3,2,1,0:T(8,128)S(1)}, f32[2,22,8,256]{3,2,1,0:T(8,128)S(1)}, u32[]{:S(2)}, u32[]{:S(2)}) collective-permute-start(f32[2,22,8,256]{3,2,1,0:T(8,128)S(1)} %get-tuple-element.32), channel_id=1, source_target_pairs={{1,0},{2,1},{3,2},{4,3},{5,4},{6,5},{7,6},{8,7},{9,8},{10,9},{11,1... | collective-permute-start | bytes 1081352 | tf_op jit(solution)/shard_map/ppermute | solution.py:497
  18.3 3.0 %collective-permute-done.2.yl_ref = f32[2,22,8,256]{3,2,1,0:T(8,128)S(1)} collective-permute-done((f32[2,22,8,256]{3,2,1,0:T(8,128)S(1)}, f32[2,22,8,256]{3,2,1,0:T(8,128)S(1)}, u32[]{:S(2)}, u32[]{:S(2)}) %collective-permute-start.2) | collective-permute-done | bytes 360480 | tf_op jit(solution)/shard_map/ppermute | solution.py:497
  21.3 2.8 %collective-permute-done.3.yr_ref = f32[2,22,8,256]{3,2,1,0:T(8,128)S(1)} collective-permute-done((f32[2,22,8,256]{3,2,1,0:T(8,128)S(1)}, f32[2,22,8,256]{3,2,1,0:T(8,128)S(1)}, u32[]{:S(2)}, u32[]{:S(2)}) %collective-permute-start.3) | collective-permute-done | bytes 360480 | tf_op jit(solution)/shard_map/ppermute | solution.py:497
  24.1 3.3 %shard_map.60 = (f32[4,8,8,128]{3,2,1,0:T(8,128)S(1)}, f32[16,16,256]{2,1,0:T(8,128)S(1)}, f32[22,24,256]{2,1,0:T(8,128)S(1)}, f32[22,24,256]{2,1,0:T(8,128)S(1)...) custom-call(f32[16,16,256]{2,1,0:T(8,128)S(1)} %copy-done, ...), custom_call_target="tpu_custom_call" | custom-call | tf_op jit(solution)/shard_map/pallas_call | solution.py:483
  27.4 3.2 %collective-permute-start.4 = (f32[4,8,8,128]{3,2,1,0:T(8,128)S(1)}, f32[4,8,8,128]{3,2,1,0:T(8,128)S(1)}, u32[]{:S(2)}, u32[]{:S(2)}) collective-permute-start(f32[4,8,8,128]{3,2,1,0:T(8,128)S(1)} %get-tuple-element.33), channel_id=1, source_target_pairs={{0,32},{32,64},{64,96},{96,128},{128,160},{160,192},{192,224},{224... | collective-permute-start | bytes 393224 | tf_op jit(solution)/shard_map/ppermute | solution.py:497
  30.6 1.3 %collective-permute-start.5 = (f32[4,8,8,128]{3,2,1,0:T(8,128)S(1)}, f32[4,8,8,128]{3,2,1,0:T(8,128)S(1)}, u32[]{:S(2)}, u32[]{:S(2)}) collective-permute-start(f32[4,8,8,128]{3,2,1,0:T(8,128)S(1)} %get-tuple-element.33), channel_id=1, source_target_pairs={{32,0},{64,32},{96,64},{128,96},{160,128},{192,160},{224,192},{256... | collective-permute-start | bytes 393224 | tf_op jit(solution)/shard_map/ppermute | solution.py:497
  31.9 0.6 collective-permute-done.4
  32.5 3.8 %collective-permute-done.5 = f32[4,8,8,128]{3,2,1,0:T(8,128)S(1)} collective-permute-done((f32[4,8,8,128]{3,2,1,0:T(8,128)S(1)}, f32[4,8,8,128]{3,2,1,0:T(8,128)S(1)}, u32[]{:S(2)}, u32[]{:S(2)}) %collective-permute-start.5) | collective-permute-done | bytes 131104 | tf_op jit(solution)/shard_map/ppermute | solution.py:497
  36.3 5.6 %collective-permute-start.7 = (f32[4,24,8,128]{3,2,1,0:T(8,128)S(1)}, f32[4,24,8,128]{3,2,1,0:T(8,128)S(1)}, u32[]{:S(2)}, u32[]{:S(2)}) collective-permute-start(f32[4,24,8,128]{3,2,1,0:T(8,128)S(1)} %constant_dynamic-update-slice_fusion.o_ref), channel_id=1, source_target_pairs={{1,0},{2,1},{3,2},{4,3},{5,4},{6,5},{7,6},{8,7},{9,8},{10,9},{11,1... | collective-permute-start | bytes 1179656 | tf_op jit(solution)/shard_map/ppermute | solution.py:497
  41.9 0.0 collective-permute-start.6
  41.9 1.6 %collective-permute-done.7.r_ref = f32[4,24,8,128]{3,2,1,0:T(8,128)S(1)} collective-permute-done((f32[4,24,8,128]{3,2,1,0:T(8,128)S(1)}, f32[4,24,8,128]{3,2,1,0:T(8,128)S(1)}, u32[]{:S(2)}, u32[]{:S(2)}) %collective-permute-start.7) | collective-permute-done | bytes 393248 | tf_op jit(solution)/shard_map/ppermute | solution.py:497
  43.6 3.1 %collective-permute-done.6.l_ref = f32[4,24,8,128]{3,2,1,0:T(8,128)S(1)} collective-permute-done((f32[4,24,8,128]{3,2,1,0:T(8,128)S(1)}, f32[4,24,8,128]{3,2,1,0:T(8,128)S(1)}, u32[]{:S(2)}, u32[]{:S(2)}) %collective-permute-start.6) | collective-permute-done | bytes 393248 | tf_op jit(solution)/shard_map/ppermute | solution.py:497
  46.7 1.8 %shard_map.61 = (f32[24,8,128]{2,1,0:T(8,128)S(1)}, f32[24,8,128]{2,1,0:T(8,128)S(1)}, f32[2,8,8,128]{3,2,1,0:T(8,128)S(1)}, f32[24,24,128]{2,1,0:T(8,128)S(1)},...) custom-call(f32[4,24,8,128]{3,2,1,0:T(8,128)S(1)} %collective-permut, ...), custom_call_target="tpu_custom_call" | custom-call | tf_op jit(solution)/shard_map/pallas_call | solution.py:483
  48.5 4.2 %collective-permute-start.8 = (f32[24,8,128]{2,1,0:T(8,128)S(1)}, f32[24,8,128]{2,1,0:T(8,128)S(1)}, u32[]{:S(2)}, u32[]{:S(2)}) collective-permute-start(f32[24,8,128]{2,1,0:T(8,128)S(1)} %get-tuple-element.35), channel_id=1, source_target_pairs={{0,32},{32,64},{64,96},{96,128},{128,160},{160,192},{192,224},{224... | collective-permute-start | bytes 294920 | tf_op jit(solution)/shard_map/ppermute | solution.py:497
  52.7 1.3 %collective-permute-start.9 = (f32[24,8,128]{2,1,0:T(8,128)S(1)}, f32[24,8,128]{2,1,0:T(8,128)S(1)}, u32[]{:S(2)}, u32[]{:S(2)}) collective-permute-start(f32[24,8,128]{2,1,0:T(8,128)S(1)} %get-tuple-element.36), channel_id=1, source_target_pairs={{32,0},{64,32},{96,64},{128,96},{160,128},{192,160},{224,192},{256... | collective-permute-start | bytes 294920 | tf_op jit(solution)/shard_map/ppermute | solution.py:497
  54.0 0.3 collective-permute-done.8.xl_ref
  54.3 4.0 %collective-permute-done.9.xr_ref = f32[24,8,128]{2,1,0:T(8,128)S(1)} collective-permute-done((f32[24,8,128]{2,1,0:T(8,128)S(1)}, f32[24,8,128]{2,1,0:T(8,128)S(1)}, u32[]{:S(2)}, u32[]{:S(2)}) %collective-permute-start.9) | collective-permute-done | bytes 98336 | tf_op jit(solution)/shard_map/ppermute | solution.py:497
  58.3 0.1 shard_map.62
  58.4 3.6 %collective-permute-start.10 = (f32[54,8,128]{2,1,0:T(8,128)S(1)}, f32[54,8,128]{2,1,0:T(8,128)S(1)}, u32[]{:S(2)}, u32[]{:S(2)}) collective-permute-start(f32[54,8,128]{2,1,0:T(8,128)S(1)} %get-tuple-element.38), channel_id=1, source_target_pairs={{0,1},{1,2},{2,3},{3,4},{4,5},{5,6},{6,7},{7,8},{8,9},{9,10},{10,1... | collective-permute-start | bytes 663560 | tf_op jit(solution)/shard_map/ppermute | solution.py:497
  62.0 3.6 %collective-permute-start.11 = (f32[54,8,128]{2,1,0:T(8,128)S(1)}, f32[54,8,128]{2,1,0:T(8,128)S(1)}, u32[]{:S(2)}, u32[]{:S(2)}) collective-permute-start(f32[54,8,128]{2,1,0:T(8,128)S(1)} %get-tuple-element.39), channel_id=1, source_target_pairs={{1,0},{2,1},{3,2},{4,3},{5,4},{6,5},{7,6},{8,7},{9,8},{10,9},{11,1... | collective-permute-start | bytes 663560 | tf_op jit(solution)/shard_map/ppermute | solution.py:497
  65.7 0.9 collective-permute-done.10.yl_ref
  66.6 0.8 collective-permute-done.11.yr_ref
  67.4 6.0 %shard_map.63 = (f32[16,16,256]{2,1,0:T(8,128)}, f32[8,128]{1,0:T(8,128)S(1)}) custom-call(f32[54,8,128]{2,1,0:T(8,128)S(1)} %collective-permute-done.10.yl_ref, f32[54,8,128]{2,1,0:T(8,128)S(1)} %collective-permute-done.11.yr_ref, f32[32,8,128]{2,1,0:T(8,128)S(1)} %get-tuple-element.40.o2_ref, f32[22,16,256]{2,1,0:T(8,128)S(1)} %get-tuple-element.41.u0_ref, ...), custom_call_target="tpu_custom_call" | custom-call | tf_op jit(solution)/shard_map/pallas_call | solution.py:483
  73.4 14.3 %all_to_all.12 = f32[16,1,128]{2,1,0:T(1,128)S(1)} all-to-all(f32[16,1,128]{2,1,0:T(1,128)S(1)} %broadcast_in_dim.6), channel_id=1, replica_groups=mesh['gx'=16,'gy'=32] {'gx'}, dimensions={0} | all-to-all | bytes 16384 | tf_op jit(solution)/shard_map/all_to_all | solution.py:503
  87.7 27.7 %all_to_all.13 = f32[32,1,128]{2,1,0:T(1,128)S(1)} all-to-all(f32[32,1,128]{2,1,0:T(1,128)S(1)} %broadcast_in_dim.7), channel_id=1, replica_groups=mesh['gx'=16,'gy'=32] {'gy'}, dimensions={0} | all-to-all | bytes 32768 | tf_op jit(solution)/shard_map/all_to_all | solution.py:503
  (10 shorter events, 0.1 us)
Async XLA Ops:
  0.6 1.0 copy-start
  1.6 11.2 %copy-start.3 = (f32[16,16,256]{2,1,0:T(8,128)S(1)}, f32[16,16,256]{2,1,0:T(8,128)}, u32[]{:S(2)}) copy-start(f32[16,16,256]{2,1,0:T(8,128)} %f_ref.3) | copy-start | bytes 786436
  2.5 10.3 %copy-start.1 = (f32[16,16,256]{2,1,0:T(8,128)S(1)}, f32[16,16,256]{2,1,0:T(8,128)}, u32[]{:S(2)}) copy-start(f32[16,16,256]{2,1,0:T(8,128)} %e_ref.3) | copy-start | bytes 786436
  2.5 10.3 %copy-start.2 = (f32[16,16,256]{2,1,0:T(8,128)S(1)}, f32[16,16,256]{2,1,0:T(8,128)}, u32[]{:S(2)}) copy-start(f32[16,16,256]{2,1,0:T(8,128)} %k_ref.3) | copy-start | bytes 786436
  2.6 6.4 %collective-permute-start = (f32[10,16,256]{2,1,0:T(8,128)S(1)}, f32[10,16,256]{2,1,0:T(8,128)S(1)}, u32[]{:S(2)}, u32[]{:S(2)}) collective-permute-start(f32[10,16,256]{2,1,0:T(8,128)S(1)} %pad_maximum_fusion), channel_id=1, source_target_pairs={{0,32},{32,64},{64,96},{96,128},{128,160},{160,192},{192,224},{224... | collective-permute-start | bytes 491528 | tf_op jit(solution)/shard_map/ppermute | solution.py:497
  6.8 6.1 %collective-permute-start.1 = (f32[10,16,256]{2,1,0:T(8,128)S(1)}, f32[10,16,256]{2,1,0:T(8,128)S(1)}, u32[]{:S(2)}, u32[]{:S(2)}) collective-permute-start(f32[10,16,256]{2,1,0:T(8,128)S(1)} %pad_maximum_fusion.1), channel_id=1, source_target_pairs={{32,0},{64,32},{96,64},{128,96},{160,128},{192,160},{224,192},{256... | collective-permute-start | bytes 491528 | tf_op jit(solution)/shard_map/ppermute | solution.py:497
  12.9 8.4 %collective-permute-start.2 = (f32[2,22,8,256]{3,2,1,0:T(8,128)S(1)}, f32[2,22,8,256]{3,2,1,0:T(8,128)S(1)}, u32[]{:S(2)}, u32[]{:S(2)}) collective-permute-start(f32[2,22,8,256]{3,2,1,0:T(8,128)S(1)} %get-tuple-element.31), channel_id=1, source_target_pairs={{0,1},{1,2},{2,3},{3,4},{4,5},{5,6},{6,7},{7,8},{8,9},{9,10},{10,1... | collective-permute-start | bytes 1081352 | tf_op jit(solution)/shard_map/ppermute | solution.py:497
  16.9 7.1 %collective-permute-start.3 = (f32[2,22,8,256]{3,2,1,0:T(8,128)S(1)}, f32[2,22,8,256]{3,2,1,0:T(8,128)S(1)}, u32[]{:S(2)}, u32[]{:S(2)}) collective-permute-start(f32[2,22,8,256]{3,2,1,0:T(8,128)S(1)} %get-tuple-element.32), channel_id=1, source_target_pairs={{1,0},{2,1},{3,2},{4,3},{5,4},{6,5},{7,6},{8,7},{9,8},{10,9},{11,1... | collective-permute-start | bytes 1081352 | tf_op jit(solution)/shard_map/ppermute | solution.py:497
  27.4 5.1 %collective-permute-start.4 = (f32[4,8,8,128]{3,2,1,0:T(8,128)S(1)}, f32[4,8,8,128]{3,2,1,0:T(8,128)S(1)}, u32[]{:S(2)}, u32[]{:S(2)}) collective-permute-start(f32[4,8,8,128]{3,2,1,0:T(8,128)S(1)} %get-tuple-element.33), channel_id=1, source_target_pairs={{0,32},{32,64},{64,96},{96,128},{128,160},{160,192},{192,224},{224... | collective-permute-start | bytes 393224 | tf_op jit(solution)/shard_map/ppermute | solution.py:497
  30.6 5.7 %collective-permute-start.5 = (f32[4,8,8,128]{3,2,1,0:T(8,128)S(1)}, f32[4,8,8,128]{3,2,1,0:T(8,128)S(1)}, u32[]{:S(2)}, u32[]{:S(2)}) collective-permute-start(f32[4,8,8,128]{3,2,1,0:T(8,128)S(1)} %get-tuple-element.33), channel_id=1, source_target_pairs={{32,0},{64,32},{96,64},{128,96},{160,128},{192,160},{224,192},{256... | collective-permute-start | bytes 393224 | tf_op jit(solution)/shard_map/ppermute | solution.py:497
  36.3 7.3 %collective-permute-start.7 = (f32[4,24,8,128]{3,2,1,0:T(8,128)S(1)}, f32[4,24,8,128]{3,2,1,0:T(8,128)S(1)}, u32[]{:S(2)}, u32[]{:S(2)}) collective-permute-start(f32[4,24,8,128]{3,2,1,0:T(8,128)S(1)} %constant_dynamic-update-slice_fusion.o_ref), channel_id=1, source_target_pairs={{1,0},{2,1},{3,2},{4,3},{5,4},{6,5},{7,6},{8,7},{9,8},{10,9},{11,1... | collective-permute-start | bytes 1179656 | tf_op jit(solution)/shard_map/ppermute | solution.py:497
  41.9 4.7 %collective-permute-start.6 = (f32[4,24,8,128]{3,2,1,0:T(8,128)S(1)}, f32[4,24,8,128]{3,2,1,0:T(8,128)S(1)}, u32[]{:S(2)}, u32[]{:S(2)}) collective-permute-start(f32[4,24,8,128]{3,2,1,0:T(8,128)S(1)} %constant_dynamic-update-slice_fusion.o_ref), channel_id=1, source_target_pairs={{0,1},{1,2},{2,3},{3,4},{4,5},{5,6},{6,7},{7,8},{8,9},{9,10},{10,1... | collective-permute-start | bytes 1179656 | tf_op jit(solution)/shard_map/ppermute | solution.py:497
  48.5 5.8 %collective-permute-start.8 = (f32[24,8,128]{2,1,0:T(8,128)S(1)}, f32[24,8,128]{2,1,0:T(8,128)S(1)}, u32[]{:S(2)}, u32[]{:S(2)}) collective-permute-start(f32[24,8,128]{2,1,0:T(8,128)S(1)} %get-tuple-element.35), channel_id=1, source_target_pairs={{0,32},{32,64},{64,96},{96,128},{128,160},{160,192},{192,224},{224... | collective-permute-start | bytes 294920 | tf_op jit(solution)/shard_map/ppermute | solution.py:497
  52.7 5.6 %collective-permute-start.9 = (f32[24,8,128]{2,1,0:T(8,128)S(1)}, f32[24,8,128]{2,1,0:T(8,128)S(1)}, u32[]{:S(2)}, u32[]{:S(2)}) collective-permute-start(f32[24,8,128]{2,1,0:T(8,128)S(1)} %get-tuple-element.36), channel_id=1, source_target_pairs={{32,0},{64,32},{96,64},{128,96},{160,128},{192,160},{224,192},{256... | collective-permute-start | bytes 294920 | tf_op jit(solution)/shard_map/ppermute | solution.py:497
  58.4 8.2 %collective-permute-start.10 = (f32[54,8,128]{2,1,0:T(8,128)S(1)}, f32[54,8,128]{2,1,0:T(8,128)S(1)}, u32[]{:S(2)}, u32[]{:S(2)}) collective-permute-start(f32[54,8,128]{2,1,0:T(8,128)S(1)} %get-tuple-element.38), channel_id=1, source_target_pairs={{0,1},{1,2},{2,3},{3,4},{4,5},{5,6},{6,7},{7,8},{8,9},{9,10},{10,1... | collective-permute-start | bytes 663560 | tf_op jit(solution)/shard_map/ppermute | solution.py:497
  62.0 5.4 %collective-permute-start.11 = (f32[54,8,128]{2,1,0:T(8,128)S(1)}, f32[54,8,128]{2,1,0:T(8,128)S(1)}, u32[]{:S(2)}, u32[]{:S(2)}) collective-permute-start(f32[54,8,128]{2,1,0:T(8,128)S(1)} %get-tuple-element.39), channel_id=1, source_target_pairs={{1,0},{2,1},{3,2},{4,3},{5,4},{6,5},{7,6},{8,7},{9,8},{10,9},{11,1... | collective-permute-start | bytes 663560 | tf_op jit(solution)/shard_map/ppermute | solution.py:497

commit v4 on v3

--- a/solution.py
+++ b/solution.py
@@ -12,6 +12,7 @@
 F32 = jnp.float32
 LANES = 128
 VMEM_LIMIT = 24 * 1024 * 1024
+AT_ONCE_0, AT_ONCE_1, AT_ONCE_2 = 1, 3, 7
 
 RIM_X0, RIM_Y0 = 3, 4
 RIM_1 = 8
@@ -81,7 +82,7 @@
     lax.fori_loop(first, last, loop_body, 0, unroll=last - first)
 
 
-def fill_weights(e_ref, weights, planes, scale, wrap_free):
+def fill_weights(e_ref, weights, planes, scale, wrap_free, first=0):
     wx, wy, wz, wb, total = weights
     half = 0.5 * scale
     shape = e_ref.shape[1:]
@@ -91,7 +92,7 @@
     def along_x(x):
         wx[x] = half * (e_ref[x] + e_ref[x + 1])
 
-    over_planes(0, planes - 1, along_x)
+    over_planes(first, planes - 1 - first, along_x)
 
     def others(x):
         e = e_ref[x]
@@ -108,18 +109,29 @@
         wz[x] = z
         total[x] = faces
 
-    over_planes(1, planes - 1, others)
-
-
-def flux_of(x, u_ref, weights):
+    over_planes(first + 1, planes - 1 - first, others)
+
+
+def planes_at(ref, x, count):
+    if count == 1:
+        return ref[x]
+    return ref[x : x + count].reshape(count * ref.shape[1], ref.shape[2])
+
+
+def runs(first, last, count):
+    return [(x, min(count, last - x)) for x in range(first, last, count)]
+
+
+def flux_of(x, u_ref, weights, count=1):
     wx, wy, wz, wb, _ = weights
-    u = u_ref[x]
-    py = wy[x] * (roll(u, -1, 0) - u)
-    pz = wz[x] * (roll(u, -1, 1) - u)
-    flux = wx[x - 1] * (u - u_ref[x - 1]) - wx[x] * (u_ref[x + 1] - u)
+    u = planes_at(u_ref, x, count)
+    py = planes_at(wy, x, count) * (roll(u, -1, 0) - u)
+    pz = planes_at(wz, x, count) * (roll(u, -1, 1) - u)
+    flux = planes_at(wx, x - 1, count) * (u - planes_at(u_ref, x - 1, count))
+    flux = flux - planes_at(wx, x, count) * (planes_at(u_ref, x + 1, count) - u)
     flux = flux + (roll(py, 1, 0) - py) + (roll(pz, 1, 1) - pz)
     if wb is not None:
-        flux = flux + wb[x] * u
+        flux = flux + planes_at(wb, x, count) * u
     return u, flux
 
 
@@ -127,23 +139,32 @@
     return jnp.exp(u - LN2), jnp.exp(-u - LN2)
 
 
-def sweep(u_ref, out_ref, weights, k_ref, f_ref, first, last, rows, origin, size):
-    def step(x):
-        u, flux = flux_of(x, u_ref, weights)
+def sweep(u_ref, out_ref, weights, k_ref, f_ref, first, last, rows, origin, size, at_once=1):
+    height = u_ref.shape[1]
+    for x, count in runs(first, last, at_once):
+        u, flux = flux_of(x, u_ref, weights, count)
         up, down = halves(u)
-        k = k_ref[x]
-        defect = f_ref[x] - (flux + k * (up - down))
-        slope = weights[4][x] + k * (up + down)
+        k = planes_at(k_ref, x, count)
+        defect = planes_at(f_ref, x, count) - (flux + k * (up - down))
+        slope = planes_at(weights[4], x, count) + k * (up + down)
         moved = u + OMEGA * defect / slope
-        out_ref[x] = jnp.where(rows > plane_bar(origin + x, size), moved, 0.0)
-
-    over_planes(first, last, step)
-
-
-def defect_at(x, u_ref, weights, k_ref, load):
-    u, flux = flux_of(x, u_ref, weights)
+        for i in range(count):
+            plane = moved[i * height : (i + 1) * height]
+            out_ref[x + i] = jnp.where(rows > plane_bar(origin + x + i, size), plane, 0.0)
+
+
+def defect_at(x, u_ref, weights, k_ref, load, count=1):
+    u, flux = flux_of(x, u_ref, weights, count)
     up, down = halves(u)
-    return load - (flux + k_ref[x] * (up - down))
+    return load - (flux + planes_at(k_ref, x, count) * (up - down))
+
+
+def defects(u_ref, weights, k_ref, f_ref, first, last, at_once):
+    height = u_ref.shape[1]
+    for x, count in runs(first, last, at_once):
+        d = defect_at(x, u_ref, weights, k_ref, planes_at(f_ref, x, count), count)
+        for i in range(count):
+            f_ref[x + i] = d[i * height : (i + 1) * height]
 
 
 def pair_rows(ref, base, count=8):
@@ -176,26 +197,55 @@
     return ref[x, 8 * tile : 8 * tile + 8, :]
 
 
-def pack_fine(s_ref, e_ref, k_ref, f_ref, xl_ref, xr_ref, up_ref, down_ref):
-    bricks = (s_ref, e_ref, k_ref, f_ref)
-    planes = s_ref.shape[0] + 2 * RIM_X0
-    shape = (8, s_ref.shape[2])
-    low = low_half(shape)
-    zero = jnp.zeros(shape, F32)
-    for x in range(planes):
+def pack_fine(bricks, planes, up_ref, down_ref):
+    low = low_half(up_ref.shape[2:])
+    for at, sources in enumerate(planes):
         for pair in range(2):
-            places = [fine_plane(x, 2 * pair + i, bricks[2 * pair + i], xl_ref, xr_ref) for i in range(2)]
-            if places[0] is None:
-                up_ref[pair, x] = zero
-                down_ref[pair, x] = zero
+            first, second = (place(bricks) for place in sources[2 * pair : 2 * pair + 2])
+            if first is None:
+                up_ref[pair, at] = jnp.zeros(up_ref.shape[2:], F32)
+                down_ref[pair, at] = jnp.zeros(up_ref.shape[2:], F32)
                 continue
-            up_ref[pair, x] = jnp.where(low, roll(tile_of(places[0], 1), 4, 0), tile_of(places[1], 1))
-            down_ref[pair, x] = jnp.where(low, tile_of(places[0], 0), roll(tile_of(places[1], 0), 4, 0))
+            up_ref[pair, at] = jnp.where(low, roll(tile_of(first, 1), 4, 0), tile_of(second, 1))
+            down_ref[pair, at] = jnp.where(low, tile_of(first, 0), roll(tile_of(second, 0), 4, 0))
+
+
+def pack_fine_own(s_ref, e_ref, k_ref, f_ref, up_ref, down_ref):
+    planes = [
+        [functools.partial(lambda refs, i, x: (refs[i], x), i=i, x=x) for i in range(4)]
+        for x in range(s_ref.shape[0])
+    ]
+    pack_fine((s_ref, e_ref, k_ref, f_ref), planes, up_ref, down_ref)
+
+
+def rim_planes(own):
+    return list(range(RIM_X0)) + list(range(RIM_X0 + own, RIM_X0 + own + RIM_X0))
+
+
+def pack_fine_rim(xl_ref, xr_ref, up_ref, down_ref):
+    own = xl_ref.shape[1]
+    brick = jax.ShapeDtypeStruct((own,), F32)
+    planes = [
+        [functools.partial(lambda refs, i, x: fine_plane(x, i, brick, *refs), i=i, x=x) for i in range(4)]
+        for x in rim_planes(own)
+    ]
+    pack_fine((xl_ref, xr_ref), planes, up_ref, down_ref)
+
+
+def hand_on(in_ref, out_ref):
+    out_ref[...] = in_ref[...]
+
+
+def join_rims(xl_ref, xr_ref, yl_ref, yr_ref, rim_ref):
+    del yl_ref, yr_ref
+    planes = xl_ref.shape[1]
+    rim_ref[:, :planes] = xl_ref[...]
+    rim_ref[:, planes:] = xr_ref[...]
 
 
 def fine_first(
-    s_ref, e_ref, k_ref, f_ref, xl_ref, xr_ref, yl_ref, yr_ref,
-    stack_ref, u0_ref, kw_ref, fw_ref, wx, wy, wz, wb, total,
+    s_ref, e_ref, k_ref, f_ref, xl_ref, xr_ref, yl_ref, yr_ref, cl_ref, cr_ref,
+    up_ref, down_ref, stack_ref, u0_ref, kw_ref, fw_ref, wx, wy, wz, wb, total,
     ua, ub, ew_ref, gather, summed,
     *, size_x, size_y,
 ):
@@ -205,14 +255,19 @@
     planes = own_x + 2 * RIM_X0
     rows = own_y + 2 * RIM_Y0
     keep_left, keep_right = inner_sides((8, nz))
+    corners = rim_planes(own_x)
     for x in range(planes):
+        if x in corners:
+            l_ref, r_ref, at = cl_ref, cr_ref, corners.index(x)
+        else:
+            l_ref, r_ref, at = yl_ref, yr_ref, x - RIM_X0
         for index in range(4):
             place = fine_plane(x, index, bricks[index], xl_ref, xr_ref)
             if place is None:
                 windows[index][x] = jnp.zeros((rows, nz), F32)
                 continue
-            left = jnp.where(keep_left, yl_ref[index // 2, x], 0.0)
-            right = jnp.where(keep_right, yr_ref[index // 2, x], 0.0)
+            left = jnp.where(keep_left, l_ref[index // 2, at], 0.0)
+            right = jnp.where(keep_right, r_ref[index // 2, at], 0.0)
             if index % 2 == 0:
                 right = roll(right, 4, 0)
             else:
@@ -226,9 +281,9 @@
     origin_y = lax.axis_index("gy") * own_y - RIM_Y0
     shape = (rows, nz)
     mask = row_mask(shape, 2, rows - 2, origin_y, size_y)
-    sweep(ua, ub, weights, kw_ref, fw_ref, 1, planes - 1, mask, origin_x, size_x)
+    sweep(ua, ub, weights, kw_ref, fw_ref, 1, planes - 1, mask, origin_x, size_x, AT_ONCE_0)
     mask = row_mask(shape, 3, rows - 3, origin_y, size_y)
-    sweep(ub, ua, weights, kw_ref, fw_ref, 2, planes - 2, mask, origin_x, size_x)
+    sweep(ub, ua, weights, kw_ref, fw_ref, 2, planes - 2, mask, origin_x, size_x, AT_ONCE_0)
 
     low = low_half((8, nz))
     pairs = own_x // 2
@@ -252,47 +307,56 @@
             gather[at : at + own_y, :] = ref[2 * j] + ref[2 * j + 1]
     summed[...] = dot(gather[...], shared_matrix(nz, nz // 2, 2, 1, 0.125))
     for j in range(pairs):
-        stack_ref[0, j] = pair_rows(summed, base + j * own_y)
-        stack_ref[1, j] = pair_rows(summed, base + (pairs + j) * own_y)
-        stack_ref[2, j] = pair_rows(summed, j * rows + RIM_Y0)
-        stack_ref[3, j] = pair_rows(summed, (pairs + j) * rows + RIM_Y0)
+        tiles = (
+            pair_rows(summed, base + j * own_y),
+            pair_rows(summed, base + (pairs + j) * own_y),
+            pair_rows(summed, j * rows + RIM_Y0),
+            pair_rows(summed, (pairs + j) * rows + RIM_Y0),
+        )
+        for index, tile in enumerate(tiles):
+            stack_ref[index, j] = tile
+            if j > 0:
+                up_ref[index, j - 1] = tile
+            if j < pairs - 1:
+                down_ref[index, j] = tile
 
 
 def middle_first(
-    l_ref, o_ref, r_ref, u0_ref,
-    up_ref, down_ref, stack_ref, w_ref, f_ref, k, v, wx, wy, wz, wb, total,
+    o_ref, xl_ref, xr_ref, yl_ref, yr_ref, cl_ref, cr_ref, u0_ref,
+    up_ref, down_ref, y_up_ref, y_down_ref, stack_ref, w_ref, f_ref, k, v, wx, wy, wz, wb, total,
     e, wa, gather, summed,
     *, size_x, size_y,
 ):
-    planes, own, nz = o_ref.shape[1:]
+    own, nz = o_ref.shape[2:]
+    planes = own + 2 * RIM_1
     rows = own + 2 * RIM_1
     shape = (rows, nz)
     keep_left, keep_right = inner_sides((own, nz))
-
-    def joined(index, x):
-        left = jnp.where(keep_left, l_ref[index, x], 0.0)
-        right = jnp.where(keep_right, r_ref[index, x], 0.0)
-        return jnp.concatenate([left, o_ref[index, x], right], axis=0)
-
-    def assemble(x):
-        e[x] = joined(0, x)
-        k[x] = joined(1, x)
-        v[x] = joined(2, x)
-
-    over_planes(0, planes, assemble)
+    sent = RIM_1 - 1
+
+    def assemble(x, middle, left, right, at, side):
+        for index, ref in enumerate((e, k, v, f_ref)):
+            lower = jnp.where(keep_left, left[index, side], 0.0)
+            upper = jnp.where(keep_right, right[index, side], 0.0)
+            ref[x] = jnp.concatenate([lower, middle[index, at], upper], axis=0)
+
+    for x in range(1, planes - 1):
+        if x < RIM_1:
+            assemble(x, xl_ref, cl_ref, cr_ref, x - 1, x - 1)
+        elif x < RIM_1 + own:
+            assemble(x, o_ref, yl_ref, yr_ref, x - RIM_1, x - RIM_1)
+        else:
+            assemble(x, xr_ref, cl_ref, cr_ref, x - RIM_1 - own, sent + x - RIM_1 - own)
     weights = (wx, wy, wz, wb, total)
-    fill_weights(e, weights, planes, 0.25, False)
+    fill_weights(e, weights, planes, 0.25, False, 1)
     origin_x = lax.axis_index("gx") * own - RIM_1
     origin_y = lax.axis_index("gy") * own - RIM_1
 
-    def load(x):
-        f_ref[x] = defect_at(x, v, weights, k, joined(3, x))
-
-    over_planes(2, planes - 2, load)
+    defects(v, weights, k, f_ref, 2, planes - 2, AT_ONCE_1)
     mask = row_mask(shape, 2, rows - 2, origin_y, size_y)
-    sweep(v, wa, weights, k, f_ref, 2, planes - 2, mask, origin_x, size_x)
+    sweep(v, wa, weights, k, f_ref, 2, planes - 2, mask, origin_x, size_x, AT_ONCE_1)
     mask = row_mask(shape, 3, rows - 3, origin_y, size_y)
-    sweep(wa, w_ref, weights, k, f_ref, 3, planes - 3, mask, origin_x, size_x)
+    sweep(wa, w_ref, weights, k, f_ref, 3, planes - 3, mask, origin_x, size_x, AT_ONCE_1)
     pairs = (planes - 8) // 2
 
     def finish(j):
@@ -307,7 +371,6 @@
 
     over_planes(0, pairs, finish)
     summed[...] = dot(gather[...], shared_matrix(2 * nz, nz, 2, 1, 0.125))
-    own_planes = u0_ref.shape[0]
     for a in range(2):
         for j in range(pairs):
             tile = pair_rows(summed, (a * pairs + j) * rows + 4)
@@ -316,51 +379,47 @@
                 up_ref[a * RIM_2 + j] = tile
             if j >= pairs - RIM_2:
                 down_ref[a * RIM_2 + j - (pairs - RIM_2)] = tile
-    for x in range(RIM_X0):
+    for a in range(2):
+        for x in range(4):
+            tile = stack_ref[a, pairs // 2 - 2 + x]
+            y_up_ref[4 * a + x] = tile
+            y_down_ref[4 * a + x] = tile
+    own_planes = u0_ref.shape[0]
+    for x in range(own_planes):
+        tiles = quarter_tiles(u0_ref, x)
+        y_up_ref[8 + x], y_down_ref[8 + x] = pack_rows(tiles)
         for t in range(4):
-            rows_at, lanes_at = 8 * (t // 2), LANES * (t % 2)
-            at = 2 * RIM_2 + 4 * x + t
-            up_ref[at] = u0_ref[own_planes - RIM_X0 + x, rows_at : rows_at + 8, lanes_at : lanes_at + LANES]
-            down_ref[at] = u0_ref[x, rows_at : rows_at + 8, lanes_at : lanes_at + LANES]
-
-
-def pack_coarse(xl_ref, xr_ref, stack_ref, u0_ref, up_ref, down_ref, own_ref, rim_ref):
-    spare = stack_ref.shape[1] // 2 - 2
-    planes = 2 * RIM_2 + 4
-    low = low_half((8, LANES))
+            if x < RIM_X0:
+                down_ref[2 * RIM_2 + 4 * x + t] = tiles[t]
+            if x >= own_planes - RIM_X0:
+                up_ref[2 * RIM_2 + 4 * (x - own_planes + RIM_X0) + t] = tiles[t]
+
+
+def quarter_tiles(ref, x):
+    return [ref[x, 8 * (t // 2) : 8 * (t // 2) + 8, LANES * (t % 2) : LANES * (t % 2) + LANES] for t in range(4)]
+
+
+def pack_rows(tiles):
+    low = low_half(tiles[0].shape)
+    last = jnp.where(low, roll(tiles[2], 4, 0), tiles[3])
+    return last, jnp.where(low, tiles[0], roll(tiles[1], 4, 0))
+
+
+def pack_coarse(xl_ref, xr_ref, yl_ref, yr_ref, up_ref, down_ref):
+    del yl_ref, yr_ref
     for a in range(2):
-        for x in range(planes):
-            if x < RIM_2:
-                tile = xl_ref[a * RIM_2 + x]
-            elif x < RIM_2 + 4:
-                tile = stack_ref[a, x - RIM_2 + spare]
-            else:
-                tile = xr_ref[a * RIM_2 + x - RIM_2 - 4]
-            at = a * planes + x
-            own_ref[at] = tile
-            up_ref[at] = tile
-            down_ref[at] = tile
-    own_planes = u0_ref.shape[0]
-    base = 2 * RIM_2
-    for x in range(own_planes + 2 * RIM_X0):
-        if x < RIM_X0:
-            tiles = [xl_ref[base + 4 * x + t] for t in range(4)]
-        elif x < RIM_X0 + own_planes:
-            tiles = [
-                u0_ref[x - RIM_X0, 8 * (t // 2) : 8 * (t // 2) + 8, LANES * (t % 2) : LANES * (t % 2) + LANES]
-                for t in range(4)
-            ]
-        else:
-            tiles = [xr_ref[base + 4 * (x - RIM_X0 - own_planes) + t] for t in range(4)]
-        at = 2 * planes + x
-        up_ref[at] = jnp.where(low, roll(tiles[2], 4, 0), tiles[3])
-        down_ref[at] = jnp.where(low, tiles[0], roll(tiles[1], 4, 0))
-        for t in range(4):
-            rim_ref[x, 8 * (t // 2) : 8 * (t // 2) + 8, LANES * (t % 2) : LANES * (t % 2) + LANES] = tiles[t]
+        for x in range(2 * RIM_2):
+            tile = xl_ref[a * RIM_2 + x] if x < RIM_2 else xr_ref[a * RIM_2 + x - RIM_2]
+            up_ref[2 * RIM_2 * a + x] = tile
+            down_ref[2 * RIM_2 * a + x] = tile
+    for x in range(2 * RIM_X0):
+        ref, at = (xl_ref, x) if x < RIM_X0 else (xr_ref, x - RIM_X0)
+        tiles = [ref[2 * RIM_2 + 4 * at + t] for t in range(4)]
+        up_ref[4 * RIM_2 + x], down_ref[4 * RIM_2 + x] = pack_rows(tiles)
 
 
 def coarse_and_last(
-    yl_ref, yr_ref, o2_ref, u0_ref,
+    xl_ref, xr_ref, yl_ref, yr_ref, cl_ref, cr_ref, o2_ref, u0_ref,
     w1_ref, f1_ref, k1, v1_ref, wx1, wy1, wz1, wb1, t1,
     kw_ref, fw_ref, wx0, wy0, wz0, wb0, t0,
     out_ref, part_ref,
@@ -377,35 +436,43 @@
     inside = iota(shape2, 1) < nz2
     keep_left, keep_right = inner_sides((8, LANES))
 
-    def window2(at):
-        own = roll(o2_ref[at], 4, 0)
-        upper = jnp.where(row8 >= 6, own, jnp.where(keep_left, yl_ref[at], 0.0))
-        lower = jnp.where(row8 < 2, own, jnp.where(keep_right, yr_ref[at], 0.0))
+    spare = o2_ref.shape[1] // 2 - 2
+
+    def window2(a, x):
+        if x < RIM_2:
+            own, at = xl_ref[a * RIM_2 + x], 2 * RIM_2 * a + x
+            left, right = cl_ref[at], cr_ref[at]
+        elif x < RIM_2 + 4:
+            own, at = o2_ref[a, spare + x - RIM_2], 4 * a + x - RIM_2
+            left, right = yl_ref[at], yr_ref[at]
+        else:
+            own, at = xr_ref[a * RIM_2 + x - RIM_2 - 4], 2 * RIM_2 * a + x - 4
+            left, right = cl_ref[at], cr_ref[at]
+        own = roll(own, 4, 0)
+        upper = jnp.where(row8 >= 6, own, jnp.where(keep_left, left, 0.0))
+        lower = jnp.where(row8 < 2, own, jnp.where(keep_right, right, 0.0))
         return jnp.concatenate([upper, lower], axis=0)
 
-    def assemble2(x):
-        both = window2(x)
+    for x in range(planes2):
+        both = window2(0, x)
         e2[x] = jnp.where(inside, both, 0.0)
         k2[x] = jnp.where(inside, roll(both, nz2, 1), 0.0)
-        both = window2(planes2 + x)
+        both = window2(1, x)
         v2[x] = jnp.where(inside, both, 0.0)
         f2[x] = jnp.where(inside, roll(both, nz2, 1), 0.0)
 
-    over_planes(0, planes2, assemble2)
     weights2 = (wx2, wy2, wz2, None, t2)
     fill_weights(e2, weights2, planes2, 0.0625, True)
     origin_x = place_x * 4 - RIM_2
     origin_y = place_y * 4 - RIM_2
 
-    def load2(x):
-        f2[x] = defect_at(x, v2, weights2, k2, f2[x])
-
-    over_planes(1, planes2 - 1, load2)
+    defects(v2, weights2, k2, f2, 1, planes2 - 1, AT_ONCE_2)
     source = v2
     for i in range(4):
         target = a2 if i % 2 == 0 else b2
         mask = row_mask(shape2, 1 + i, rows2 - 1 - i, origin_y, size_y // 4, nz2)
-        sweep(source, target, weights2, k2, f2, 1 + i, planes2 - 1 - i, mask, origin_x, size_x // 4)
+        last = planes2 - 1 - i
+        sweep(source, target, weights2, k2, f2, 1 + i, last, mask, origin_x, size_x // 4, AT_ONCE_2)
         source = target
     for j in range(8):
         q2[16 * j : 16 * j + 16, :] = source[4 + j] - v2[4 + j]
@@ -426,9 +493,9 @@
         at = rows1 * ((x - 4) // 2)
         a1[x] = w1_ref[x] + d2[at : at + rows1, :]
     mask = row_mask(shape1, 5, rows1 - 5, origin_y, size_y // 2)
-    sweep(a1, b1, weights1, k1, f1_ref, 5, planes1 - 5, mask, origin_x, size_x // 2)
+    sweep(a1, b1, weights1, k1, f1_ref, 5, planes1 - 5, mask, origin_x, size_x // 2, AT_ONCE_1)
     mask = row_mask(shape1, 6, rows1 - 6, origin_y, size_y // 2)
-    sweep(b1, a1, weights1, k1, f1_ref, 6, planes1 - 6, mask, origin_x, size_x // 2)
+    sweep(b1, a1, weights1, k1, f1_ref, 6, planes1 - 6, mask, origin_x, size_x // 2, AT_ONCE_1)
     for j in range(12):
         rows = roll(a1[6 + j] - v1_ref[6 + j], -6, 0)[:16]
         d1[pl.ds(32 * j, 16, 2), :] = rows
@@ -440,13 +507,23 @@
     planes0 = own_x + 2 * RIM_X0
     rows0 = own_y + 2 * RIM_Y0
     shape0 = (rows0, nz0)
-    base = 2 * planes2
+    corners = rim_planes(own_x)
     for x in range(planes0):
-        left = jnp.where(keep_left, yl_ref[base + x], 0.0)
-        right = jnp.where(keep_right, yr_ref[base + x], 0.0)
+        if x in corners:
+            at = corners.index(x)
+            ref, first = (xl_ref, at) if x < RIM_X0 else (xr_ref, at - RIM_X0)
+            tiles = [ref[2 * RIM_2 + 4 * first + t] for t in range(4)]
+            left, right = cl_ref[4 * RIM_2 + at], cr_ref[4 * RIM_2 + at]
+        else:
+            tiles = quarter_tiles(u0_ref, x - RIM_X0)
+            left, right = yl_ref[8 + x - RIM_X0], yr_ref[8 + x - RIM_X0]
+        upper = jnp.concatenate(tiles[:2], axis=1)
+        lower = jnp.concatenate(tiles[2:], axis=1)
+        left = jnp.where(keep_left, left, 0.0)
+        right = jnp.where(keep_right, right, 0.0)
         left = jnp.concatenate([left, roll(left, 4, 0)], axis=1)
         right = jnp.concatenate([roll(right, 4, 0), right], axis=1)
-        tiles = shifted_tiles(u0_ref[x, 0:8, :], u0_ref[x, 8:16, :], left, right)
+        tiles = shifted_tiles(upper, lower, left, right)
         at = 32 * ((x + 1) // 2)
         for i, tile in enumerate(tiles):
             a0[x, 8 * i : 8 * i + 8, :] = tile + q0[at + 8 * i : at + 8 * i + 8, :]
@@ -454,9 +531,9 @@
     origin_x = place_x * own_x - RIM_X0
     origin_y = place_y * own_y - RIM_Y0
     mask = row_mask(shape0, 2, rows0 - 2, origin_y, size_y)
-    sweep(a0, b0, weights0, kw_ref, fw_ref, 1, planes0 - 1, mask, origin_x, size_x)
+    sweep(a0, b0, weights0, kw_ref, fw_ref, 1, planes0 - 1, mask, origin_x, size_x, AT_ONCE_0)
     mask = row_mask(shape0, 3, rows0 - 3, origin_y, size_y)
-    sweep(b0, a0, weights0, kw_ref, fw_ref, 2, planes0 - 2, mask, origin_x, size_x)
+    sweep(b0, a0, weights0, kw_ref, fw_ref, 2, planes0 - 2, mask, origin_x, size_x, AT_ONCE_0)
     low = low_half((8, nz0))
 
     def finish(x, acc):
@@ -514,47 +591,46 @@
     upward = jnp.concatenate([a[own_x - d :] for a, d in zip(fields, depths)], axis=0)
     downward = jnp.concatenate([a[:d] for a, d in zip(fields, depths)], axis=0)
     xl, xr = swap(upward, downward, "gx")
-    packed = arr(2, planes0, 8, nz)
-    upward, downward = call(pack_fine, [packed, packed], [], *fields, xl, xr)
-    yl, yr = swap(upward, downward, "gy", True)
+    yl, yr = swap(*call(pack_fine_own, [arr(2, own_x, 8, nz)] * 2, [], *fields), "gy", True)
+    cl, cr = swap(*call(pack_fine_rim, [arr(2, 2 * RIM_X0, 8, nz)] * 2, [], xl, xr), "gy", True)
     own1, own1_y, nz1 = own_x // 2, own_y // 2, nz // 2
     gathered = 2 * own1 * rows0 + 2 * own1 * own_y
-    stack1, u0, *level0 = call(
+    upward, downward, stack1, u0, *level0 = call(
         functools.partial(fine_first, size_x=size_x, size_y=size_y),
-        [arr(4, own1, own1_y, nz1), arr(own_x, own_y, nz)] + [arr(*window0)] * 7,
+        [arr(4, own1 - 1, own1_y, nz1)] * 2 + [arr(4, own1, own1_y, nz1)]
+        + [arr(own_x, own_y, nz)] + [arr(*window0)] * 7,
         [window0] * 3 + [(gathered, nz), (gathered, nz1)],
-        *fields, xl, xr, yl, yr,
+        *fields, xl, xr, yl, yr, cl, cr,
     )
 
-    xl, xr = swap(stack1, stack1, "gx")
-    own = jnp.concatenate([xl, stack1, xr], axis=1)
-    yl1, yr1 = swap(own, own, "gy", True)
+    xl, xr = swap(upward, downward, "gx")
+    (stack1,) = call(hand_on, [stack1], [], stack1)
+    yl, yr = swap(stack1, stack1, "gy", True)
+    (rim,) = call(join_rims, [arr(4, 2 * (own1 - 1), own1_y, nz1)], [], xl, xr, yl, yr)
+    cl, cr = swap(rim, rim, "gy", True)
     planes1 = own1 + 2 * RIM_1
     window1 = (planes1, own1_y + 2 * RIM_1, nz1)
     sent_x = 2 * RIM_2 + 4 * RIM_X0
-    upward, downward, stack2, *level1 = call(
+    sent_y = 8 + own_x
+    upward, downward, y_upward, y_downward, stack2, *level1 = call(
         functools.partial(middle_first, size_x=size_x // 2, size_y=size_y // 2),
-        [arr(sent_x, 8, LANES)] * 2 + [arr(2, 8, 8, LANES)] + [arr(*window1)] * 9,
+        [arr(sent_x, 8, LANES)] * 2 + [arr(sent_y, 8, LANES)] * 2 + [arr(2, 8, 8, LANES)] + [arr(*window1)] * 9,
         [window1] * 2 + [(16 * window1[1], 2 * nz1), (16 * window1[1], nz1)],
-        yl1, own, yr1, u0,
+        stack1, xl, xr, yl, yr, cl, cr, u0,
     )
 
     xl, xr = swap(upward, downward, "gx")
+    yl, yr = swap(y_upward, y_downward, "gy", True)
+    rim = arr(4 * RIM_2 + 2 * RIM_X0, 8, LANES)
+    cl, cr = swap(*call(pack_coarse, [rim, rim], [], xl, xr, yl, yr), "gy", True)
     planes2 = 2 * RIM_2 + 4
-    sent_y = 2 * planes2 + planes0
-    upward, downward, own2, rim0 = call(
-        pack_coarse,
-        [arr(sent_y, 8, LANES)] * 2 + [arr(2 * planes2, 8, LANES), arr(planes0, own_y, nz)],
-        [], xl, xr, stack2, u0,
-    )
-    yl, yr = swap(upward, downward, "gy", True)
     window2 = (planes2, planes2, LANES)
     relaxed, part = call(
         functools.partial(coarse_and_last, size_x=size_x, size_y=size_y),
         [arr(own_x, own_y, nz), arr(8, LANES)],
         [window2] * 10 + [(LANES, LANES)] * 2 + [(8 * window1[1], LANES)]
         + [window1] * 2 + [(12 * 32, nz1)] + [window0] * 2 + [(12 * 32, nz)],
-        yl, yr, own2, rim0, *level1, *level0,
+        xl, xr, yl, yr, cl, cr, stack2, u0, *level1, *level0,
     )
     total = sum_over(sum_over(part[:1], "gx"), "gy")[0, 0]
     return relaxed, jnp.sqrt(total / (size_x * size_y * nz))

time: 117 us -> 114 us (0.974)
  waiting for transfers between devices: 25.7 us -> 13.5 us
  starting transfers between devices: 33.7 us -> 44 us
    ppermute x12 -> x18, waiting for transfers between devices: 25.7 us -> 13.5 us  [swap(): return (lax.ppermute(upward, axis, up), lax.ppermute(downward, axis, down))]
    ppermute x12 -> x18, starting transfers between devices: 33.7 us -> 44 us  [swap(): return (lax.ppermute(upward, axis, up), lax.ppermute(downward, axis, down))]
    pallas_call x5 -> x8, Pallas kernels: 11.3 us -> 10.2 us  [call(): pl.pallas_call(kernel, out_shape=outs, in_specs=[pl.BlockSpec(memory_spac...]
  transfers between devices with their start and end apart: 12 -> 18, of which waited for: 12 -> 11; matrix products, arithmetic and copies ran while one was open for 0% -> 0% of each run, Pallas kernels for 0% -> 0%
where the time goes in v4:
time: 114 us; the launch traced here: 113 us
  starting transfers between devices  44 us (39%)
  blocking collectives  41.5 us (36%)
  waiting for transfers between devices  13.5 us (12%)
  Pallas kernels  10.2 us (9%)
  between operations  2.02 us (2%)
  local copies, waits for them, and re-layouts  1.92 us (2%)
    ppermute x18, starting transfers between devices, swap(): return (lax.ppermute(upward, axis, up), lax.ppermute(downward, axis, down))  44 us
    all_to_all x2, blocking collectives, sum_over(): lax.all_to_all(rows, axis, 0, 0, tiled=True)  41.5 us
    ppermute x18, waiting for transfers between devices, swap(): return (lax.ppermute(upward, axis, up), lax.ppermute(downward, axis, down))  13.5 us
    pallas_call x8, Pallas kernels, call(): pl.pallas_call(kernel, out_shape=outs, in_specs=[pl.BlockSpec(memory_spac...  10.2 us
  transfers between devices with their start and end apart: 18, of which 11 were waited for; matrix products, arithmetic and copies ran while one was open for 0% of the time, Pallas kernels for 0%

profile of v4, /device:TPU:1, one launch (start us, length us, event | category | flops | bytes accessed | tf_op | source)
XLA Modules:
  0.0 113.2 jit_solution(3547401827181655314)
XLA Ops:
  0.6 0.0 copy-start
  0.6 0.9 fusion.2
  1.5 0.1 copy-done
  1.6 0.0 copy-start.3
  1.6 0.9 fusion
  2.5 0.0 copy-start.1
  2.5 0.0 copy-start.2
  2.6 4.2 %collective-permute-start = (f32[10,16,256]{2,1,0:T(8,128)S(1)}, f32[10,16,256]{2,1,0:T(8,128)S(1)}, u32[]{:S(2)}, u32[]{:S(2)}) collective-permute-start(f32[10,16,256]{2,1,0:T(8,128)S(1)} %pad_maximum_fusion), channel_id=1, source_target_pairs={{0,32},{32,64},{64,96},{96,128},{128,160},{160,192},{192,224},{224... | collective-permute-start | bytes 491528 | tf_op jit(solution)/shard_map/ppermute | solution.py:574
  6.8 1.3 %collective-permute-start.1 = (f32[10,16,256]{2,1,0:T(8,128)S(1)}, f32[10,16,256]{2,1,0:T(8,128)S(1)}, u32[]{:S(2)}, u32[]{:S(2)}) collective-permute-start(f32[10,16,256]{2,1,0:T(8,128)S(1)} %pad_maximum_fusion.1), channel_id=1, source_target_pairs={{32,0},{64,32},{96,64},{128,96},{160,128},{192,160},{224,192},{256... | collective-permute-start | bytes 491528 | tf_op jit(solution)/shard_map/ppermute | solution.py:574
  8.1 0.0 copy-done.3
  8.1 0.0 copy-done.1
  8.1 0.0 copy-done.2
  8.1 0.1 shard_map.59
  8.2 2.5 %collective-permute-start.2 = (f32[2,16,8,256]{3,2,1,0:T(8,128)S(1)}, f32[2,16,8,256]{3,2,1,0:T(8,128)S(1)}, u32[]{:S(2)}, u32[]{:S(2)}) collective-permute-start(f32[2,16,8,256]{3,2,1,0:T(8,128)S(1)} %get-tuple-element.35), channel_id=1, source_target_pairs={{0,1},{1,2},{2,3},{3,4},{4,5},{5,6},{6,7},{7,8},{8,9},{9,10},{10,1... | collective-permute-start | bytes 786440 | tf_op jit(solution)/shard_map/ppermute | solution.py:574
  10.7 1.7 %collective-permute-start.3 = (f32[2,16,8,256]{3,2,1,0:T(8,128)S(1)}, f32[2,16,8,256]{3,2,1,0:T(8,128)S(1)}, u32[]{:S(2)}, u32[]{:S(2)}) collective-permute-start(f32[2,16,8,256]{3,2,1,0:T(8,128)S(1)} %get-tuple-element.36), channel_id=1, source_target_pairs={{1,0},{2,1},{3,2},{4,3},{5,4},{6,5},{7,6},{8,7},{9,8},{10,9},{11,1... | collective-permute-start | bytes 786440 | tf_op jit(solution)/shard_map/ppermute | solution.py:574
  12.3 0.0 collective-permute-done.xl_ref
  12.4 0.5 collective-permute-done.1.xr_ref
  12.9 4.0 %collective-permute-start.4 = (f32[2,6,8,256]{3,2,1,0:T(8,128)S(1)}, f32[2,6,8,256]{3,2,1,0:T(8,128)S(1)}, u32[]{:S(2)}, u32[]{:S(2)}) collective-permute-start(f32[2,6,8,256]{3,2,1,0:T(8,128)S(1)} %get-tuple-element.37), channel_id=1, source_target_pairs={{0,1},{1,2},{2,3},{3,4},{4,5},{5,6},{6,7},{7,8},{8,9},{9,10},{10,1... | collective-permute-start | bytes 294920 | tf_op jit(solution)/shard_map/ppermute | solution.py:574
  16.8 1.3 %collective-permute-start.5 = (f32[2,6,8,256]{3,2,1,0:T(8,128)S(1)}, f32[2,6,8,256]{3,2,1,0:T(8,128)S(1)}, u32[]{:S(2)}, u32[]{:S(2)}) collective-permute-start(f32[2,6,8,256]{3,2,1,0:T(8,128)S(1)} %get-tuple-element.38), channel_id=1, source_target_pairs={{1,0},{2,1},{3,2},{4,3},{5,4},{6,5},{7,6},{8,7},{9,8},{10,9},{11,1... | collective-permute-start | bytes 294920 | tf_op jit(solution)/shard_map/ppermute | solution.py:574
  18.2 0.8 collective-permute-done.4.cl_ref
  19.0 2.2 %collective-permute-done.5.cr_ref = f32[2,6,8,256]{3,2,1,0:T(8,128)S(1)} collective-permute-done((f32[2,6,8,256]{3,2,1,0:T(8,128)S(1)}, f32[2,6,8,256]{3,2,1,0:T(8,128)S(1)}, u32[]{:S(2)}, u32[]{:S(2)}) %collective-permute-start.5) | collective-permute-done | bytes 98336 | tf_op jit(solution)/shard_map/ppermute | solution.py:574
  21.2 0.0 collective-permute-done.2.yl_ref
  21.2 0.0 collective-permute-done.3.yr_ref
  21.2 3.3 %shard_map.61 = (f32[4,7,8,128]{3,2,1,0:T(8,128)S(1)}, f32[4,7,8,128]{3,2,1,0:T(8,128)S(1)}, f32[4,8,8,128]{3,2,1,0:T(8,128)S(1)}, f32[16,16,256]{2,1,0:T(8,128)...) custom-call(f32[16,16,256]{2,1,0:T(8,128)S(1)} %copy-done, ...), custom_call_target="tpu_custom_call" | custom-call | tf_op jit(solution)/shard_map/pallas_call | solution.py:560
  24.5 4.2 %collective-permute-start.9 = (f32[4,8,8,128]{3,2,1,0:T(8,128)S(1)}, f32[4,8,8,128]{3,2,1,0:T(8,128)S(1)}, u32[]{:S(2)}, u32[]{:S(2)}) collective-permute-start(f32[4,8,8,128]{3,2,1,0:T(8,128)S(1)} %shard_map.62.o_ref), channel_id=1, source_target_pairs={{1,0},{2,1},{3,2},{4,3},{5,4},{6,5},{7,6},{8,7},{9,8},{10,9},{11,1... | collective-permute-start | bytes 393224 | tf_op jit(solution)/shard_map/ppermute | solution.py:574
  28.7 0.0 collective-permute-start.8
  28.7 3.2 %collective-permute-start.6 = (f32[4,7,8,128]{3,2,1,0:T(8,128)S(1)}, f32[4,7,8,128]{3,2,1,0:T(8,128)S(1)}, u32[]{:S(2)}, u32[]{:S(2)}) collective-permute-start(f32[4,7,8,128]{3,2,1,0:T(8,128)S(1)} %get-tuple-element.40), channel_id=1, source_target_pairs={{0,32},{32,64},{64,96},{96,128},{128,160},{160,192},{192,224},{224... | collective-permute-start | bytes 344072 | tf_op jit(solution)/shard_map/ppermute | solution.py:574
  31.9 1.3 %collective-permute-start.7 = (f32[4,7,8,128]{3,2,1,0:T(8,128)S(1)}, f32[4,7,8,128]{3,2,1,0:T(8,128)S(1)}, u32[]{:S(2)}, u32[]{:S(2)}) collective-permute-start(f32[4,7,8,128]{3,2,1,0:T(8,128)S(1)} %get-tuple-element.41), channel_id=1, source_target_pairs={{32,0},{64,32},{96,64},{128,96},{160,128},{192,160},{224,192},{256... | collective-permute-start | bytes 344072 | tf_op jit(solution)/shard_map/ppermute | solution.py:574
  33.2 0.5 collective-permute-done.6.xl_ref
  33.7 3.8 %collective-permute-done.7.xr_ref = f32[4,7,8,128]{3,2,1,0:T(8,128)S(1)} collective-permute-done((f32[4,7,8,128]{3,2,1,0:T(8,128)S(1)}, f32[4,7,8,128]{3,2,1,0:T(8,128)S(1)}, u32[]{:S(2)}, u32[]{:S(2)}) %collective-permute-start.7) | collective-permute-done | bytes 114720 | tf_op jit(solution)/shard_map/ppermute | solution.py:574
  37.5 0.0 collective-permute-done.9.yr_ref
  37.5 0.0 collective-permute-done.8.yl_ref
  37.5 4.4 %collective-permute-start.11 = (f32[4,14,8,128]{3,2,1,0:T(8,128)S(1)}, f32[4,14,8,128]{3,2,1,0:T(8,128)S(1)}, u32[]{:S(2)}, u32[]{:S(2)}) collective-permute-start(f32[4,14,8,128]{3,2,1,0:T(8,128)S(1)} %shard_map.63), channel_id=1, source_target_pairs={{1,0},{2,1},{3,2},{4,3},{5,4},{6,5},{7,6},{8,7},{9,8},{10,9},{11,1... | collective-permute-start | bytes 688136 | tf_op jit(solution)/shard_map/ppermute | solution.py:574
  41.9 0.0 collective-permute-start.10
  41.9 1.1 collective-permute-done.11.cr_ref
  43.0 2.7 %collective-permute-done.10.cl_ref = f32[4,14,8,128]{3,2,1,0:T(8,128)S(1)} collective-permute-done((f32[4,14,8,128]{3,2,1,0:T(8,128)S(1)}, f32[4,14,8,128]{3,2,1,0:T(8,128)S(1)}, u32[]{:S(2)}, u32[]{:S(2)}) %collective-permute-start.10) | collective-permute-done | bytes 229408 | tf_op jit(solution)/shard_map/ppermute | solution.py:574
  45.8 1.8 %shard_map.64 = (f32[24,8,128]{2,1,0:T(8,128)S(1)}, f32[24,8,128]{2,1,0:T(8,128)S(1)}, f32[24,8,128]{2,1,0:T(8,128)S(1)}, f32[24,8,128]{2,1,0:T(8,128)S(1)}, f32...) custom-call(f32[4,8,8,128]{3,2,1,0:T(8,128)S(1)} %shard_map.62.o_ref, ...), custom_call_target="tpu_custom_call" | custom-call | tf_op jit(solution)/shard_map/pallas_call | solution.py:560
  47.6 4.4 %collective-permute-start.12 = (f32[24,8,128]{2,1,0:T(8,128)S(1)}, f32[24,8,128]{2,1,0:T(8,128)S(1)}, u32[]{:S(2)}, u32[]{:S(2)}) collective-permute-start(f32[24,8,128]{2,1,0:T(8,128)S(1)} %get-tuple-element.43), channel_id=1, source_target_pairs={{0,32},{32,64},{64,96},{96,128},{128,160},{160,192},{192,224},{224... | collective-permute-start | bytes 294920 | tf_op jit(solution)/shard_map/ppermute | solution.py:574
  52.0 1.3 %collective-permute-start.13 = (f32[24,8,128]{2,1,0:T(8,128)S(1)}, f32[24,8,128]{2,1,0:T(8,128)S(1)}, u32[]{:S(2)}, u32[]{:S(2)}) collective-permute-start(f32[24,8,128]{2,1,0:T(8,128)S(1)} %get-tuple-element.44), channel_id=1, source_target_pairs={{32,0},{64,32},{96,64},{128,96},{160,128},{192,160},{224,192},{256... | collective-permute-start | bytes 294920 | tf_op jit(solution)/shard_map/ppermute | solution.py:574
  53.3 1.7 %collective-permute-start.14 = (f32[24,8,128]{2,1,0:T(8,128)S(1)}, f32[24,8,128]{2,1,0:T(8,128)S(1)}, u32[]{:S(2)}, u32[]{:S(2)}) collective-permute-start(f32[24,8,128]{2,1,0:T(8,128)S(1)} %get-tuple-element.45), channel_id=1, source_target_pairs={{0,1},{1,2},{2,3},{3,4},{4,5},{5,6},{6,7},{7,8},{8,9},{9,10},{10,1... | collective-permute-start | bytes 294920 | tf_op jit(solution)/shard_map/ppermute | solution.py:574
  54.9 4.3 %collective-permute-start.15 = (f32[24,8,128]{2,1,0:T(8,128)S(1)}, f32[24,8,128]{2,1,0:T(8,128)S(1)}, u32[]{:S(2)}, u32[]{:S(2)}) collective-permute-start(f32[24,8,128]{2,1,0:T(8,128)S(1)} %get-tuple-element.46), channel_id=1, source_target_pairs={{1,0},{2,1},{3,2},{4,3},{5,4},{6,5},{7,6},{8,7},{9,8},{10,9},{11,1... | collective-permute-start | bytes 294920 | tf_op jit(solution)/shard_map/ppermute | solution.py:574
  59.3 0.0 collective-permute-done.12.xl_ref
  59.3 0.0 collective-permute-done.13.xr_ref
  59.3 0.8 collective-permute-done.14.yl_ref
  60.0 0.2 collective-permute-done.15.yr_ref
  60.2 0.0 collective-permute-start.16
  60.3 4.3 %collective-permute-start.17 = (f32[30,8,128]{2,1,0:T(8,128)S(1)}, f32[30,8,128]{2,1,0:T(8,128)S(1)}, u32[]{:S(2)}, u32[]{:S(2)}) collective-permute-start(f32[30,8,128]{2,1,0:T(8,128)S(1)} %get-tuple-element.48), channel_id=1, source_target_pairs={{1,0},{2,1},{3,2},{4,3},{5,4},{6,5},{7,6},{8,7},{9,8},{10,9},{11,1... | collective-permute-start | bytes 368648 | tf_op jit(solution)/shard_map/ppermute | solution.py:574
  64.6 0.8 collective-permute-done.16.cl_ref
  65.4 0.2 collective-permute-done.17.cr_ref
  65.5 4.9 %shard_map.66 = (f32[16,16,256]{2,1,0:T(8,128)}, f32[8,128]{1,0:T(8,128)S(1)}) custom-call(f32[24,8,128]{2,1,0:T(8,128)S(1)} %collective-permute-done.12.xl_ref, f32[24,8,128]{2,1,0:T(8,128)S(1)} %collective-permute-done.13.xr_ref, f32[24,8,128]{2,1,0:T(8,128)S(1)} %collective-permute-done.14.yl_ref, f32[24,8,128]{2,1,0:T(8,128)S(1)} %collective-permute-done.15.yr_ref, ...), custom_call_target="tpu_custom_call" | custom-call | tf_op jit(solution)/shard_map/pallas_call | solution.py:560
  70.5 14.8 %all_to_all.12 = f32[16,1,128]{2,1,0:T(1,128)S(1)} all-to-all(f32[16,1,128]{2,1,0:T(1,128)S(1)} %broadcast_in_dim.6), channel_id=1, replica_groups=mesh['gx'=16,'gy'=32] {'gx'}, dimensions={0} | all-to-all | bytes 16384 | tf_op jit(solution)/shard_map/all_to_all | solution.py:580
  85.3 26.7 %all_to_all.13 = f32[32,1,128]{2,1,0:T(1,128)S(1)} all-to-all(f32[32,1,128]{2,1,0:T(1,128)S(1)} %broadcast_in_dim.7), channel_id=1, replica_groups=mesh['gx'=16,'gy'=32] {'gy'}, dimensions={0} | all-to-all | bytes 32768 | tf_op jit(solution)/shard_map/all_to_all | solution.py:580
  (11 shorter events, 0.2 us)
Async XLA Ops:
  0.6 1.0 copy-start
  1.6 6.4 %copy-start.3 = (f32[16,16,256]{2,1,0:T(8,128)S(1)}, f32[16,16,256]{2,1,0:T(8,128)}, u32[]{:S(2)}) copy-start(f32[16,16,256]{2,1,0:T(8,128)} %f_ref.3) | copy-start | bytes 786436
  2.5 5.6 %copy-start.1 = (f32[16,16,256]{2,1,0:T(8,128)S(1)}, f32[16,16,256]{2,1,0:T(8,128)}, u32[]{:S(2)}) copy-start(f32[16,16,256]{2,1,0:T(8,128)} %e_ref.3) | copy-start | bytes 786436
  2.5 5.6 %copy-start.2 = (f32[16,16,256]{2,1,0:T(8,128)S(1)}, f32[16,16,256]{2,1,0:T(8,128)}, u32[]{:S(2)}) copy-start(f32[16,16,256]{2,1,0:T(8,128)} %k_ref.3) | copy-start | bytes 786436
  2.6 9.8 %collective-permute-start = (f32[10,16,256]{2,1,0:T(8,128)S(1)}, f32[10,16,256]{2,1,0:T(8,128)S(1)}, u32[]{:S(2)}, u32[]{:S(2)}) collective-permute-start(f32[10,16,256]{2,1,0:T(8,128)S(1)} %pad_maximum_fusion), channel_id=1, source_target_pairs={{0,32},{32,64},{64,96},{96,128},{128,160},{160,192},{192,224},{224... | collective-permute-start | bytes 491528 | tf_op jit(solution)/shard_map/ppermute | solution.py:574
  6.8 6.1 %collective-permute-start.1 = (f32[10,16,256]{2,1,0:T(8,128)S(1)}, f32[10,16,256]{2,1,0:T(8,128)S(1)}, u32[]{:S(2)}, u32[]{:S(2)}) collective-permute-start(f32[10,16,256]{2,1,0:T(8,128)S(1)} %pad_maximum_fusion.1), channel_id=1, source_target_pairs={{32,0},{64,32},{96,64},{128,96},{160,128},{192,160},{224,192},{256... | collective-permute-start | bytes 491528 | tf_op jit(solution)/shard_map/ppermute | solution.py:574
  8.2 13.0 %collective-permute-start.2 = (f32[2,16,8,256]{3,2,1,0:T(8,128)S(1)}, f32[2,16,8,256]{3,2,1,0:T(8,128)S(1)}, u32[]{:S(2)}, u32[]{:S(2)}) collective-permute-start(f32[2,16,8,256]{3,2,1,0:T(8,128)S(1)} %get-tuple-element.35), channel_id=1, source_target_pairs={{0,1},{1,2},{2,3},{3,4},{4,5},{5,6},{6,7},{7,8},{8,9},{9,10},{10,1... | collective-permute-start | bytes 786440 | tf_op jit(solution)/shard_map/ppermute | solution.py:574
  10.7 10.5 %collective-permute-start.3 = (f32[2,16,8,256]{3,2,1,0:T(8,128)S(1)}, f32[2,16,8,256]{3,2,1,0:T(8,128)S(1)}, u32[]{:S(2)}, u32[]{:S(2)}) collective-permute-start(f32[2,16,8,256]{3,2,1,0:T(8,128)S(1)} %get-tuple-element.36), channel_id=1, source_target_pairs={{1,0},{2,1},{3,2},{4,3},{5,4},{6,5},{7,6},{8,7},{9,8},{10,9},{11,1... | collective-permute-start | bytes 786440 | tf_op jit(solution)/shard_map/ppermute | solution.py:574
  12.9 6.1 %collective-permute-start.4 = (f32[2,6,8,256]{3,2,1,0:T(8,128)S(1)}, f32[2,6,8,256]{3,2,1,0:T(8,128)S(1)}, u32[]{:S(2)}, u32[]{:S(2)}) collective-permute-start(f32[2,6,8,256]{3,2,1,0:T(8,128)S(1)} %get-tuple-element.37), channel_id=1, source_target_pairs={{0,1},{1,2},{2,3},{3,4},{4,5},{5,6},{6,7},{7,8},{8,9},{9,10},{10,1... | collective-permute-start | bytes 294920 | tf_op jit(solution)/shard_map/ppermute | solution.py:574
  16.8 4.3 %collective-permute-start.5 = (f32[2,6,8,256]{3,2,1,0:T(8,128)S(1)}, f32[2,6,8,256]{3,2,1,0:T(8,128)S(1)}, u32[]{:S(2)}, u32[]{:S(2)}) collective-permute-start(f32[2,6,8,256]{3,2,1,0:T(8,128)S(1)} %get-tuple-element.38), channel_id=1, source_target_pairs={{1,0},{2,1},{3,2},{4,3},{5,4},{6,5},{7,6},{8,7},{9,8},{10,9},{11,1... | collective-permute-start | bytes 294920 | tf_op jit(solution)/shard_map/ppermute | solution.py:574
  24.5 13.0 %collective-permute-start.9 = (f32[4,8,8,128]{3,2,1,0:T(8,128)S(1)}, f32[4,8,8,128]{3,2,1,0:T(8,128)S(1)}, u32[]{:S(2)}, u32[]{:S(2)}) collective-permute-start(f32[4,8,8,128]{3,2,1,0:T(8,128)S(1)} %shard_map.62.o_ref), channel_id=1, source_target_pairs={{1,0},{2,1},{3,2},{4,3},{5,4},{6,5},{7,6},{8,7},{9,8},{10,9},{11,1... | collective-permute-start | bytes 393224 | tf_op jit(solution)/shard_map/ppermute | solution.py:574
  28.7 8.7 %collective-permute-start.8 = (f32[4,8,8,128]{3,2,1,0:T(8,128)S(1)}, f32[4,8,8,128]{3,2,1,0:T(8,128)S(1)}, u32[]{:S(2)}, u32[]{:S(2)}) collective-permute-start(f32[4,8,8,128]{3,2,1,0:T(8,128)S(1)} %shard_map.62.o_ref), channel_id=1, source_target_pairs={{0,1},{1,2},{2,3},{3,4},{4,5},{5,6},{6,7},{7,8},{8,9},{9,10},{10,1... | collective-permute-start | bytes 393224 | tf_op jit(solution)/shard_map/ppermute | solution.py:574
  28.7 5.0 %collective-permute-start.6 = (f32[4,7,8,128]{3,2,1,0:T(8,128)S(1)}, f32[4,7,8,128]{3,2,1,0:T(8,128)S(1)}, u32[]{:S(2)}, u32[]{:S(2)}) collective-permute-start(f32[4,7,8,128]{3,2,1,0:T(8,128)S(1)} %get-tuple-element.40), channel_id=1, source_target_pairs={{0,32},{32,64},{64,96},{96,128},{128,160},{160,192},{192,224},{224... | collective-permute-start | bytes 344072 | tf_op jit(solution)/shard_map/ppermute | solution.py:574
  31.9 5.5 %collective-permute-start.7 = (f32[4,7,8,128]{3,2,1,0:T(8,128)S(1)}, f32[4,7,8,128]{3,2,1,0:T(8,128)S(1)}, u32[]{:S(2)}, u32[]{:S(2)}) collective-permute-start(f32[4,7,8,128]{3,2,1,0:T(8,128)S(1)} %get-tuple-element.41), channel_id=1, source_target_pairs={{32,0},{64,32},{96,64},{128,96},{160,128},{192,160},{224,192},{256... | collective-permute-start | bytes 344072 | tf_op jit(solution)/shard_map/ppermute | solution.py:574
  37.5 5.5 %collective-permute-start.11 = (f32[4,14,8,128]{3,2,1,0:T(8,128)S(1)}, f32[4,14,8,128]{3,2,1,0:T(8,128)S(1)}, u32[]{:S(2)}, u32[]{:S(2)}) collective-permute-start(f32[4,14,8,128]{3,2,1,0:T(8,128)S(1)} %shard_map.63), channel_id=1, source_target_pairs={{1,0},{2,1},{3,2},{4,3},{5,4},{6,5},{7,6},{8,7},{9,8},{10,9},{11,1... | collective-permute-start | bytes 688136 | tf_op jit(solution)/shard_map/ppermute | solution.py:574
  41.9 3.9 %collective-permute-start.10 = (f32[4,14,8,128]{3,2,1,0:T(8,128)S(1)}, f32[4,14,8,128]{3,2,1,0:T(8,128)S(1)}, u32[]{:S(2)}, u32[]{:S(2)}) collective-permute-start(f32[4,14,8,128]{3,2,1,0:T(8,128)S(1)} %shard_map.63), channel_id=1, source_target_pairs={{0,1},{1,2},{2,3},{3,4},{4,5},{5,6},{6,7},{7,8},{8,9},{9,10},{10,1... | collective-permute-start | bytes 688136 | tf_op jit(solution)/shard_map/ppermute | solution.py:574
  47.6 11.7 %collective-permute-start.12 = (f32[24,8,128]{2,1,0:T(8,128)S(1)}, f32[24,8,128]{2,1,0:T(8,128)S(1)}, u32[]{:S(2)}, u32[]{:S(2)}) collective-permute-start(f32[24,8,128]{2,1,0:T(8,128)S(1)} %get-tuple-element.43), channel_id=1, source_target_pairs={{0,32},{32,64},{64,96},{96,128},{128,160},{160,192},{192,224},{224... | collective-permute-start | bytes 294920 | tf_op jit(solution)/shard_map/ppermute | solution.py:574
  52.0 7.3 %collective-permute-start.13 = (f32[24,8,128]{2,1,0:T(8,128)S(1)}, f32[24,8,128]{2,1,0:T(8,128)S(1)}, u32[]{:S(2)}, u32[]{:S(2)}) collective-permute-start(f32[24,8,128]{2,1,0:T(8,128)S(1)} %get-tuple-element.44), channel_id=1, source_target_pairs={{32,0},{64,32},{96,64},{128,96},{160,128},{192,160},{224,192},{256... | collective-permute-start | bytes 294920 | tf_op jit(solution)/shard_map/ppermute | solution.py:574
  53.3 6.8 %collective-permute-start.14 = (f32[24,8,128]{2,1,0:T(8,128)S(1)}, f32[24,8,128]{2,1,0:T(8,128)S(1)}, u32[]{:S(2)}, u32[]{:S(2)}) collective-permute-start(f32[24,8,128]{2,1,0:T(8,128)S(1)} %get-tuple-element.45), channel_id=1, source_target_pairs={{0,1},{1,2},{2,3},{3,4},{4,5},{5,6},{6,7},{7,8},{8,9},{9,10},{10,1... | collective-permute-start | bytes 294920 | tf_op jit(solution)/shard_map/ppermute | solution.py:574
  54.9 5.3 %collective-permute-start.15 = (f32[24,8,128]{2,1,0:T(8,128)S(1)}, f32[24,8,128]{2,1,0:T(8,128)S(1)}, u32[]{:S(2)}, u32[]{:S(2)}) collective-permute-start(f32[24,8,128]{2,1,0:T(8,128)S(1)} %get-tuple-element.46), channel_id=1, source_target_pairs={{1,0},{2,1},{3,2},{4,3},{5,4},{6,5},{7,6},{8,7},{9,8},{10,9},{11,1... | collective-permute-start | bytes 294920 | tf_op jit(solution)/shard_map/ppermute | solution.py:574
  60.2 5.1 %collective-permute-start.16 = (f32[30,8,128]{2,1,0:T(8,128)S(1)}, f32[30,8,128]{2,1,0:T(8,128)S(1)}, u32[]{:S(2)}, u32[]{:S(2)}) collective-permute-start(f32[30,8,128]{2,1,0:T(8,128)S(1)} %get-tuple-element.47), channel_id=1, source_target_pairs={{0,1},{1,2},{2,3},{3,4},{4,5},{5,6},{6,7},{7,8},{8,9},{9,10},{10,1... | collective-permute-start | bytes 368648 | tf_op jit(solution)/shard_map/ppermute | solution.py:574
  60.3 5.3 %collective-permute-start.17 = (f32[30,8,128]{2,1,0:T(8,128)S(1)}, f32[30,8,128]{2,1,0:T(8,128)S(1)}, u32[]{:S(2)}, u32[]{:S(2)}) collective-permute-start(f32[30,8,128]{2,1,0:T(8,128)S(1)} %get-tuple-element.48), channel_id=1, source_target_pairs={{1,0},{2,1},{3,2},{4,3},{5,4},{6,5},{7,6},{8,7},{9,8},{10,9},{11,1... | collective-permute-start | bytes 368648 | tf_op jit(solution)/shard_map/ppermute | solution.py:574

commit v5 on v4

--- a/solution.py
+++ b/solution.py
@@ -232,20 +232,17 @@
     pack_fine((xl_ref, xr_ref), planes, up_ref, down_ref)
 
 
-def hand_on(in_ref, out_ref):
-    out_ref[...] = in_ref[...]
-
-
-def join_rims(xl_ref, xr_ref, yl_ref, yr_ref, rim_ref):
+def join_rims(xl_ref, xr_ref, yl_ref, yr_ref, up_ref, down_ref):
     del yl_ref, yr_ref
-    planes = xl_ref.shape[1]
-    rim_ref[:, :planes] = xl_ref[...]
-    rim_ref[:, planes:] = xr_ref[...]
+    sent = xl_ref.shape[1] - 1
+    for ref in (up_ref, down_ref):
+        ref[:, :sent] = xl_ref[:, 1:]
+        ref[:, sent:] = xr_ref[:, :sent]
 
 
 def fine_first(
     s_ref, e_ref, k_ref, f_ref, xl_ref, xr_ref, yl_ref, yr_ref, cl_ref, cr_ref,
-    up_ref, down_ref, stack_ref, u0_ref, kw_ref, fw_ref, wx, wy, wz, wb, total,
+    up_ref, down_ref, y_up_ref, y_down_ref, stack_ref, u0_ref, kw_ref, fw_ref, wx, wy, wz, wb, total,
     ua, ub, ew_ref, gather, summed,
     *, size_x, size_y,
 ):
@@ -315,10 +312,10 @@
         )
         for index, tile in enumerate(tiles):
             stack_ref[index, j] = tile
-            if j > 0:
-                up_ref[index, j - 1] = tile
-            if j < pairs - 1:
-                down_ref[index, j] = tile
+            y_up_ref[index, j] = tile
+            y_down_ref[index, j] = tile
+            up_ref[index, j] = tile
+            down_ref[index, j] = tile
 
 
 def middle_first(
@@ -342,7 +339,7 @@
 
     for x in range(1, planes - 1):
         if x < RIM_1:
-            assemble(x, xl_ref, cl_ref, cr_ref, x - 1, x - 1)
+            assemble(x, xl_ref, cl_ref, cr_ref, x, x - 1)
         elif x < RIM_1 + own:
             assemble(x, o_ref, yl_ref, yr_ref, x - RIM_1, x - RIM_1)
         else:
@@ -595,19 +592,18 @@
     cl, cr = swap(*call(pack_fine_rim, [arr(2, 2 * RIM_X0, 8, nz)] * 2, [], xl, xr), "gy", True)
     own1, own1_y, nz1 = own_x // 2, own_y // 2, nz // 2
     gathered = 2 * own1 * rows0 + 2 * own1 * own_y
-    upward, downward, stack1, u0, *level0 = call(
+    upward, downward, y_upward, y_downward, stack1, u0, *level0 = call(
         functools.partial(fine_first, size_x=size_x, size_y=size_y),
-        [arr(4, own1 - 1, own1_y, nz1)] * 2 + [arr(4, own1, own1_y, nz1)]
+        [arr(4, own1, own1_y, nz1)] * 5
         + [arr(own_x, own_y, nz)] + [arr(*window0)] * 7,
         [window0] * 3 + [(gathered, nz), (gathered, nz1)],
         *fields, xl, xr, yl, yr, cl, cr,
     )
 
     xl, xr = swap(upward, downward, "gx")
-    (stack1,) = call(hand_on, [stack1], [], stack1)
-    yl, yr = swap(stack1, stack1, "gy", True)
-    (rim,) = call(join_rims, [arr(4, 2 * (own1 - 1), own1_y, nz1)], [], xl, xr, yl, yr)
-    cl, cr = swap(rim, rim, "gy", True)
+    yl, yr = swap(y_upward, y_downward, "gy", True)
+    rim = arr(4, 2 * (own1 - 1), own1_y, nz1)
+    cl, cr = swap(*call(join_rims, [rim, rim], [], xl, xr, yl, yr), "gy", True)
     planes1 = own1 + 2 * RIM_1
     window1 = (planes1, own1_y + 2 * RIM_1, nz1)
     sent_x = 2 * RIM_2 + 4 * RIM_X0

time: 114 us -> 111 us (0.974)
  waiting for transfers between devices: 13.5 us -> 7.94 us
  blocking collectives: 41.5 us -> 44.3 us
    ppermute x18, waiting for transfers between devices: 13.5 us -> 7.94 us  [swap(): return (lax.ppermute(upward, axis, up), lax.ppermute(downward, axis, down))]
    all_to_all x2, blocking collectives: 41.5 us -> 44.3 us  [sum_over(): lax.all_to_all(rows, axis, 0, 0, tiled=True)]
    pallas_call x8 -> x7, Pallas kernels: 10.2 us -> 9.86 us  [call(): pl.pallas_call(kernel, out_shape=outs, in_specs=[pl.BlockSpec(memory_spac...]
where the time goes in v5:
time: 111 us; the launch traced here: 110 us
  starting transfers between devices  44.3 us (40%)
  blocking collectives  44.3 us (40%)
  Pallas kernels  9.86 us (9%)
  waiting for transfers between devices  7.94 us (7%)
  between operations  2.02 us (2%)
  local copies, waits for them, and re-layouts  1.92 us (2%)
    ppermute x18, starting transfers between devices, swap(): return (lax.ppermute(upward, axis, up), lax.ppermute(downward, axis, down))  44.3 us
    all_to_all x2, blocking collectives, sum_over(): lax.all_to_all(rows, axis, 0, 0, tiled=True)  44.3 us
    pallas_call x7, Pallas kernels, call(): pl.pallas_call(kernel, out_shape=outs, in_specs=[pl.BlockSpec(memory_spac...  9.86 us
    ppermute x18, waiting for transfers between devices, swap(): return (lax.ppermute(upward, axis, up), lax.ppermute(downward, axis, down))  7.94 us
  transfers between devices with their start and end apart: 18, of which 11 were waited for; matrix products, arithmetic and copies ran while one was open for 0% of the time, Pallas kernels for 0%

profile of v5, /device:TPU:1, one launch (start us, length us, event | category | flops | bytes accessed | tf_op | source)
XLA Modules:
  0.0 110.4 jit_solution(5675124221944070418)
XLA Ops:
  0.6 0.0 copy-start
  0.6 0.9 fusion.2
  1.5 0.1 copy-done
  1.6 0.0 copy-start.3
  1.6 0.9 fusion
  2.5 0.0 copy-start.1
  2.5 0.0 copy-start.2
  2.6 4.2 %collective-permute-start = (f32[10,16,256]{2,1,0:T(8,128)S(1)}, f32[10,16,256]{2,1,0:T(8,128)S(1)}, u32[]{:S(2)}, u32[]{:S(2)}) collective-permute-start(f32[10,16,256]{2,1,0:T(8,128)S(1)} %pad_maximum_fusion), channel_id=1, source_target_pairs={{0,32},{32,64},{64,96},{96,128},{128,160},{160,192},{192,224},{224... | collective-permute-start | bytes 491528 | tf_op jit(solution)/shard_map/ppermute | solution.py:571
  6.8 1.3 %collective-permute-start.1 = (f32[10,16,256]{2,1,0:T(8,128)S(1)}, f32[10,16,256]{2,1,0:T(8,128)S(1)}, u32[]{:S(2)}, u32[]{:S(2)}) collective-permute-start(f32[10,16,256]{2,1,0:T(8,128)S(1)} %pad_maximum_fusion.1), channel_id=1, source_target_pairs={{32,0},{64,32},{96,64},{128,96},{160,128},{192,160},{224,192},{256... | collective-permute-start | bytes 491528 | tf_op jit(solution)/shard_map/ppermute | solution.py:571
  8.1 0.0 copy-done.3
  8.1 0.0 copy-done.1
  8.1 0.0 copy-done.2
  8.1 0.1 shard_map.59
  8.2 2.5 %collective-permute-start.2 = (f32[2,16,8,256]{3,2,1,0:T(8,128)S(1)}, f32[2,16,8,256]{3,2,1,0:T(8,128)S(1)}, u32[]{:S(2)}, u32[]{:S(2)}) collective-permute-start(f32[2,16,8,256]{3,2,1,0:T(8,128)S(1)} %get-tuple-element.39), channel_id=1, source_target_pairs={{0,1},{1,2},{2,3},{3,4},{4,5},{5,6},{6,7},{7,8},{8,9},{9,10},{10,1... | collective-permute-start | bytes 786440 | tf_op jit(solution)/shard_map/ppermute | solution.py:571
  10.7 1.7 %collective-permute-start.3 = (f32[2,16,8,256]{3,2,1,0:T(8,128)S(1)}, f32[2,16,8,256]{3,2,1,0:T(8,128)S(1)}, u32[]{:S(2)}, u32[]{:S(2)}) collective-permute-start(f32[2,16,8,256]{3,2,1,0:T(8,128)S(1)} %get-tuple-element.40), channel_id=1, source_target_pairs={{1,0},{2,1},{3,2},{4,3},{5,4},{6,5},{7,6},{8,7},{9,8},{10,9},{11,1... | collective-permute-start | bytes 786440 | tf_op jit(solution)/shard_map/ppermute | solution.py:571
  12.3 0.0 collective-permute-done.xl_ref
  12.4 0.5 collective-permute-done.1.xr_ref
  12.9 4.0 %collective-permute-start.4 = (f32[2,6,8,256]{3,2,1,0:T(8,128)S(1)}, f32[2,6,8,256]{3,2,1,0:T(8,128)S(1)}, u32[]{:S(2)}, u32[]{:S(2)}) collective-permute-start(f32[2,6,8,256]{3,2,1,0:T(8,128)S(1)} %get-tuple-element.41), channel_id=1, source_target_pairs={{0,1},{1,2},{2,3},{3,4},{4,5},{5,6},{6,7},{7,8},{8,9},{9,10},{10,1... | collective-permute-start | bytes 294920 | tf_op jit(solution)/shard_map/ppermute | solution.py:571
  16.8 1.3 %collective-permute-start.5 = (f32[2,6,8,256]{3,2,1,0:T(8,128)S(1)}, f32[2,6,8,256]{3,2,1,0:T(8,128)S(1)}, u32[]{:S(2)}, u32[]{:S(2)}) collective-permute-start(f32[2,6,8,256]{3,2,1,0:T(8,128)S(1)} %get-tuple-element.42), channel_id=1, source_target_pairs={{1,0},{2,1},{3,2},{4,3},{5,4},{6,5},{7,6},{8,7},{9,8},{10,9},{11,1... | collective-permute-start | bytes 294920 | tf_op jit(solution)/shard_map/ppermute | solution.py:571
  18.2 0.8 collective-permute-done.4.cl_ref
  19.0 2.2 %collective-permute-done.5.cr_ref = f32[2,6,8,256]{3,2,1,0:T(8,128)S(1)} collective-permute-done((f32[2,6,8,256]{3,2,1,0:T(8,128)S(1)}, f32[2,6,8,256]{3,2,1,0:T(8,128)S(1)}, u32[]{:S(2)}, u32[]{:S(2)}) %collective-permute-start.5) | collective-permute-done | bytes 98336 | tf_op jit(solution)/shard_map/ppermute | solution.py:571
  21.2 0.0 collective-permute-done.2.yl_ref
  21.2 0.0 collective-permute-done.3.yr_ref
  21.2 3.1 %shard_map.61 = (f32[4,8,8,128]{3,2,1,0:T(8,128)S(1)}, f32[4,8,8,128]{3,2,1,0:T(8,128)S(1)}, f32[4,8,8,128]{3,2,1,0:T(8,128)S(1)}, f32[4,8,8,128]{3,2,1,0:T(8,12...) custom-call(f32[16,16,256]{2,1,0:T(8,128)S(1)} %copy-done, ...), custom_call_target="tpu_custom_call" | custom-call | tf_op jit(solution)/shard_map/pallas_call | solution.py:557
  24.3 3.2 %collective-permute-start.6 = (f32[4,8,8,128]{3,2,1,0:T(8,128)S(1)}, f32[4,8,8,128]{3,2,1,0:T(8,128)S(1)}, u32[]{:S(2)}, u32[]{:S(2)}) collective-permute-start(f32[4,8,8,128]{3,2,1,0:T(8,128)S(1)} %get-tuple-element.44), channel_id=1, source_target_pairs={{0,32},{32,64},{64,96},{96,128},{128,160},{160,192},{192,224},{224... | collective-permute-start | bytes 393224 | tf_op jit(solution)/shard_map/ppermute | solution.py:571
  27.5 1.3 %collective-permute-start.7 = (f32[4,8,8,128]{3,2,1,0:T(8,128)S(1)}, f32[4,8,8,128]{3,2,1,0:T(8,128)S(1)}, u32[]{:S(2)}, u32[]{:S(2)}) collective-permute-start(f32[4,8,8,128]{3,2,1,0:T(8,128)S(1)} %get-tuple-element.45), channel_id=1, source_target_pairs={{32,0},{64,32},{96,64},{128,96},{160,128},{192,160},{224,192},{256... | collective-permute-start | bytes 393224 | tf_op jit(solution)/shard_map/ppermute | solution.py:571
  28.8 0.0 collective-permute-start.8
  28.9 4.5 %collective-permute-start.9 = (f32[4,8,8,128]{3,2,1,0:T(8,128)S(1)}, f32[4,8,8,128]{3,2,1,0:T(8,128)S(1)}, u32[]{:S(2)}, u32[]{:S(2)}) collective-permute-start(f32[4,8,8,128]{3,2,1,0:T(8,128)S(1)} %get-tuple-element.47), channel_id=1, source_target_pairs={{1,0},{2,1},{3,2},{4,3},{5,4},{6,5},{7,6},{8,7},{9,8},{10,9},{11,1... | collective-permute-start | bytes 393224 | tf_op jit(solution)/shard_map/ppermute | solution.py:571
  33.4 0.0 collective-permute-done.6.xl_ref
  33.4 0.0 collective-permute-done.7.xr_ref
  33.4 0.8 collective-permute-done.8.yl_ref
  34.2 0.2 collective-permute-done.9.yr_ref
  34.4 0.7 collective-permute-start.10
  35.1 3.9 %collective-permute-start.11 = (f32[4,14,8,128]{3,2,1,0:T(8,128)S(1)}, f32[4,14,8,128]{3,2,1,0:T(8,128)S(1)}, u32[]{:S(2)}, u32[]{:S(2)}) collective-permute-start(f32[4,14,8,128]{3,2,1,0:T(8,128)S(1)} %get-tuple-element.49), channel_id=1, source_target_pairs={{1,0},{2,1},{3,2},{4,3},{5,4},{6,5},{7,6},{8,7},{9,8},{10,9},{11,1... | collective-permute-start | bytes 688136 | tf_op jit(solution)/shard_map/ppermute | solution.py:571
  39.0 1.0 collective-permute-done.10.cl_ref
  40.0 0.6 collective-permute-done.11.cr_ref
  40.6 1.8 %shard_map.63 = (f32[24,8,128]{2,1,0:T(8,128)S(1)}, f32[24,8,128]{2,1,0:T(8,128)S(1)}, f32[24,8,128]{2,1,0:T(8,128)S(1)}, f32[24,8,128]{2,1,0:T(8,128)S(1)}, f32...) custom-call(f32[4,8,8,128]{3,2,1,0:T(8,128)S(1)} %get-tuple-element., ...), custom_call_target="tpu_custom_call" | custom-call | tf_op jit(solution)/shard_map/pallas_call | solution.py:557
  42.4 3.8 %collective-permute-start.12 = (f32[24,8,128]{2,1,0:T(8,128)S(1)}, f32[24,8,128]{2,1,0:T(8,128)S(1)}, u32[]{:S(2)}, u32[]{:S(2)}) collective-permute-start(f32[24,8,128]{2,1,0:T(8,128)S(1)} %get-tuple-element.51), channel_id=1, source_target_pairs={{0,32},{32,64},{64,96},{96,128},{128,160},{160,192},{192,224},{224... | collective-permute-start | bytes 294920 | tf_op jit(solution)/shard_map/ppermute | solution.py:571
  46.2 1.3 %collective-permute-start.13 = (f32[24,8,128]{2,1,0:T(8,128)S(1)}, f32[24,8,128]{2,1,0:T(8,128)S(1)}, u32[]{:S(2)}, u32[]{:S(2)}) collective-permute-start(f32[24,8,128]{2,1,0:T(8,128)S(1)} %get-tuple-element.52), channel_id=1, source_target_pairs={{32,0},{64,32},{96,64},{128,96},{160,128},{192,160},{224,192},{256... | collective-permute-start | bytes 294920 | tf_op jit(solution)/shard_map/ppermute | solution.py:571
  47.5 0.3 collective-permute-start.14
  47.8 5.5 %collective-permute-start.15 = (f32[24,8,128]{2,1,0:T(8,128)S(1)}, f32[24,8,128]{2,1,0:T(8,128)S(1)}, u32[]{:S(2)}, u32[]{:S(2)}) collective-permute-start(f32[24,8,128]{2,1,0:T(8,128)S(1)} %get-tuple-element.54), channel_id=1, source_target_pairs={{1,0},{2,1},{3,2},{4,3},{5,4},{6,5},{7,6},{8,7},{9,8},{10,9},{11,1... | collective-permute-start | bytes 294920 | tf_op jit(solution)/shard_map/ppermute | solution.py:571
  53.4 0.0 collective-permute-done.12.xl_ref
  53.4 0.0 collective-permute-done.13.xr_ref
  53.4 0.8 collective-permute-done.14.yl_ref
  54.1 0.2 collective-permute-done.15.yr_ref
  54.3 0.0 collective-permute-start.16
  54.4 4.8 %collective-permute-start.17 = (f32[30,8,128]{2,1,0:T(8,128)S(1)}, f32[30,8,128]{2,1,0:T(8,128)S(1)}, u32[]{:S(2)}, u32[]{:S(2)}) collective-permute-start(f32[30,8,128]{2,1,0:T(8,128)S(1)} %get-tuple-element.56), channel_id=1, source_target_pairs={{1,0},{2,1},{3,2},{4,3},{5,4},{6,5},{7,6},{8,7},{9,8},{10,9},{11,1... | collective-permute-start | bytes 368648 | tf_op jit(solution)/shard_map/ppermute | solution.py:571
  59.1 0.8 collective-permute-done.16.cl_ref
  59.9 0.2 collective-permute-done.17.cr_ref
  60.1 4.8 %shard_map.65 = (f32[16,16,256]{2,1,0:T(8,128)}, f32[8,128]{1,0:T(8,128)S(1)}) custom-call(f32[24,8,128]{2,1,0:T(8,128)S(1)} %collective-permute-done.12.xl_ref, f32[24,8,128]{2,1,0:T(8,128)S(1)} %collective-permute-done.13.xr_ref, f32[24,8,128]{2,1,0:T(8,128)S(1)} %collective-permute-done.14.yl_ref, f32[24,8,128]{2,1,0:T(8,128)S(1)} %collective-permute-done.15.yr_ref, ...), custom_call_target="tpu_custom_call" | custom-call | tf_op jit(solution)/shard_map/pallas_call | solution.py:557
  64.9 16.4 %all_to_all.12 = f32[16,1,128]{2,1,0:T(1,128)S(1)} all-to-all(f32[16,1,128]{2,1,0:T(1,128)S(1)} %broadcast_in_dim.6), channel_id=1, replica_groups=mesh['gx'=16,'gy'=32] {'gx'}, dimensions={0} | all-to-all | bytes 16384 | tf_op jit(solution)/shard_map/all_to_all | solution.py:577
  81.3 27.9 %all_to_all.13 = f32[32,1,128]{2,1,0:T(1,128)S(1)} all-to-all(f32[32,1,128]{2,1,0:T(1,128)S(1)} %broadcast_in_dim.7), channel_id=1, replica_groups=mesh['gx'=16,'gy'=32] {'gy'}, dimensions={0} | all-to-all | bytes 32768 | tf_op jit(solution)/shard_map/all_to_all | solution.py:577
  (10 shorter events, 0.2 us)
Async XLA Ops:
  0.6 1.0 copy-start
  1.6 6.4 %copy-start.3 = (f32[16,16,256]{2,1,0:T(8,128)S(1)}, f32[16,16,256]{2,1,0:T(8,128)}, u32[]{:S(2)}) copy-start(f32[16,16,256]{2,1,0:T(8,128)} %f_ref.3) | copy-start | bytes 786436
  2.5 5.6 %copy-start.1 = (f32[16,16,256]{2,1,0:T(8,128)S(1)}, f32[16,16,256]{2,1,0:T(8,128)}, u32[]{:S(2)}) copy-start(f32[16,16,256]{2,1,0:T(8,128)} %e_ref.3) | copy-start | bytes 786436
  2.5 5.6 %copy-start.2 = (f32[16,16,256]{2,1,0:T(8,128)S(1)}, f32[16,16,256]{2,1,0:T(8,128)}, u32[]{:S(2)}) copy-start(f32[16,16,256]{2,1,0:T(8,128)} %k_ref.3) | copy-start | bytes 786436
  2.6 9.8 %collective-permute-start = (f32[10,16,256]{2,1,0:T(8,128)S(1)}, f32[10,16,256]{2,1,0:T(8,128)S(1)}, u32[]{:S(2)}, u32[]{:S(2)}) collective-permute-start(f32[10,16,256]{2,1,0:T(8,128)S(1)} %pad_maximum_fusion), channel_id=1, source_target_pairs={{0,32},{32,64},{64,96},{96,128},{128,160},{160,192},{192,224},{224... | collective-permute-start | bytes 491528 | tf_op jit(solution)/shard_map/ppermute | solution.py:571
  6.8 6.1 %collective-permute-start.1 = (f32[10,16,256]{2,1,0:T(8,128)S(1)}, f32[10,16,256]{2,1,0:T(8,128)S(1)}, u32[]{:S(2)}, u32[]{:S(2)}) collective-permute-start(f32[10,16,256]{2,1,0:T(8,128)S(1)} %pad_maximum_fusion.1), channel_id=1, source_target_pairs={{32,0},{64,32},{96,64},{128,96},{160,128},{192,160},{224,192},{256... | collective-permute-start | bytes 491528 | tf_op jit(solution)/shard_map/ppermute | solution.py:571
  8.2 13.0 %collective-permute-start.2 = (f32[2,16,8,256]{3,2,1,0:T(8,128)S(1)}, f32[2,16,8,256]{3,2,1,0:T(8,128)S(1)}, u32[]{:S(2)}, u32[]{:S(2)}) collective-permute-start(f32[2,16,8,256]{3,2,1,0:T(8,128)S(1)} %get-tuple-element.39), channel_id=1, source_target_pairs={{0,1},{1,2},{2,3},{3,4},{4,5},{5,6},{6,7},{7,8},{8,9},{9,10},{10,1... | collective-permute-start | bytes 786440 | tf_op jit(solution)/shard_map/ppermute | solution.py:571
  10.7 10.5 %collective-permute-start.3 = (f32[2,16,8,256]{3,2,1,0:T(8,128)S(1)}, f32[2,16,8,256]{3,2,1,0:T(8,128)S(1)}, u32[]{:S(2)}, u32[]{:S(2)}) collective-permute-start(f32[2,16,8,256]{3,2,1,0:T(8,128)S(1)} %get-tuple-element.40), channel_id=1, source_target_pairs={{1,0},{2,1},{3,2},{4,3},{5,4},{6,5},{7,6},{8,7},{9,8},{10,9},{11,1... | collective-permute-start | bytes 786440 | tf_op jit(solution)/shard_map/ppermute | solution.py:571
  12.9 6.1 %collective-permute-start.4 = (f32[2,6,8,256]{3,2,1,0:T(8,128)S(1)}, f32[2,6,8,256]{3,2,1,0:T(8,128)S(1)}, u32[]{:S(2)}, u32[]{:S(2)}) collective-permute-start(f32[2,6,8,256]{3,2,1,0:T(8,128)S(1)} %get-tuple-element.41), channel_id=1, source_target_pairs={{0,1},{1,2},{2,3},{3,4},{4,5},{5,6},{6,7},{7,8},{8,9},{9,10},{10,1... | collective-permute-start | bytes 294920 | tf_op jit(solution)/shard_map/ppermute | solution.py:571
  16.8 4.3 %collective-permute-start.5 = (f32[2,6,8,256]{3,2,1,0:T(8,128)S(1)}, f32[2,6,8,256]{3,2,1,0:T(8,128)S(1)}, u32[]{:S(2)}, u32[]{:S(2)}) collective-permute-start(f32[2,6,8,256]{3,2,1,0:T(8,128)S(1)} %get-tuple-element.42), channel_id=1, source_target_pairs={{1,0},{2,1},{3,2},{4,3},{5,4},{6,5},{7,6},{8,7},{9,8},{10,9},{11,1... | collective-permute-start | bytes 294920 | tf_op jit(solution)/shard_map/ppermute | solution.py:571
  24.3 9.0 %collective-permute-start.6 = (f32[4,8,8,128]{3,2,1,0:T(8,128)S(1)}, f32[4,8,8,128]{3,2,1,0:T(8,128)S(1)}, u32[]{:S(2)}, u32[]{:S(2)}) collective-permute-start(f32[4,8,8,128]{3,2,1,0:T(8,128)S(1)} %get-tuple-element.44), channel_id=1, source_target_pairs={{0,32},{32,64},{64,96},{96,128},{128,160},{160,192},{192,224},{224... | collective-permute-start | bytes 393224 | tf_op jit(solution)/shard_map/ppermute | solution.py:571
  27.5 5.8 %collective-permute-start.7 = (f32[4,8,8,128]{3,2,1,0:T(8,128)S(1)}, f32[4,8,8,128]{3,2,1,0:T(8,128)S(1)}, u32[]{:S(2)}, u32[]{:S(2)}) collective-permute-start(f32[4,8,8,128]{3,2,1,0:T(8,128)S(1)} %get-tuple-element.45), channel_id=1, source_target_pairs={{32,0},{64,32},{96,64},{128,96},{160,128},{192,160},{224,192},{256... | collective-permute-start | bytes 393224 | tf_op jit(solution)/shard_map/ppermute | solution.py:571
  28.8 5.3 %collective-permute-start.8 = (f32[4,8,8,128]{3,2,1,0:T(8,128)S(1)}, f32[4,8,8,128]{3,2,1,0:T(8,128)S(1)}, u32[]{:S(2)}, u32[]{:S(2)}) collective-permute-start(f32[4,8,8,128]{3,2,1,0:T(8,128)S(1)} %get-tuple-element.46), channel_id=1, source_target_pairs={{0,1},{1,2},{2,3},{3,4},{4,5},{5,6},{6,7},{7,8},{8,9},{9,10},{10,1... | collective-permute-start | bytes 393224 | tf_op jit(solution)/shard_map/ppermute | solution.py:571
  28.9 5.5 %collective-permute-start.9 = (f32[4,8,8,128]{3,2,1,0:T(8,128)S(1)}, f32[4,8,8,128]{3,2,1,0:T(8,128)S(1)}, u32[]{:S(2)}, u32[]{:S(2)}) collective-permute-start(f32[4,8,8,128]{3,2,1,0:T(8,128)S(1)} %get-tuple-element.47), channel_id=1, source_target_pairs={{1,0},{2,1},{3,2},{4,3},{5,4},{6,5},{7,6},{8,7},{9,8},{10,9},{11,1... | collective-permute-start | bytes 393224 | tf_op jit(solution)/shard_map/ppermute | solution.py:571
  34.4 5.6 %collective-permute-start.10 = (f32[4,14,8,128]{3,2,1,0:T(8,128)S(1)}, f32[4,14,8,128]{3,2,1,0:T(8,128)S(1)}, u32[]{:S(2)}, u32[]{:S(2)}) collective-permute-start(f32[4,14,8,128]{3,2,1,0:T(8,128)S(1)} %get-tuple-element.48), channel_id=1, source_target_pairs={{0,1},{1,2},{2,3},{3,4},{4,5},{5,6},{6,7},{7,8},{8,9},{9,10},{10,1... | collective-permute-start | bytes 688136 | tf_op jit(solution)/shard_map/ppermute | solution.py:571
  35.1 5.4 %collective-permute-start.11 = (f32[4,14,8,128]{3,2,1,0:T(8,128)S(1)}, f32[4,14,8,128]{3,2,1,0:T(8,128)S(1)}, u32[]{:S(2)}, u32[]{:S(2)}) collective-permute-start(f32[4,14,8,128]{3,2,1,0:T(8,128)S(1)} %get-tuple-element.49), channel_id=1, source_target_pairs={{1,0},{2,1},{3,2},{4,3},{5,4},{6,5},{7,6},{8,7},{9,8},{10,9},{11,1... | collective-permute-start | bytes 688136 | tf_op jit(solution)/shard_map/ppermute | solution.py:571
  42.4 11.0 %collective-permute-start.12 = (f32[24,8,128]{2,1,0:T(8,128)S(1)}, f32[24,8,128]{2,1,0:T(8,128)S(1)}, u32[]{:S(2)}, u32[]{:S(2)}) collective-permute-start(f32[24,8,128]{2,1,0:T(8,128)S(1)} %get-tuple-element.51), channel_id=1, source_target_pairs={{0,32},{32,64},{64,96},{96,128},{128,160},{160,192},{192,224},{224... | collective-permute-start | bytes 294920 | tf_op jit(solution)/shard_map/ppermute | solution.py:571
  46.2 7.1 %collective-permute-start.13 = (f32[24,8,128]{2,1,0:T(8,128)S(1)}, f32[24,8,128]{2,1,0:T(8,128)S(1)}, u32[]{:S(2)}, u32[]{:S(2)}) collective-permute-start(f32[24,8,128]{2,1,0:T(8,128)S(1)} %get-tuple-element.52), channel_id=1, source_target_pairs={{32,0},{64,32},{96,64},{128,96},{160,128},{192,160},{224,192},{256... | collective-permute-start | bytes 294920 | tf_op jit(solution)/shard_map/ppermute | solution.py:571
  47.5 6.6 %collective-permute-start.14 = (f32[24,8,128]{2,1,0:T(8,128)S(1)}, f32[24,8,128]{2,1,0:T(8,128)S(1)}, u32[]{:S(2)}, u32[]{:S(2)}) collective-permute-start(f32[24,8,128]{2,1,0:T(8,128)S(1)} %get-tuple-element.53), channel_id=1, source_target_pairs={{0,1},{1,2},{2,3},{3,4},{4,5},{5,6},{6,7},{7,8},{8,9},{9,10},{10,1... | collective-permute-start | bytes 294920 | tf_op jit(solution)/shard_map/ppermute | solution.py:571
  47.8 6.5 %collective-permute-start.15 = (f32[24,8,128]{2,1,0:T(8,128)S(1)}, f32[24,8,128]{2,1,0:T(8,128)S(1)}, u32[]{:S(2)}, u32[]{:S(2)}) collective-permute-start(f32[24,8,128]{2,1,0:T(8,128)S(1)} %get-tuple-element.54), channel_id=1, source_target_pairs={{1,0},{2,1},{3,2},{4,3},{5,4},{6,5},{7,6},{8,7},{9,8},{10,9},{11,1... | collective-permute-start | bytes 294920 | tf_op jit(solution)/shard_map/ppermute | solution.py:571
  54.3 5.6 %collective-permute-start.16 = (f32[30,8,128]{2,1,0:T(8,128)S(1)}, f32[30,8,128]{2,1,0:T(8,128)S(1)}, u32[]{:S(2)}, u32[]{:S(2)}) collective-permute-start(f32[30,8,128]{2,1,0:T(8,128)S(1)} %get-tuple-element.55), channel_id=1, source_target_pairs={{0,1},{1,2},{2,3},{3,4},{4,5},{5,6},{6,7},{7,8},{8,9},{9,10},{10,1... | collective-permute-start | bytes 368648 | tf_op jit(solution)/shard_map/ppermute | solution.py:571
  54.4 5.7 %collective-permute-start.17 = (f32[30,8,128]{2,1,0:T(8,128)S(1)}, f32[30,8,128]{2,1,0:T(8,128)S(1)}, u32[]{:S(2)}, u32[]{:S(2)}) collective-permute-start(f32[30,8,128]{2,1,0:T(8,128)S(1)} %get-tuple-element.56), channel_id=1, source_target_pairs={{1,0},{2,1},{3,2},{4,3},{5,4},{6,5},{7,6},{8,7},{9,8},{10,9},{11,1... | collective-permute-start | bytes 368648 | tf_op jit(solution)/shard_map/ppermute | solution.py:571

commit v6 on v5

--- a/solution.py
+++ b/solution.py
@@ -12,7 +12,7 @@
 F32 = jnp.float32
 LANES = 128
 VMEM_LIMIT = 24 * 1024 * 1024
-AT_ONCE_0, AT_ONCE_1, AT_ONCE_2 = 1, 3, 7
+AT_ONCE_0, AT_ONCE_1, AT_ONCE_2 = 1, 3, 14
 
 RIM_X0, RIM_Y0 = 3, 4
 RIM_1 = 8
@@ -628,7 +628,7 @@
         + [window1] * 2 + [(12 * 32, nz1)] + [window0] * 2 + [(12 * 32, nz)],
         xl, xr, yl, yr, cl, cr, stack2, u0, *level1, *level0,
     )
-    total = sum_over(sum_over(part[:1], "gx"), "gy")[0, 0]
+    total = sum_over(sum_over(part[:1], "gy"), "gx")[0, 0]
     return relaxed, jnp.sqrt(total / (size_x * size_y * nz))
 
 

time: 111 us -> 110 us (level)
    all_to_all x2, blocking collectives: 44.3 us -> 43.2 us  [sum_over(): lax.all_to_all(rows, axis, 0, 0, tiled=True)]
where the time goes in v6:
time: 110 us; the launch traced here: 109 us
  starting transfers between devices  44.3 us (40%)
  blocking collectives  43.2 us (39%)
  Pallas kernels  9.76 us (9%)
  waiting for transfers between devices  7.94 us (7%)
  between operations  2.02 us (2%)
  local copies, waits for them, and re-layouts  1.92 us (2%)
    ppermute x18, starting transfers between devices, swap(): return (lax.ppermute(upward, axis, up), lax.ppermute(downward, axis, down))  44.3 us
    all_to_all x2, blocking collectives, sum_over(): lax.all_to_all(rows, axis, 0, 0, tiled=True)  43.2 us
    pallas_call x7, Pallas kernels, call(): pl.pallas_call(kernel, out_shape=outs, in_specs=[pl.BlockSpec(memory_spac...  9.76 us
    ppermute x18, waiting for transfers between devices, swap(): return (lax.ppermute(upward, axis, up), lax.ppermute(downward, axis, down))  7.94 us
  transfers between devices with their start and end apart: 18, of which 11 were waited for; matrix products, arithmetic and copies ran while one was open for 0% of the time, Pallas kernels for 0%

profile of v6, /device:TPU:1, one launch (start us, length us, event | category | flops | bytes accessed | tf_op | source)
XLA Modules:
  0.0 109.2 jit_solution(16849750672543299614)
XLA Ops:
  0.6 0.0 copy-start
  0.6 0.9 fusion.2
  1.5 0.1 copy-done
  1.6 0.0 copy-start.3
  1.6 0.9 fusion
  2.5 0.0 copy-start.1
  2.5 0.0 copy-start.2
  2.6 4.2 %collective-permute-start = (f32[10,16,256]{2,1,0:T(8,128)S(1)}, f32[10,16,256]{2,1,0:T(8,128)S(1)}, u32[]{:S(2)}, u32[]{:S(2)}) collective-permute-start(f32[10,16,256]{2,1,0:T(8,128)S(1)} %pad_maximum_fusion), channel_id=1, source_target_pairs={{0,32},{32,64},{64,96},{96,128},{128,160},{160,192},{192,224},{224... | collective-permute-start | bytes 491528 | tf_op jit(solution)/shard_map/ppermute | solution.py:571
  6.8 1.3 %collective-permute-start.1 = (f32[10,16,256]{2,1,0:T(8,128)S(1)}, f32[10,16,256]{2,1,0:T(8,128)S(1)}, u32[]{:S(2)}, u32[]{:S(2)}) collective-permute-start(f32[10,16,256]{2,1,0:T(8,128)S(1)} %pad_maximum_fusion.1), channel_id=1, source_target_pairs={{32,0},{64,32},{96,64},{128,96},{160,128},{192,160},{224,192},{256... | collective-permute-start | bytes 491528 | tf_op jit(solution)/shard_map/ppermute | solution.py:571
  8.1 0.0 copy-done.3
  8.1 0.0 copy-done.1
  8.1 0.0 copy-done.2
  8.1 0.1 shard_map.59
  8.2 2.5 %collective-permute-start.2 = (f32[2,16,8,256]{3,2,1,0:T(8,128)S(1)}, f32[2,16,8,256]{3,2,1,0:T(8,128)S(1)}, u32[]{:S(2)}, u32[]{:S(2)}) collective-permute-start(f32[2,16,8,256]{3,2,1,0:T(8,128)S(1)} %get-tuple-element.39), channel_id=1, source_target_pairs={{0,1},{1,2},{2,3},{3,4},{4,5},{5,6},{6,7},{7,8},{8,9},{9,10},{10,1... | collective-permute-start | bytes 786440 | tf_op jit(solution)/shard_map/ppermute | solution.py:571
  10.7 1.7 %collective-permute-start.3 = (f32[2,16,8,256]{3,2,1,0:T(8,128)S(1)}, f32[2,16,8,256]{3,2,1,0:T(8,128)S(1)}, u32[]{:S(2)}, u32[]{:S(2)}) collective-permute-start(f32[2,16,8,256]{3,2,1,0:T(8,128)S(1)} %get-tuple-element.40), channel_id=1, source_target_pairs={{1,0},{2,1},{3,2},{4,3},{5,4},{6,5},{7,6},{8,7},{9,8},{10,9},{11,1... | collective-permute-start | bytes 786440 | tf_op jit(solution)/shard_map/ppermute | solution.py:571
  12.3 0.0 collective-permute-done.xl_ref
  12.4 0.5 collective-permute-done.1.xr_ref
  12.9 4.0 %collective-permute-start.4 = (f32[2,6,8,256]{3,2,1,0:T(8,128)S(1)}, f32[2,6,8,256]{3,2,1,0:T(8,128)S(1)}, u32[]{:S(2)}, u32[]{:S(2)}) collective-permute-start(f32[2,6,8,256]{3,2,1,0:T(8,128)S(1)} %get-tuple-element.41), channel_id=1, source_target_pairs={{0,1},{1,2},{2,3},{3,4},{4,5},{5,6},{6,7},{7,8},{8,9},{9,10},{10,1... | collective-permute-start | bytes 294920 | tf_op jit(solution)/shard_map/ppermute | solution.py:571
  16.8 1.3 %collective-permute-start.5 = (f32[2,6,8,256]{3,2,1,0:T(8,128)S(1)}, f32[2,6,8,256]{3,2,1,0:T(8,128)S(1)}, u32[]{:S(2)}, u32[]{:S(2)}) collective-permute-start(f32[2,6,8,256]{3,2,1,0:T(8,128)S(1)} %get-tuple-element.42), channel_id=1, source_target_pairs={{1,0},{2,1},{3,2},{4,3},{5,4},{6,5},{7,6},{8,7},{9,8},{10,9},{11,1... | collective-permute-start | bytes 294920 | tf_op jit(solution)/shard_map/ppermute | solution.py:571
  18.2 0.8 collective-permute-done.4.cl_ref
  19.0 2.2 %collective-permute-done.5.cr_ref = f32[2,6,8,256]{3,2,1,0:T(8,128)S(1)} collective-permute-done((f32[2,6,8,256]{3,2,1,0:T(8,128)S(1)}, f32[2,6,8,256]{3,2,1,0:T(8,128)S(1)}, u32[]{:S(2)}, u32[]{:S(2)}) %collective-permute-start.5) | collective-permute-done | bytes 98336 | tf_op jit(solution)/shard_map/ppermute | solution.py:571
  21.2 0.0 collective-permute-done.2.yl_ref
  21.2 0.0 collective-permute-done.3.yr_ref
  21.2 3.1 %shard_map.61 = (f32[4,8,8,128]{3,2,1,0:T(8,128)S(1)}, f32[4,8,8,128]{3,2,1,0:T(8,128)S(1)}, f32[4,8,8,128]{3,2,1,0:T(8,128)S(1)}, f32[4,8,8,128]{3,2,1,0:T(8,12...) custom-call(f32[16,16,256]{2,1,0:T(8,128)S(1)} %copy-done, ...), custom_call_target="tpu_custom_call" | custom-call | tf_op jit(solution)/shard_map/pallas_call | solution.py:557
  24.3 3.2 %collective-permute-start.6 = (f32[4,8,8,128]{3,2,1,0:T(8,128)S(1)}, f32[4,8,8,128]{3,2,1,0:T(8,128)S(1)}, u32[]{:S(2)}, u32[]{:S(2)}) collective-permute-start(f32[4,8,8,128]{3,2,1,0:T(8,128)S(1)} %get-tuple-element.44), channel_id=1, source_target_pairs={{0,32},{32,64},{64,96},{96,128},{128,160},{160,192},{192,224},{224... | collective-permute-start | bytes 393224 | tf_op jit(solution)/shard_map/ppermute | solution.py:571
  27.5 1.3 %collective-permute-start.7 = (f32[4,8,8,128]{3,2,1,0:T(8,128)S(1)}, f32[4,8,8,128]{3,2,1,0:T(8,128)S(1)}, u32[]{:S(2)}, u32[]{:S(2)}) collective-permute-start(f32[4,8,8,128]{3,2,1,0:T(8,128)S(1)} %get-tuple-element.45), channel_id=1, source_target_pairs={{32,0},{64,32},{96,64},{128,96},{160,128},{192,160},{224,192},{256... | collective-permute-start | bytes 393224 | tf_op jit(solution)/shard_map/ppermute | solution.py:571
  28.8 0.0 collective-permute-start.8
  28.9 4.5 %collective-permute-start.9 = (f32[4,8,8,128]{3,2,1,0:T(8,128)S(1)}, f32[4,8,8,128]{3,2,1,0:T(8,128)S(1)}, u32[]{:S(2)}, u32[]{:S(2)}) collective-permute-start(f32[4,8,8,128]{3,2,1,0:T(8,128)S(1)} %get-tuple-element.47), channel_id=1, source_target_pairs={{1,0},{2,1},{3,2},{4,3},{5,4},{6,5},{7,6},{8,7},{9,8},{10,9},{11,1... | collective-permute-start | bytes 393224 | tf_op jit(solution)/shard_map/ppermute | solution.py:571
  33.4 0.0 collective-permute-done.6.xl_ref
  33.4 0.0 collective-permute-done.7.xr_ref
  33.4 0.8 collective-permute-done.8.yl_ref
  34.2 0.2 collective-permute-done.9.yr_ref
  34.4 0.7 collective-permute-start.10
  35.1 3.9 %collective-permute-start.11 = (f32[4,14,8,128]{3,2,1,0:T(8,128)S(1)}, f32[4,14,8,128]{3,2,1,0:T(8,128)S(1)}, u32[]{:S(2)}, u32[]{:S(2)}) collective-permute-start(f32[4,14,8,128]{3,2,1,0:T(8,128)S(1)} %get-tuple-element.49), channel_id=1, source_target_pairs={{1,0},{2,1},{3,2},{4,3},{5,4},{6,5},{7,6},{8,7},{9,8},{10,9},{11,1... | collective-permute-start | bytes 688136 | tf_op jit(solution)/shard_map/ppermute | solution.py:571
  39.0 1.0 collective-permute-done.10.cl_ref
  40.0 0.6 collective-permute-done.11.cr_ref
  40.6 1.8 %shard_map.63 = (f32[24,8,128]{2,1,0:T(8,128)S(1)}, f32[24,8,128]{2,1,0:T(8,128)S(1)}, f32[24,8,128]{2,1,0:T(8,128)S(1)}, f32[24,8,128]{2,1,0:T(8,128)S(1)}, f32...) custom-call(f32[4,8,8,128]{3,2,1,0:T(8,128)S(1)} %get-tuple-element., ...), custom_call_target="tpu_custom_call" | custom-call | tf_op jit(solution)/shard_map/pallas_call | solution.py:557
  42.4 3.8 %collective-permute-start.12 = (f32[24,8,128]{2,1,0:T(8,128)S(1)}, f32[24,8,128]{2,1,0:T(8,128)S(1)}, u32[]{:S(2)}, u32[]{:S(2)}) collective-permute-start(f32[24,8,128]{2,1,0:T(8,128)S(1)} %get-tuple-element.51), channel_id=1, source_target_pairs={{0,32},{32,64},{64,96},{96,128},{128,160},{160,192},{192,224},{224... | collective-permute-start | bytes 294920 | tf_op jit(solution)/shard_map/ppermute | solution.py:571
  46.2 1.3 %collective-permute-start.13 = (f32[24,8,128]{2,1,0:T(8,128)S(1)}, f32[24,8,128]{2,1,0:T(8,128)S(1)}, u32[]{:S(2)}, u32[]{:S(2)}) collective-permute-start(f32[24,8,128]{2,1,0:T(8,128)S(1)} %get-tuple-element.52), channel_id=1, source_target_pairs={{32,0},{64,32},{96,64},{128,96},{160,128},{192,160},{224,192},{256... | collective-permute-start | bytes 294920 | tf_op jit(solution)/shard_map/ppermute | solution.py:571
  47.5 0.3 collective-permute-start.14
  47.8 5.5 %collective-permute-start.15 = (f32[24,8,128]{2,1,0:T(8,128)S(1)}, f32[24,8,128]{2,1,0:T(8,128)S(1)}, u32[]{:S(2)}, u32[]{:S(2)}) collective-permute-start(f32[24,8,128]{2,1,0:T(8,128)S(1)} %get-tuple-element.54), channel_id=1, source_target_pairs={{1,0},{2,1},{3,2},{4,3},{5,4},{6,5},{7,6},{8,7},{9,8},{10,9},{11,1... | collective-permute-start | bytes 294920 | tf_op jit(solution)/shard_map/ppermute | solution.py:571
  53.4 0.0 collective-permute-done.12.xl_ref
  53.4 0.0 collective-permute-done.13.xr_ref
  53.4 0.8 collective-permute-done.14.yl_ref
  54.1 0.2 collective-permute-done.15.yr_ref
  54.3 0.0 collective-permute-start.16
  54.4 4.8 %collective-permute-start.17 = (f32[30,8,128]{2,1,0:T(8,128)S(1)}, f32[30,8,128]{2,1,0:T(8,128)S(1)}, u32[]{:S(2)}, u32[]{:S(2)}) collective-permute-start(f32[30,8,128]{2,1,0:T(8,128)S(1)} %get-tuple-element.56), channel_id=1, source_target_pairs={{1,0},{2,1},{3,2},{4,3},{5,4},{6,5},{7,6},{8,7},{9,8},{10,9},{11,1... | collective-permute-start | bytes 368648 | tf_op jit(solution)/shard_map/ppermute | solution.py:571
  59.1 0.8 collective-permute-done.16.cl_ref
  59.9 0.2 collective-permute-done.17.cr_ref
  60.1 4.7 %shard_map.65 = (f32[16,16,256]{2,1,0:T(8,128)}, f32[8,128]{1,0:T(8,128)S(1)}) custom-call(f32[24,8,128]{2,1,0:T(8,128)S(1)} %collective-permute-done.12.xl_ref, f32[24,8,128]{2,1,0:T(8,128)S(1)} %collective-permute-done.13.xr_ref, f32[24,8,128]{2,1,0:T(8,128)S(1)} %collective-permute-done.14.yl_ref, f32[24,8,128]{2,1,0:T(8,128)S(1)} %collective-permute-done.15.yr_ref, ...), custom_call_target="tpu_custom_call" | custom-call | tf_op jit(solution)/shard_map/pallas_call | solution.py:557
  64.8 26.8 %all_to_all.12 = f32[32,1,128]{2,1,0:T(1,128)S(1)} all-to-all(f32[32,1,128]{2,1,0:T(1,128)S(1)} %broadcast_in_dim.6), channel_id=1, replica_groups=mesh['gx'=16,'gy'=32] {'gy'}, dimensions={0} | all-to-all | bytes 32768 | tf_op jit(solution)/shard_map/all_to_all | solution.py:577
  91.7 16.3 %all_to_all.13 = f32[16,1,128]{2,1,0:T(1,128)S(1)} all-to-all(f32[16,1,128]{2,1,0:T(1,128)S(1)} %broadcast_in_dim.7), channel_id=1, replica_groups=mesh['gx'=16,'gy'=32] {'gx'}, dimensions={0} | all-to-all | bytes 16384 | tf_op jit(solution)/shard_map/all_to_all | solution.py:577
  (10 shorter events, 0.2 us)
Async XLA Ops:
  0.6 1.0 copy-start
  1.6 6.4 %copy-start.3 = (f32[16,16,256]{2,1,0:T(8,128)S(1)}, f32[16,16,256]{2,1,0:T(8,128)}, u32[]{:S(2)}) copy-start(f32[16,16,256]{2,1,0:T(8,128)} %f_ref.3) | copy-start | bytes 786436
  2.5 5.6 %copy-start.1 = (f32[16,16,256]{2,1,0:T(8,128)S(1)}, f32[16,16,256]{2,1,0:T(8,128)}, u32[]{:S(2)}) copy-start(f32[16,16,256]{2,1,0:T(8,128)} %e_ref.3) | copy-start | bytes 786436
  2.5 5.6 %copy-start.2 = (f32[16,16,256]{2,1,0:T(8,128)S(1)}, f32[16,16,256]{2,1,0:T(8,128)}, u32[]{:S(2)}) copy-start(f32[16,16,256]{2,1,0:T(8,128)} %k_ref.3) | copy-start | bytes 786436
  2.6 9.8 %collective-permute-start = (f32[10,16,256]{2,1,0:T(8,128)S(1)}, f32[10,16,256]{2,1,0:T(8,128)S(1)}, u32[]{:S(2)}, u32[]{:S(2)}) collective-permute-start(f32[10,16,256]{2,1,0:T(8,128)S(1)} %pad_maximum_fusion), channel_id=1, source_target_pairs={{0,32},{32,64},{64,96},{96,128},{128,160},{160,192},{192,224},{224... | collective-permute-start | bytes 491528 | tf_op jit(solution)/shard_map/ppermute | solution.py:571
  6.8 6.1 %collective-permute-start.1 = (f32[10,16,256]{2,1,0:T(8,128)S(1)}, f32[10,16,256]{2,1,0:T(8,128)S(1)}, u32[]{:S(2)}, u32[]{:S(2)}) collective-permute-start(f32[10,16,256]{2,1,0:T(8,128)S(1)} %pad_maximum_fusion.1), channel_id=1, source_target_pairs={{32,0},{64,32},{96,64},{128,96},{160,128},{192,160},{224,192},{256... | collective-permute-start | bytes 491528 | tf_op jit(solution)/shard_map/ppermute | solution.py:571
  8.2 13.0 %collective-permute-start.2 = (f32[2,16,8,256]{3,2,1,0:T(8,128)S(1)}, f32[2,16,8,256]{3,2,1,0:T(8,128)S(1)}, u32[]{:S(2)}, u32[]{:S(2)}) collective-permute-start(f32[2,16,8,256]{3,2,1,0:T(8,128)S(1)} %get-tuple-element.39), channel_id=1, source_target_pairs={{0,1},{1,2},{2,3},{3,4},{4,5},{5,6},{6,7},{7,8},{8,9},{9,10},{10,1... | collective-permute-start | bytes 786440 | tf_op jit(solution)/shard_map/ppermute | solution.py:571
  10.7 10.5 %collective-permute-start.3 = (f32[2,16,8,256]{3,2,1,0:T(8,128)S(1)}, f32[2,16,8,256]{3,2,1,0:T(8,128)S(1)}, u32[]{:S(2)}, u32[]{:S(2)}) collective-permute-start(f32[2,16,8,256]{3,2,1,0:T(8,128)S(1)} %get-tuple-element.40), channel_id=1, source_target_pairs={{1,0},{2,1},{3,2},{4,3},{5,4},{6,5},{7,6},{8,7},{9,8},{10,9},{11,1... | collective-permute-start | bytes 786440 | tf_op jit(solution)/shard_map/ppermute | solution.py:571
  12.9 6.1 %collective-permute-start.4 = (f32[2,6,8,256]{3,2,1,0:T(8,128)S(1)}, f32[2,6,8,256]{3,2,1,0:T(8,128)S(1)}, u32[]{:S(2)}, u32[]{:S(2)}) collective-permute-start(f32[2,6,8,256]{3,2,1,0:T(8,128)S(1)} %get-tuple-element.41), channel_id=1, source_target_pairs={{0,1},{1,2},{2,3},{3,4},{4,5},{5,6},{6,7},{7,8},{8,9},{9,10},{10,1... | collective-permute-start | bytes 294920 | tf_op jit(solution)/shard_map/ppermute | solution.py:571
  16.8 4.3 %collective-permute-start.5 = (f32[2,6,8,256]{3,2,1,0:T(8,128)S(1)}, f32[2,6,8,256]{3,2,1,0:T(8,128)S(1)}, u32[]{:S(2)}, u32[]{:S(2)}) collective-permute-start(f32[2,6,8,256]{3,2,1,0:T(8,128)S(1)} %get-tuple-element.42), channel_id=1, source_target_pairs={{1,0},{2,1},{3,2},{4,3},{5,4},{6,5},{7,6},{8,7},{9,8},{10,9},{11,1... | collective-permute-start | bytes 294920 | tf_op jit(solution)/shard_map/ppermute | solution.py:571
  24.3 9.0 %collective-permute-start.6 = (f32[4,8,8,128]{3,2,1,0:T(8,128)S(1)}, f32[4,8,8,128]{3,2,1,0:T(8,128)S(1)}, u32[]{:S(2)}, u32[]{:S(2)}) collective-permute-start(f32[4,8,8,128]{3,2,1,0:T(8,128)S(1)} %get-tuple-element.44), channel_id=1, source_target_pairs={{0,32},{32,64},{64,96},{96,128},{128,160},{160,192},{192,224},{224... | collective-permute-start | bytes 393224 | tf_op jit(solution)/shard_map/ppermute | solution.py:571
  27.5 5.8 %collective-permute-start.7 = (f32[4,8,8,128]{3,2,1,0:T(8,128)S(1)}, f32[4,8,8,128]{3,2,1,0:T(8,128)S(1)}, u32[]{:S(2)}, u32[]{:S(2)}) collective-permute-start(f32[4,8,8,128]{3,2,1,0:T(8,128)S(1)} %get-tuple-element.45), channel_id=1, source_target_pairs={{32,0},{64,32},{96,64},{128,96},{160,128},{192,160},{224,192},{256... | collective-permute-start | bytes 393224 | tf_op jit(solution)/shard_map/ppermute | solution.py:571
  28.8 5.3 %collective-permute-start.8 = (f32[4,8,8,128]{3,2,1,0:T(8,128)S(1)}, f32[4,8,8,128]{3,2,1,0:T(8,128)S(1)}, u32[]{:S(2)}, u32[]{:S(2)}) collective-permute-start(f32[4,8,8,128]{3,2,1,0:T(8,128)S(1)} %get-tuple-element.46), channel_id=1, source_target_pairs={{0,1},{1,2},{2,3},{3,4},{4,5},{5,6},{6,7},{7,8},{8,9},{9,10},{10,1... | collective-permute-start | bytes 393224 | tf_op jit(solution)/shard_map/ppermute | solution.py:571
  28.9 5.5 %collective-permute-start.9 = (f32[4,8,8,128]{3,2,1,0:T(8,128)S(1)}, f32[4,8,8,128]{3,2,1,0:T(8,128)S(1)}, u32[]{:S(2)}, u32[]{:S(2)}) collective-permute-start(f32[4,8,8,128]{3,2,1,0:T(8,128)S(1)} %get-tuple-element.47), channel_id=1, source_target_pairs={{1,0},{2,1},{3,2},{4,3},{5,4},{6,5},{7,6},{8,7},{9,8},{10,9},{11,1... | collective-permute-start | bytes 393224 | tf_op jit(solution)/shard_map/ppermute | solution.py:571
  34.4 5.6 %collective-permute-start.10 = (f32[4,14,8,128]{3,2,1,0:T(8,128)S(1)}, f32[4,14,8,128]{3,2,1,0:T(8,128)S(1)}, u32[]{:S(2)}, u32[]{:S(2)}) collective-permute-start(f32[4,14,8,128]{3,2,1,0:T(8,128)S(1)} %get-tuple-element.48), channel_id=1, source_target_pairs={{0,1},{1,2},{2,3},{3,4},{4,5},{5,6},{6,7},{7,8},{8,9},{9,10},{10,1... | collective-permute-start | bytes 688136 | tf_op jit(solution)/shard_map/ppermute | solution.py:571
  35.1 5.4 %collective-permute-start.11 = (f32[4,14,8,128]{3,2,1,0:T(8,128)S(1)}, f32[4,14,8,128]{3,2,1,0:T(8,128)S(1)}, u32[]{:S(2)}, u32[]{:S(2)}) collective-permute-start(f32[4,14,8,128]{3,2,1,0:T(8,128)S(1)} %get-tuple-element.49), channel_id=1, source_target_pairs={{1,0},{2,1},{3,2},{4,3},{5,4},{6,5},{7,6},{8,7},{9,8},{10,9},{11,1... | collective-permute-start | bytes 688136 | tf_op jit(solution)/shard_map/ppermute | solution.py:571
  42.4 11.0 %collective-permute-start.12 = (f32[24,8,128]{2,1,0:T(8,128)S(1)}, f32[24,8,128]{2,1,0:T(8,128)S(1)}, u32[]{:S(2)}, u32[]{:S(2)}) collective-permute-start(f32[24,8,128]{2,1,0:T(8,128)S(1)} %get-tuple-element.51), channel_id=1, source_target_pairs={{0,32},{32,64},{64,96},{96,128},{128,160},{160,192},{192,224},{224... | collective-permute-start | bytes 294920 | tf_op jit(solution)/shard_map/ppermute | solution.py:571
  46.2 7.1 %collective-permute-start.13 = (f32[24,8,128]{2,1,0:T(8,128)S(1)}, f32[24,8,128]{2,1,0:T(8,128)S(1)}, u32[]{:S(2)}, u32[]{:S(2)}) collective-permute-start(f32[24,8,128]{2,1,0:T(8,128)S(1)} %get-tuple-element.52), channel_id=1, source_target_pairs={{32,0},{64,32},{96,64},{128,96},{160,128},{192,160},{224,192},{256... | collective-permute-start | bytes 294920 | tf_op jit(solution)/shard_map/ppermute | solution.py:571
  47.5 6.6 %collective-permute-start.14 = (f32[24,8,128]{2,1,0:T(8,128)S(1)}, f32[24,8,128]{2,1,0:T(8,128)S(1)}, u32[]{:S(2)}, u32[]{:S(2)}) collective-permute-start(f32[24,8,128]{2,1,0:T(8,128)S(1)} %get-tuple-element.53), channel_id=1, source_target_pairs={{0,1},{1,2},{2,3},{3,4},{4,5},{5,6},{6,7},{7,8},{8,9},{9,10},{10,1... | collective-permute-start | bytes 294920 | tf_op jit(solution)/shard_map/ppermute | solution.py:571
  47.8 6.5 %collective-permute-start.15 = (f32[24,8,128]{2,1,0:T(8,128)S(1)}, f32[24,8,128]{2,1,0:T(8,128)S(1)}, u32[]{:S(2)}, u32[]{:S(2)}) collective-permute-start(f32[24,8,128]{2,1,0:T(8,128)S(1)} %get-tuple-element.54), channel_id=1, source_target_pairs={{1,0},{2,1},{3,2},{4,3},{5,4},{6,5},{7,6},{8,7},{9,8},{10,9},{11,1... | collective-permute-start | bytes 294920 | tf_op jit(solution)/shard_map/ppermute | solution.py:571
  54.3 5.6 %collective-permute-start.16 = (f32[30,8,128]{2,1,0:T(8,128)S(1)}, f32[30,8,128]{2,1,0:T(8,128)S(1)}, u32[]{:S(2)}, u32[]{:S(2)}) collective-permute-start(f32[30,8,128]{2,1,0:T(8,128)S(1)} %get-tuple-element.55), channel_id=1, source_target_pairs={{0,1},{1,2},{2,3},{3,4},{4,5},{5,6},{6,7},{7,8},{8,9},{9,10},{10,1... | collective-permute-start | bytes 368648 | tf_op jit(solution)/shard_map/ppermute | solution.py:571
  54.4 5.7 %collective-permute-start.17 = (f32[30,8,128]{2,1,0:T(8,128)S(1)}, f32[30,8,128]{2,1,0:T(8,128)S(1)}, u32[]{:S(2)}, u32[]{:S(2)}) collective-permute-start(f32[30,8,128]{2,1,0:T(8,128)S(1)} %get-tuple-element.56), channel_id=1, source_target_pairs={{1,0},{2,1},{3,2},{4,3},{5,4},{6,5},{7,6},{8,7},{9,8},{10,9},{11,1... | collective-permute-start | bytes 368648 | tf_op jit(solution)/shard_map/ppermute | solution.py:571
